TPU v7x, 32 devices: a whole 2x2x4 slice. The times are simulated.
32 devices in a mesh: gx: 8 (over y, x, core), gy: 4 (over z).
Axes of the slice: x: 2, y: 2, z: 4, core: 2. Of those that a mesh axis runs over, the one named last changes fastest.
Arguments:
- waveforms: bfloat16 [64, 3, 1536], P(('gx', 'gy')), may hold values from -100 to 100
- templates: bfloat16 [1024, 8, 1536], P(('gx', 'gy')), may hold values from -100 to 100
- tpl_stations: int32 [1024, 8], P(('gx', 'gy')), may hold values from 0 to 63, all different within a row; in each aligned block of 32 rows (0 to 31, 32 to 63, ...) at most 8 rows name the same one
- det_station: int32 [2048], P(('gx', 'gy')), may hold values from 0 to 1
- det_time: int32 [2048], P(('gx', 'gy')), may hold values from 64 to 1216
- partner: int32 [2048, 4], P(('gx', 'gy')), may hold values from 0 to 63
Outputs:
- stack: float32 [1024, 1024], P(('gx', 'gy'))
- diffcc: float32 [2048, 4, 128], P(('gx', 'gy'))
Inputs may be any that keep to these rules, and one draw needn't show every extreme that they name: `tpl_stations`: each row names 8 different stations; among the templates of one station group no station is named more than 8 times.
All inputs are finite; a program needn't handle non-finite values.
Results may differ from a plain program's by a relative error of at most 0.0007.
Values may be sent and summed in bfloat16 or wider, within the bound.
No kernel may reach another device: no remote copies, remote signals or barrier semaphores. Data moves between devices by JAX's collectives and lax.ppermute only.
A program may use at most 128 MiB of HBM per device.

v0:
```python
import jax
import jax.numpy as jnp
from jax import lax
from jax.sharding import PartitionSpec as P

W = 256
DTLAG = 128


def from_behind(value, axis, steps):
    count = lax.axis_size(axis)
    leading, last = (max(0, -steps), min(count, count - steps))
    return lax.ppermute(value, axis, [(source, source + steps) for source in range(leading, last)])


def lagged_rows(series, rows, lags):
    length = series.shape[-1]
    lead = series.shape[:-1]
    tiled = jnp.tile(series, (1,) * len(lead) + (rows + 1,))
    tiled = tiled[..., : rows * (length + 1)].reshape(lead + (rows, length + 1))
    return tiled[..., :lags]


def on_device(waveforms, templates, tpl_stations, det_station, det_time, partner):
    sta_dev = waveforms.shape[0]
    samples = waveforms.shape[2]
    tpl_dev, k_slots, row_len = templates.shape
    tlen = row_len // 3
    nlag = samples - tlen
    ngx = lax.axis_size("gx")
    ngy = lax.axis_size("gy")
    groups = ngx * ngy
    stations = sta_dev * groups
    cap = max(2, (2 * tpl_dev * k_slots + stations - 1) // stations)
    flat_station = tpl_stations.reshape(-1)
    count = flat_station.shape[0]
    order = jnp.arange(count, dtype=jnp.int32)
    same = (flat_station[:, None] == flat_station[None, :]) & (order[None, :] < order[:, None])
    rank = jnp.sum(same.astype(jnp.int32), axis=1)
    owner = flat_station // sta_dev
    within = flat_station % sta_dev
    slot = (within * groups + owner) * cap + rank
    outbox = jnp.zeros((sta_dev * groups * cap, row_len), jnp.bfloat16)
    outbox = outbox.at[slot].set(templates.reshape(count, row_len))
    inbox = lax.all_to_all(
        outbox.reshape(sta_dev, groups, cap, row_len),
        ("gx", "gy"),
        split_axis=1,
        concat_axis=1,
        tiled=True,
    )
    inbox = inbox.reshape(sta_dev, groups * cap, row_len)

    def correlate(pair):
        station_data, tiles = pair
        lagged = lagged_rows(station_data, tlen, nlag).reshape(3 * tlen, nlag)
        raw = jnp.dot(tiles, lagged, preferred_element_type=jnp.float32)
        tile_mean = jnp.einsum("mr,mr->m", tiles, tiles, preferred_element_type=jnp.float32) / (
            3 * tlen
        )
        values = station_data.astype(jnp.float32)
        energy = jnp.sum(values * values, axis=0)
        window_sum = lax.reduce_window(energy, jnp.float32(0.0), lax.add, (tlen,), (1,), "VALID")
        win_mean = window_sum[:nlag] / (3 * tlen)
        return (
            raw
            * lax.rsqrt(3 * tlen * (tile_mean + 1e-06))[:, None]
            * lax.rsqrt(win_mean + 1e-06)[None, :]
        )

    traces = lax.map(correlate, (waveforms, inbox))
    returned = lax.all_to_all(
        traces.reshape(sta_dev, groups, cap, nlag),
        ("gx", "gy"),
        split_axis=1,
        concat_axis=1,
        tiled=True,
    )
    picked = returned.reshape(sta_dev * groups * cap, nlag)[slot]
    stack = jnp.sum(picked.reshape(tpl_dev, k_slots, nlag), axis=1) / jnp.sqrt(jnp.float32(k_slots))
    half = DTLAG // 2
    wide_len = W + DTLAG
    det_dev = det_station.shape[0]

    def cut(sta, start, size):
        return lax.dynamic_slice(waveforms, (sta, jnp.int32(0), start), (1, 3, size))[0]

    local = jax.vmap(lambda s, t: cut(s, t, W))(det_station, det_time)
    wide = jax.vmap(lambda s, t: cut(s, t - half, wide_len))(det_station, det_time)
    across = [from_behind(wide, "gx", step) for step in (-1, 1)]
    along = [from_behind(wide, "gy", step) for step in (-1, 1)]
    received = jnp.stack([across[0], across[1], along[0], along[1]])
    chosen = jax.vmap(lambda rows, picks: rows[picks])(received, partner.T)
    pieces = chosen.reshape(4 * det_dev, 3, wide_len)
    locals_all = jnp.broadcast_to(local[None], (4, det_dev, 3, W)).reshape(4 * det_dev, 3, W)
    blocks = 4 * det_dev // 16

    def window_block(pair):
        piece, mine = pair
        lagged = lagged_rows(piece, W, DTLAG)
        raw = jnp.einsum("bct,bctl->bl", mine, lagged, preferred_element_type=jnp.float32)
        mine_mean = jnp.einsum("bct,bct->b", mine, mine, preferred_element_type=jnp.float32) / (
            3 * W
        )
        centre = piece[:, :, half : half + W]
        piece_mean = jnp.einsum(
            "bct,bct->b", centre, centre, preferred_element_type=jnp.float32
        ) / (3 * W)
        return (
            raw
            * lax.rsqrt(3 * W * (mine_mean + 1e-06))[:, None]
            * lax.rsqrt(piece_mean + 1e-06)[:, None]
        )

    result = lax.map(
        window_block,
        (pieces.reshape(blocks, 16, 3, wide_len), locals_all.reshape(blocks, 16, 3, W)),
    )
    diffcc = jnp.transpose(result.reshape(4, det_dev, DTLAG), (1, 0, 2))
    return (stack, diffcc)


def solution(mesh):
    return jax.shard_map(
        on_device,
        mesh=mesh,
        in_specs=(
            P(("gx", "gy"), None, None),
            P(("gx", "gy"), None, None),
            P(("gx", "gy"), None),
            P(("gx", "gy")),
            P(("gx", "gy")),
            P(("gx", "gy"), None),
        ),
        out_specs=(P(("gx", "gy"), None), P(("gx", "gy"), None, None)),
        check_vma=False,
    )
```

profile of v0, /device:TPU:1, one launch (start us, length us, event | category | flops | bytes accessed | tf_op | source)
XLA Modules:
  0.0 1183.6 jit_solution(9723537506004801898)
XLA Ops:
  14.1 19.2 %gather_fusion.2 = bf16[64,3,384]{1,0,2:T(8,128)(2,1)} fusion(bf16[2,3,1536]{1,0,2:T(2,128)(2,1)S(1)} %copy.63, s32[64]{0:T(128)S(1)} %get-tuple-element.112), kind=kCustom, calls=%fused_computation.2 | custom fusion | bytes 295680 | tf_op jit(solution)/shard_map/vmap()/gather | solution.py:86
  33.3 8.7 copy.66
  53.5 13.1 %gather_fusion.1 = bf16[64,3,256]{1,0,2:T(8,128)(2,1)} fusion(bf16[2,3,1536]{1,0,2:T(2,128)(2,1)S(1)} %copy.63, s32[64]{0:T(128)S(1)} %get-tuple-element.113), kind=kCustom, calls=%fused_computation.1 | custom fusion | bytes 197376 | tf_op jit(solution)/shard_map/vmap()/gather | solution.py:86
  77.6 232.1 %while.20 = (s32[]{:T(128)}, f32[2,256,1024]{2,1,0:T(8,128)}, bf16[2,256,1536]{2,1,0:T(8,128)(2,1)S(1)}, bf16[2,3,1536]{2,1,0:T(4,128)(2,1)S(1)}, s32[]{:T(128)}, /*index=5*/f32[]{:T(128)}) while((s32[]{:T(128)}, f32[2,256,1024]{2,1,0:T(8,128)}, bf16[2,256,1536]{2,1,0:T(8,128)(2,1)S(1)}, bf16[2,3,1536]{2,1,0:T(4,128)(2,1)S(1)}, s32[]{:T(128)}, ...), condition=%wide.region_5.6_spmd, body=%wide.region_2.5_spmd.sunk | while | flops 807548928 | bytes 54645844 | solution.py:71
  89.7 9.1 reshape.278
  98.9 12.0 %reshape.279 = bf16[3,512,1537]{2,1,0:T(8,128)(2,1)} reshape(bf16[2360832]{0:T(1024)(128)(2,1)} %reshape.278) | data formatting | bytes 9443328 | tf_op jit(solution)/shard_map/while/body/eval_jaxpr/reshape | solution.py:20
  114.9 71.1 %reduce-window.6 = f32[1025,1]{1,0:T(8,128)S(1)} reduce-window(f32[1536,1]{1,0:T(8,128)S(1)} %reshape.280, f32[]{:T(128)} %constant.49.clone.2..sunk), window={size=512x1}, to_apply=%region_4.4 | reduce-window | flops 523775 | bytes 10248 | tf_op jit(solution)/shard_map/reduce-window
  202.8 9.1 reshape.278
  212.0 11.7 reshape.279
  227.8 71.3 %reduce-window.6 = f32[1025,1]{1,0:T(8,128)S(1)} reduce-window(f32[1536,1]{1,0:T(8,128)S(1)} %reshape.280, f32[]{:T(128)} %constant.49.clone.2..sunk), window={size=512x1}, to_apply=%region_4.4 | reduce-window | flops 523775 | bytes 10248 | tf_op jit(solution)/shard_map/reduce-window
  317.8 858.5 %while.21 = (s32[]{:T(128)}, f32[16,16,128]{2,1,0:T(8,128)S(1)}, bf16[16,16,3,256]{3,2,1,0:T(4,128)(2,1)S(1)}, bf16[16,16,3,384]{3,1,2,0:T(8,128)(2,1)S(1)}, s32[]{:T(128)}) while((s32[]{:T(128)}, f32[16,16,128]{2,1,0:T(8,128)S(1)}, bf16[16,16,3,256]{3,2,1,0:T(4,128)(2,1)S(1)}, bf16[16,16,3,384]{3,1,2,0:T(8,128)(2,1)S(1)}, s32[]{:T(128)}) %tuple.63), condition=%wide.region_8.9_spmd, body=%wide.region_7.8_spmd.sunk | while | flops 3223602 | bytes 69674432 | solution.py:115
  322.9 10.6 tile.28
  333.5 8.0 slice.57
  341.5 27.5 %reshape.281 = bf16[16,3,256,385]{3,2,0,1:T(8,128)(2,1)} reshape(bf16[16,3,98560]{2,0,1:T(8,128)(2,1)} %slice.57) | data formatting | bytes 18923520 | tf_op jit(solution)/shard_map/while/body/eval_jaxpr/reshape | solution.py:20
  376.5 10.6 tile.28
  387.2 8.0 slice.57
  395.1 27.5 %reshape.281 = bf16[16,3,256,385]{3,2,0,1:T(8,128)(2,1)} reshape(bf16[16,3,98560]{2,0,1:T(8,128)(2,1)} %slice.57) | data formatting | bytes 18923520 | tf_op jit(solution)/shard_map/while/body/eval_jaxpr/reshape | solution.py:20
  430.2 10.6 tile.28
  440.8 8.0 slice.57
  448.8 27.5 %reshape.281 = bf16[16,3,256,385]{3,2,0,1:T(8,128)(2,1)} reshape(bf16[16,3,98560]{2,0,1:T(8,128)(2,1)} %slice.57) | data formatting | bytes 18923520 | tf_op jit(solution)/shard_map/while/body/eval_jaxpr/reshape | solution.py:20
  483.8 10.6 tile.28
  494.5 8.0 slice.57
  502.5 27.5 %reshape.281 = bf16[16,3,256,385]{3,2,0,1:T(8,128)(2,1)} reshape(bf16[16,3,98560]{2,0,1:T(8,128)(2,1)} %slice.57) | data formatting | bytes 18923520 | tf_op jit(solution)/shard_map/while/body/eval_jaxpr/reshape | solution.py:20
  537.5 10.6 tile.28
  556.1 27.5 %reshape.281 = bf16[16,3,256,385]{3,2,0,1:T(8,128)(2,1)} reshape(bf16[16,3,98560]{2,0,1:T(8,128)(2,1)} %slice.57) | data formatting | bytes 18923520 | tf_op jit(solution)/shard_map/while/body/eval_jaxpr/reshape | solution.py:20
  591.1 10.6 tile.28
  609.8 27.5 %reshape.281 = bf16[16,3,256,385]{3,2,0,1:T(8,128)(2,1)} reshape(bf16[16,3,98560]{2,0,1:T(8,128)(2,1)} %slice.57) | data formatting | bytes 18923520 | tf_op jit(solution)/shard_map/while/body/eval_jaxpr/reshape | solution.py:20
  644.8 10.6 tile.28
  663.4 27.5 %reshape.281 = bf16[16,3,256,385]{3,2,0,1:T(8,128)(2,1)} reshape(bf16[16,3,98560]{2,0,1:T(8,128)(2,1)} %slice.57) | data formatting | bytes 18923520 | tf_op jit(solution)/shard_map/while/body/eval_jaxpr/reshape | solution.py:20
  698.4 10.6 tile.28
  717.1 27.5 %reshape.281 = bf16[16,3,256,385]{3,2,0,1:T(8,128)(2,1)} reshape(bf16[16,3,98560]{2,0,1:T(8,128)(2,1)} %slice.57) | data formatting | bytes 18923520 | tf_op jit(solution)/shard_map/while/body/eval_jaxpr/reshape | solution.py:20
  752.1 10.6 tile.28
  770.7 27.5 %reshape.281 = bf16[16,3,256,385]{3,2,0,1:T(8,128)(2,1)} reshape(bf16[16,3,98560]{2,0,1:T(8,128)(2,1)} %slice.57) | data formatting | bytes 18923520 | tf_op jit(solution)/shard_map/while/body/eval_jaxpr/reshape | solution.py:20
  805.8 10.6 tile.28
  824.4 27.5 %reshape.281 = bf16[16,3,256,385]{3,2,0,1:T(8,128)(2,1)} reshape(bf16[16,3,98560]{2,0,1:T(8,128)(2,1)} %slice.57) | data formatting | bytes 18923520 | tf_op jit(solution)/shard_map/while/body/eval_jaxpr/reshape | solution.py:20
  859.4 10.6 tile.28
  878.0 27.5 %reshape.281 = bf16[16,3,256,385]{3,2,0,1:T(8,128)(2,1)} reshape(bf16[16,3,98560]{2,0,1:T(8,128)(2,1)} %slice.57) | data formatting | bytes 18923520 | tf_op jit(solution)/shard_map/while/body/eval_jaxpr/reshape | solution.py:20
  913.1 10.6 tile.28
  931.7 27.5 %reshape.281 = bf16[16,3,256,385]{3,2,0,1:T(8,128)(2,1)} reshape(bf16[16,3,98560]{2,0,1:T(8,128)(2,1)} %slice.57) | data formatting | bytes 18923520 | tf_op jit(solution)/shard_map/while/body/eval_jaxpr/reshape | solution.py:20
  966.7 10.6 tile.28
  977.4 8.0 slice.57
  985.4 27.5 %reshape.281 = bf16[16,3,256,385]{3,2,0,1:T(8,128)(2,1)} reshape(bf16[16,3,98560]{2,0,1:T(8,128)(2,1)} %slice.57) | data formatting | bytes 18923520 | tf_op jit(solution)/shard_map/while/body/eval_jaxpr/reshape | solution.py:20
  1020.4 10.6 tile.28
  1039.0 27.5 %reshape.281 = bf16[16,3,256,385]{3,2,0,1:T(8,128)(2,1)} reshape(bf16[16,3,98560]{2,0,1:T(8,128)(2,1)} %slice.57) | data formatting | bytes 18923520 | tf_op jit(solution)/shard_map/while/body/eval_jaxpr/reshape | solution.py:20
  1074.0 10.6 tile.28
  1092.7 27.5 %reshape.281 = bf16[16,3,256,385]{3,2,0,1:T(8,128)(2,1)} reshape(bf16[16,3,98560]{2,0,1:T(8,128)(2,1)} %slice.57) | data formatting | bytes 18923520 | tf_op jit(solution)/shard_map/while/body/eval_jaxpr/reshape | solution.py:20
  1127.7 10.6 tile.28
  1146.3 27.5 %reshape.281 = bf16[16,3,256,385]{3,2,0,1:T(8,128)(2,1)} reshape(bf16[16,3,98560]{2,0,1:T(8,128)(2,1)} %slice.57) | data formatting | bytes 18923520 | tf_op jit(solution)/shard_map/while/body/eval_jaxpr/reshape | solution.py:20
  (215 shorter events, 300.0 us)
Async XLA Ops:
  0.6 1.2 copy-start
  4.2 9.1 copy-start.4
  4.2 9.8 copy-start.6
  4.2 9.8 copy-start.7
  5.7 70.4 %all-to-all-start = ((bf16[2,32,8,1536]{3,2,0,1:T(8,128)(2,1)}), bf16[2,32,8,1536]{3,2,0,1:T(8,128)(2,1)}, u32[]{:S(2)}, u32[]{:S(2)}) async-start(bf16[2,32,8,1536]{3,2,0,1:T(8,128)(2,1)} %copy.58), calls=%async_computation | async-start | bytes 3145728 | tf_op jit(solution)/shard_map/all_to_all | solution.py:45
  33.3 20.1 %copy-start.5 = (s32[64,4]{0,1:T(4,128)S(1)}, s32[64,4]{0,1:T(4,128)}, u32[]{:S(2)}) copy-start(s32[64,4]{0,1:T(4,128)} %param.15) | copy-start | bytes 3076
  42.0 31.6 %collective-permute-start = (bf16[64,3,384]{2,0,1:T(8,128)(2,1)S(1)}, bf16[64,3,384]{2,0,1:T(8,128)(2,1)S(1)}, u32[]{:S(2)}, u32[]{:S(2)}) collective-permute-start(bf16[64,3,384]{2,0,1:T(8,128)(2,1)S(1)} %copy.66), channel_id=1, source_target_pairs={{4,0},{8,4},{12,8},{16,12},{20,16},{24,20},{28,24},{5,1},{9,5},{13... | collective-permute-start | bytes 442376 | tf_op jit(solution)/shard_map/ppermute | solution.py:13
  44.5 29.0 %collective-permute-start.1 = (bf16[64,3,384]{2,0,1:T(8,128)(2,1)S(1)}, bf16[64,3,384]{2,0,1:T(8,128)(2,1)S(1)}, u32[]{:S(2)}, u32[]{:S(2)}) collective-permute-start(bf16[64,3,384]{2,0,1:T(8,128)(2,1)S(1)} %copy.66), channel_id=1, source_target_pairs={{0,4},{4,8},{8,12},{12,16},{16,20},{20,24},{24,28},{1,5},{5,9},{9,... | collective-permute-start | bytes 442376 | tf_op jit(solution)/shard_map/ppermute | solution.py:13
  48.1 25.5 %collective-permute-start.2 = (bf16[64,3,384]{2,0,1:T(8,128)(2,1)S(1)}, bf16[64,3,384]{2,0,1:T(8,128)(2,1)S(1)}, u32[]{:S(2)}, u32[]{:S(2)}) collective-permute-start(bf16[64,3,384]{2,0,1:T(8,128)(2,1)S(1)} %copy.66), channel_id=1, source_target_pairs={{1,0},{2,1},{3,2},{5,4},{6,5},{7,6},{9,8},{10,9},{11,10},{13,12},{... | collective-permute-start | bytes 442376 | tf_op jit(solution)/shard_map/ppermute | solution.py:13
  49.4 24.2 %collective-permute-start.3 = (bf16[64,3,384]{2,0,1:T(8,128)(2,1)S(1)}, bf16[64,3,384]{2,0,1:T(8,128)(2,1)S(1)}, u32[]{:S(2)}, u32[]{:S(2)}) collective-permute-start(bf16[64,3,384]{2,0,1:T(8,128)(2,1)S(1)} %copy.66), channel_id=1, source_target_pairs={{0,1},{1,2},{2,3},{4,5},{5,6},{6,7},{8,9},{9,10},{10,11},{12,13},{... | collective-permute-start | bytes 442376 | tf_op jit(solution)/shard_map/ppermute | solution.py:13
  313.0 4.7 copy-start.2
  313.0 4.8 copy-start.3
  313.0 864.1 %all-to-all-start.1 = ((f32[2,32,8,1024]{3,2,0,1:T(8,128)}), f32[2,32,8,1024]{3,2,0,1:T(8,128)}, u32[]{:S(2)}, u32[]{:S(2)}) async-start(f32[2,32,8,1024]{3,2,0,1:T(8,128)} %copy.61), calls=%async_computation.1 | async-start | bytes 4194304 | tf_op jit(solution)/shard_map/all_to_all | solution.py:72
  1178.8 4.5 copy-start.1
where the time goes:
time: 1190 us; the launch traced here: 1180 us
  local copies, waits for them, and re-layouts  950 us (80%)
  other arithmetic  154 us (13%)
  matrix products  46.8 us (4%)
  starting transfers between devices  23.6 us (2%)
    reshape x18, local copies, waits for them, and re-layouts, lagged_rows(): tiled = tiled[..., :rows * (length + 1)].reshape(lead + (rows, length + 1))  463 us
    another operation x48, local copies, waits for them, and re-layouts, lagged_rows(): tiled = jnp.tile(series, (1,) * len(lead) + (rows + 1,))  244 us
    another operation x2, other arithmetic  142 us
    slice x18, local copies, waits for them, and re-layouts, lagged_rows(): tiled = tiled[..., :rows * (length + 1)].reshape(lead + (rows, length + 1))  135 us
    gather x4, local copies, waits for them, and re-layouts, cut(): lax.dynamic_slice(waveforms, (sta, jnp.int32(0), start), (1, 3, size))[0]  47.3 us
    dot_general x16, matrix products, window_block(): jnp.einsum('bct,bctl->bl', mine, lagged, preferred_element_type=jnp.float32)  39 us
    while x6, local copies, waits for them, and re-layouts  34.3 us
  transfers between devices with their start and end apart: 6, of which 0 were waited for; matrix products, arithmetic and copies ran while one was open for 77% of the time, Pallas kernels for 0%

commit v1 on v0

v1 whole, which is shorter than its diff:
```python
import functools

import jax
import jax.numpy as jnp
from jax import lax
from jax.experimental import pallas as pl
from jax.experimental.pallas import tpu as pltpu
from jax.sharding import PartitionSpec as P

LANES = 128
FINE = 8
COARSE = LANES // FINE
CHANNELS = 3
TAPS = 4
BLOCKS = 12
SLOTS = 16
W = 256
DTLAG = 128
HALF = DTLAG // 2
ROWS = CHANNELS * BLOCKS * 2
PACKED = ROWS + 8
EPS = 1e-06
F32 = jnp.float32
BF16 = jnp.bfloat16
NT = (((1,), (1,)), ((), ()))


def iota(shape, axis):
    return lax.broadcasted_iota(jnp.int32, shape, axis)


def rot(value, shift):
    shift = shift % LANES
    return pltpu.roll(value, shift, 1) if shift else value


def dot(a, b):
    return jnp.dot(a, b, preferred_element_type=F32)


def dot_nt(a, b):
    return lax.dot_general(a, b, NT, preferred_element_type=F32)


def pieces(value, count):
    out = []
    for _ in range(count - 1):
        high = value.astype(BF16)
        out.append(high)
        value = value - high.astype(F32)
    out.append(value.astype(BF16))
    return out


def lanes_before(lane, bound, first, second):
    if bound <= 0:
        return second
    if bound >= LANES:
        return first
    return jnp.where(lane < bound, first, second)


def column(row):
    n = row.shape[1]
    diagonal = iota((n, n), 0) == iota((n, n), 1)
    return jnp.sum(jnp.where(diagonal, row, 0), axis=1, keepdims=True)


def pack_kernel(wave_ref, time_ref, station_ref, out_ref, rows_ref):
    start = time_ref[...] - HALF
    row = 2 * (start // LANES) + station_ref[...]
    shift = start % LANES
    pad = jnp.zeros((1, LANES - row.shape[1]), F32)
    for c in range(CHANNELS):
        series = wave_ref[c].astype(F32)
        for block in range(BLOCKS):
            at = (c * BLOCKS + block) * 2
            rows_ref[at : at + 2, :] = series[:, block * LANES : (block + 1) * LANES]
    rows_ref[ROWS : ROWS + 1, :] = jnp.concatenate([row.astype(F32), pad], axis=1)
    rows_ref[ROWS + 1 : ROWS + 2, :] = jnp.concatenate([shift.astype(F32), pad], axis=1)
    rows_ref[ROWS + 2 : PACKED, :] = jnp.zeros((PACKED - ROWS - 2, LANES), F32)
    out_ref[...] = jnp.broadcast_to(rows_ref[...].astype(BF16)[None], out_ref.shape)


def tile_kernel(tiles_ref, station_ref, sorted_ref, scale_ref, owner_ref):
    tpl_dev, k_slots, row_len = tiles_ref.shape
    count = tpl_dev * k_slots
    total = sorted_ref.shape[0]
    station = station_ref[...].astype(F32).astype(BF16)
    home = (iota((count, tpl_dev), 0) // k_slots == iota((count, tpl_dev), 1)).astype(F32).astype(BF16)
    by_row = dot_nt(home, station)
    by_col = dot_nt(station, home)
    own_col = iota((count, k_slots), 0) % k_slots == iota((count, k_slots), 1)
    own_row = iota((k_slots, count), 1) % k_slots == iota((k_slots, count), 0)
    st_col = jnp.sum(jnp.where(own_col, by_row, 0.0), axis=1, keepdims=True)
    st_row = jnp.sum(jnp.where(own_row, by_col, 0.0), axis=0, keepdims=True)
    earlier = iota((count, count), 0) < iota((count, count), 1)
    rank = jnp.sum(jnp.where((st_col == st_row) & earlier, 1.0, 0.0), axis=0, keepdims=True)
    slot = (st_row * (SLOTS // 2) + rank).astype(jnp.int32)
    tiles = tiles_ref[...].reshape(count, row_len)
    step = 128
    for first in range(0, total, step):
        place = (iota((step, count), 0) + first == slot).astype(F32).astype(BF16)
        moved = dot(place, tiles)
        sorted_ref[first : first + step, :] = moved.astype(BF16)
        mean = jnp.sum(moved * moved, axis=1, keepdims=True) / row_len
        scale = lax.rsqrt(row_len * (mean + EPS))
        scale_ref[first : first + step, :] = jnp.broadcast_to(scale, (step, LANES))
        owner_ref[first : first + step, :] = dot(place, home).astype(BF16)


def main_kernel(
    ngx,
    ngy,
    data_ref,
    sorted_ref,
    scale_ref,
    owner_ref,
    time_ref,
    station_ref,
    partner_ref,
    stack_ref,
    diff_ref,
    x0_ref,
    x1_ref,
    w0_ref,
    w1_ref,
    win_ref,
    high_ref,
    low_ref,
    cut_ref,
    dc_ref,
):
    groups = ngx * ngy
    wide = COARSE * SLOTS
    lane16 = iota((SLOTS, LANES), 1)
    x_refs, w_refs = (x0_ref, x1_ref), (w0_ref, w1_ref)
    tlen = TAPS * LANES
    row_len = CHANNELS * tlen

    tri = jnp.concatenate(
        [
            iota((LANES, LANES), 0) >= iota((LANES, LANES), 1),
            iota((LANES, LANES), 0) < iota((LANES, LANES), 1),
            iota((LANES, LANES), 0) >= 0,
        ],
        axis=1,
    )
    tri = jnp.where(tri, 1.0, 0.0).astype(BF16)
    span = 2 * BLOCKS

    def windows(q, carry):
        x = data_ref[pl.ds(q * 8, 8)].astype(F32)
        energy = sum(x[:, span * c : span * (c + 1)] * x[:, span * c : span * (c + 1)] for c in range(CHANNELS))
        sums = sum(dot(part, tri) for part in pieces(energy.reshape(8 * span, LANES), 3))
        sums = sums.reshape(8, span, CHANNELS * LANES)
        mean = sums[:, 0:SLOTS, 0:LANES]
        for j in range(1, TAPS):
            mean = mean + sums[:, 2 * j : 2 * j + SLOTS, 2 * LANES :]
        mean = (mean + sums[:, 2 * TAPS : 2 * TAPS + SLOTS, LANES : 2 * LANES]) / row_len
        win_ref[q] = lax.rsqrt(mean + EPS).reshape(8 * SLOTS, LANES).T
        return carry

    lax.fori_loop(0, groups // 8, windows, 0)

    def shifted_left(get, blocks, shift):
        turned = [rot(get(j), -shift) for j in range(blocks)]
        return [lanes_before(lane16, LANES - shift, turned[j], turned[j + 1]) for j in range(blocks - 1)]

    def build_data(source, blocks, ref):
        keep = blocks - 1
        for a in range(COARSE):
            rows = slice(a * SLOTS, (a + 1) * SLOTS)
            tail = None
            for c in range(CHANNELS):
                turned = [rot(source[c][j], -FINE * a) for j in range(blocks)]
                for j in range(keep):
                    block = lanes_before(lane16, LANES - FINE * a, turned[j], turned[j + 1])
                    at = (c * keep + j) * LANES
                    ref[rows, at : at + LANES] = block
                end = rot(source[c][keep], FINE * (c - a))
                tail = end if tail is None else jnp.where(lane16 < FINE * c, tail, end)
            at = CHANNELS * keep * LANES
            ref[rows, at : at + LANES] = tail

    def build_taps(source, blocks, ref):
        zero = jnp.zeros((SLOTS, LANES), BF16)
        for b in range(FINE):
            rows = slice(b * SLOTS, (b + 1) * SLOTS)
            tail = zero
            for c in range(CHANNELS):
                before = zero
                for j in range(blocks):
                    turned = rot(source[c][j], b)
                    at = (c * blocks + j) * LANES
                    ref[rows, at : at + LANES] = lanes_before(lane16, b, before, turned)
                    before = turned
                if b:
                    end = rot(source[c][blocks - 1], b + FINE * c)
                    inside = (lane16 >= FINE * c) & (lane16 < FINE * c + b)
                    tail = jnp.where(inside, end, tail)
            at = CHANNELS * blocks * LANES
            ref[rows, at : at + LANES] = tail

    def build(g, which):
        x = data_ref[g].astype(F32)
        source = [
            [x[span * c + 2 * j : span * c + 2 * j + SLOTS].astype(BF16) for j in range(TAPS + 1)]
            for c in range(CHANNELS)
        ]
        build_data(source, TAPS + 1, x_refs[which])
        at = pl.ds(pl.multiple_of(g * SLOTS, SLOTS), SLOTS)
        tiles = sorted_ref[at, :]
        taps = [
            [tiles[:, (TAPS * c + j) * LANES : (TAPS * c + j + 1) * LANES] for j in range(TAPS)]
            for c in range(CHANNELS)
        ]
        build_taps(taps, TAPS, w_refs[which])

    own = (iota((SLOTS, wide), 0) // (SLOTS // 2)) == (iota((SLOTS, wide), 1) % 2)

    def correlate(g, which):
        raw = dot_nt(w_refs[which][...], x_refs[which][...])
        at = pl.ds(pl.multiple_of(g * SLOTS, SLOTS), SLOTS)
        scale = scale_ref[at, :]
        scale = jnp.concatenate([scale, scale], axis=1)
        turn = g % 8
        lane8 = iota((FINE, LANES), 1)
        halves = []
        for half in range(2):
            total = jnp.zeros((FINE, LANES), F32)
            for a in range(COARSE // 2):
                part = win_ref[g // 8, pl.ds((half * 8 + a) * FINE, FINE), :]
                part = pltpu.roll(part, (a - turn + 8) % 8 * SLOTS, 1)
                total = jnp.where(lane8 // SLOTS == a, part, total)
            halves.append(total)
        window = jnp.concatenate(halves, axis=1)
        for b in range(FINE):
            factor = jnp.where(own, window[b : b + 1], 0.0)
            value = raw[b * SLOTS : (b + 1) * SLOTS] * scale * factor
            high, low = pieces(value, 2)
            high_ref[b, at, :] = high
            low_ref[b, at, :] = low

    build(0, 0)

    def pair(i, carry):
        g = 2 * i
        correlate(g, 0)
        build(g + 1, 1)
        correlate(g + 1, 1)
        build(jnp.minimum(g + 2, groups - 1), 0)
        return carry

    lax.fori_loop(0, groups // 2, pair, 0)

    det_dev = time_ref.shape[1]
    lane = iota((det_dev, LANES), 1)
    row_iota = iota((det_dev, PACKED), 1)

    def cut(data, row, shift, blocks):
        picks = [row_iota == row + (span * c + 2 * j) for c in range(CHANNELS) for j in range(blocks)]
        picks = jnp.concatenate([jnp.where(pick, 1.0, 0.0) for pick in picks], axis=0).astype(BF16)
        found = dot(picks, data)
        found = [
            [found[(c * blocks + j) * det_dev : (c * blocks + j + 1) * det_dev] for j in range(blocks)]
            for c in range(CHANNELS)
        ]
        for bit in range(7):
            size = 1 << bit
            moves = (shift // size) % 2 == 1
            for c in range(CHANNELS):
                turned = [rot(found[c][j], -size) for j in range(blocks)]
                turned.append(turned[-1])
                found[c] = [
                    jnp.where(moves, jnp.where(lane < LANES - size, turned[j], turned[j + 1]), found[c][j])
                    for j in range(blocks)
                ]
        return [found[c][: blocks - 1] for c in range(CHANNELS)]

    def mean_square(blocks):
        return sum(jnp.sum(block * block, axis=1, keepdims=True) for block in blocks) / (CHANNELS * W)

    gx, gy = lax.axis_index("gx"), lax.axis_index("gy")
    start = column(time_ref[...])
    mine = cut(data_ref[gx * ngy + gy], 2 * (start // LANES) + column(station_ref[...]), start % LANES, 3)
    mine_scale = lax.rsqrt(CHANNELS * W * (mean_square([block for own_c in mine for block in own_c]) + EPS))
    diagonal = iota((SLOTS, wide), 0) == iota((SLOTS, wide), 1) % SLOTS
    parts = det_dev // SLOTS
    keep = W // LANES
    k_det = CHANNELS * keep * LANES + LANES

    scales = []
    for d, (dx, dy) in enumerate(((1, 0), (-1, 0), (0, 1), (0, -1))):
        x, y = gx + dx, gy + dy
        valid = (x >= 0) & (x < ngx) & (y >= 0) & (y < ngy)
        other = jnp.clip(x, 0, ngx - 1) * ngy + jnp.clip(y, 0, ngy - 1)
        data = data_ref[other]
        chosen = jnp.where(lane == column(partner_ref[d : d + 1, :]), 1.0, 0.0).astype(BF16)
        info = dot_nt(chosen, data[PACKED - 16 : PACKED, :])
        row = info[:, 8:9].astype(jnp.int32)
        shift = info[:, 9:10].astype(jnp.int32)
        piece = cut(data, row, shift, 4)
        centre = []
        for c in range(CHANNELS):
            centre += [
                jnp.where(lane >= HALF, piece[c][0], 0.0),
                piece[c][1],
                jnp.where(lane < HALF, piece[c][2], 0.0),
            ]
        scale = mine_scale * lax.rsqrt(mean_square(centre) + EPS)
        scales.append(jnp.where(valid, scale, 0.0))
        for c in range(CHANNELS):
            for j in range(keep + 1):
                cut_ref[d, c * (keep + 1) + j] = piece[c][j].astype(BF16)

    for q in range(parts):
        rows = slice(q * SLOTS, (q + 1) * SLOTS)
        build_taps([[mine[c][j][rows].astype(BF16) for j in range(keep)] for c in range(CHANNELS)], keep, w0_ref)
        taps = w0_ref[:, 0:k_det]
        for d in range(4):
            source = [
                [cut_ref[d, c * (keep + 1) + j, rows, :] for j in range(keep + 1)] for c in range(CHANNELS)
            ]
            ref = x_refs[d % 2]
            build_data(source, keep + 1, ref)
            raw = dot_nt(taps, ref[:, 0:k_det])
            at = d * det_dev + q * SLOTS
            for b in range(FINE):
                value = jnp.where(diagonal, raw[b * SLOTS : (b + 1) * SLOTS], 0.0)
                for n, part in enumerate(pieces(value, 2)):
                    dc_ref[n, b, at : at + SLOTS, :] = part

    tpl_dev = stack_ref.shape[0]
    block_of = (iota((tpl_dev, wide), 1) % SLOTS) // 2
    totals = jnp.zeros((BLOCKS - TAPS, tpl_dev, LANES), F32).reshape((BLOCKS - TAPS) * tpl_dev, LANES)
    lags = jnp.zeros((4 * det_dev, LANES), F32)
    for b in range(FINE):
        spread = iota((wide, LANES), 1) == (iota((wide, LANES), 0) // SLOTS) * FINE + b
        spread = jnp.where(spread, 1.0, 0.0).astype(BF16)
        contract = (((0,), (0,)), ((), ()))
        total = lax.dot_general(owner_ref[...], high_ref[b], contract, preferred_element_type=F32)
        total = total + lax.dot_general(owner_ref[...], low_ref[b], contract, preferred_element_type=F32)
        for n, part in enumerate(pieces(total, 2)):
            part = part.astype(F32)
            by_block = [jnp.where(block_of == block, part, 0.0) for block in range(BLOCKS - TAPS)]
            totals = totals + dot(jnp.concatenate(by_block, axis=0).astype(BF16), spread)
            lags = lags + dot(dc_ref[n, b], spread)
    for block in range(BLOCKS - TAPS):
        stack_ref[:, block * LANES : (block + 1) * LANES] = totals[block * tpl_dev : (block + 1) * tpl_dev] * (
            1.0 / 8.0**0.5
        )
    for d in range(4):
        diff_ref[pl.ds(d, det_dev, stride=4), :] = lags[d * det_dev : (d + 1) * det_dev] * scales[d]


def on_device(ngx, ngy, waveforms, templates, tpl_stations, det_station, det_time, partner):
    sta_dev, channels, samples = waveforms.shape
    tpl_dev, k_slots, row_len = templates.shape
    det_dev = det_station.shape[0]
    groups = ngx * ngy
    total = groups * SLOTS
    time_row, station_row = det_time.reshape(1, det_dev), det_station.reshape(1, det_dev)
    packed = pl.pallas_call(
        pack_kernel,
        out_shape=jax.ShapeDtypeStruct((groups, PACKED, LANES), BF16),
        scratch_shapes=[pltpu.VMEM((PACKED, LANES), F32)],
        name="pack",
    )(waveforms.transpose(1, 0, 2), time_row, station_row)
    data = lax.all_to_all(packed, ("gx", "gy"), split_axis=0, concat_axis=0, tiled=True)
    tiles, scale, owner = pl.pallas_call(
        tile_kernel,
        out_shape=(
            jax.ShapeDtypeStruct((total, row_len), BF16),
            jax.ShapeDtypeStruct((total, LANES), F32),
            jax.ShapeDtypeStruct((total, tpl_dev), BF16),
        ),
        compiler_params=pltpu.CompilerParams(vmem_limit_bytes=48 << 20),
        name="tiles",
    )(templates, tpl_stations.T)
    depth = row_len + LANES
    wide = COARSE * SLOTS
    stack, diff = pl.pallas_call(
        functools.partial(main_kernel, ngx, ngy),
        out_shape=(
            jax.ShapeDtypeStruct((tpl_dev, samples - row_len // CHANNELS), F32),
            jax.ShapeDtypeStruct((4 * det_dev, DTLAG), F32),
        ),
        scratch_shapes=[
            pltpu.VMEM((wide, depth), BF16),
            pltpu.VMEM((wide, depth), BF16),
            pltpu.VMEM((FINE * SLOTS, depth), BF16),
            pltpu.VMEM((FINE * SLOTS, depth), BF16),
            pltpu.VMEM((groups // 8, LANES, LANES), F32),
            pltpu.VMEM((FINE, total, wide), BF16),
            pltpu.VMEM((FINE, total, wide), BF16),
            pltpu.VMEM((4, 9, det_dev, LANES), BF16),
            pltpu.VMEM((2, FINE, 4 * det_dev, wide), BF16),
        ],
        compiler_params=pltpu.CompilerParams(vmem_limit_bytes=(12 << 20) + groups * (5 << 17)),
        name="correlate",
    )(data, tiles, scale, owner, time_row, station_row, partner.T)
    return stack, diff.reshape(det_dev, 4, DTLAG)


def solution(mesh):
    return jax.shard_map(
        functools.partial(on_device, mesh.shape["gx"], mesh.shape["gy"]),
        mesh=mesh,
        in_specs=(
            P(("gx", "gy"), None, None),
            P(("gx", "gy"), None, None),
            P(("gx", "gy"), None),
            P(("gx", "gy")),
            P(("gx", "gy")),
            P(("gx", "gy"), None),
        ),
        out_specs=(P(("gx", "gy"), None), P(("gx", "gy"), None, None)),
        check_vma=False,
    )
```

time: 1190 us -> 57.5 us (0.05)
  local copies, waits for them, and re-layouts: 950 us -> 0.02 us
  other arithmetic: 154 us -> 0 us
  matrix products: 46.8 us -> 0 us
  Pallas kernels: 0 us -> 32.4 us
  waiting for transfers between devices: 0.02 us -> 17.1 us
  starting transfers between devices: 23.6 us -> 7.1 us
    reshape x23 -> x0, local copies, waits for them, and re-layouts: 469 us -> none  [the longest x18 463 us: lagged_rows(): tiled = tiled[..., :rows * (length + 1)].reshape(lead + (rows, length + 1))]
    another operation x49 -> x0, local copies, waits for them, and re-layouts: 244 us -> none  [the longest x48 244 us: lagged_rows(): tiled = jnp.tile(series, (1,) * len(lead) + (rows + 1,))]
    slice x20 -> x0, local copies, waits for them, and re-layouts: 143 us -> none  [the longest x18 135 us: lagged_rows(): tiled = tiled[..., :rows * (length + 1)].reshape(lead + (rows, length + 1))]
    another operation x3 -> x0, other arithmetic: 142 us -> none
    gather x7 -> x0, local copies, waits for them, and re-layouts: 51.5 us -> none  [the longest x4 47.3 us: cut(): lax.dynamic_slice(waveforms, (sta, jnp.int32(0), start), (1, 3, size))[0]]
    dot_general x18 -> x0, matrix products: 46.8 us -> none  [the longest x16 39 us: window_block(): jnp.einsum('bct,bctl->bl', mine, lagged, preferred_element_type=jnp.float32)]
    while x8 -> x0, local copies, waits for them, and re-layouts: 34.4 us -> none
    pallas_call x0 -> x3, Pallas kernels: none -> 32.4 us  [the longest x1 29.7 us: on_device(): pl.pallas_call(functools.partial(main_kernel, ngx, ngy), out_shape=(jax.S...]
  transfers between devices with their start and end apart: 6 -> 1, of which waited for: 0 -> 1; matrix products, arithmetic and copies ran while one was open for 77% -> 0% of each run, Pallas kernels for 0% -> 2%
where the time goes in v1:
time: 57.5 us; the launch traced here: 57.3 us
  Pallas kernels  32.4 us (56%)
  waiting for transfers between devices  17.1 us (30%)
  starting transfers between devices  7.1 us (12%)
  between operations  0.71 us (1%)
    pallas_call x1, Pallas kernels, on_device(): pl.pallas_call(functools.partial(main_kernel, ngx, ngy), out_shape=(jax.S...  29.7 us
    all_to_all x1, waiting for transfers between devices, on_device(): lax.all_to_all(packed, ('gx', 'gy'), split_axis=0, concat_axis=0, tiled=T...  17.1 us
    all_to_all x1, starting transfers between devices, on_device(): lax.all_to_all(packed, ('gx', 'gy'), split_axis=0, concat_axis=0, tiled=T...  7.1 us
    pallas_call x1, Pallas kernels, on_device(): pl.pallas_call(pack_kernel, out_shape=jax.ShapeDtypeStruct((groups, PACKE...  1.71 us
  transfers between devices with their start and end apart: 1, of which 1 were waited for; matrix products, arithmetic and copies ran while one was open for 0% of the time, Pallas kernels for 2%

profile of v1, /device:TPU:1, one launch (start us, length us, event | category | flops | bytes accessed | tf_op | source)
XLA Modules:
  0.0 57.3 jit_solution(7748579508525271342)
XLA Ops:
  0.6 0.0 copy-start.3
  0.6 0.0 copy-start.4
  0.7 0.0 copy-start.1
  0.7 0.0 copy-start
  0.7 0.0 copy-start.2
  0.7 1.7 %pack.1 = bf16[32,80,128]{2,1,0:T(8,128)(2,1)} custom-call(bf16[3,2,1536]{2,1,0:T(2,128)(2,1)} %bitcast.12, s32[1,64]{1,0:T(1,128)} %bitcast.8, s32[1,64]{1,0:T(1,128)} %bitcast.10), custom_call_target="tpu_custom_call" | custom-call | tf_op jit(solution)/shard_map/pack/pallas_call | solution.py:364
  2.4 7.1 %all-to-all-start = ((bf16[32,80,128]{2,1,0:T(8,128)(2,1)}), bf16[32,80,128]{2,1,0:T(8,128)(2,1)S(1)}, u32[]{:S(2)}, u32[]{:S(2)}) async-start(bf16[32,80,128]{2,1,0:T(8,128)(2,1)} %pack.1), calls=%async_computation | async-start | bytes 1310720 | tf_op jit(solution)/shard_map/all_to_all | solution.py:370
  9.5 0.0 copy-done.1
  9.5 0.0 copy-done
  9.5 1.0 %tiles.1 = (bf16[512,1536]{1,0:T(8,128)(2,1)S(1)}, f32[512,128]{1,0:T(8,128)S(1)}, bf16[512,32]{1,0:T(8,128)(2,1)S(1)}) custom-call(bf16[32,8,1536]{2,1,0:T(8,128)(2,1)S(1)} %copy-done, s32[8,32]{1,0:T(8,128)S(1)} %bitcast.6), custom_call_target="tpu_custom_call" | custom-call | tf_op jit(solution)/shard_map/tiles/pallas_call | solution.py:371
  10.5 17.1 %all-to-all-done.data_ref = bf16[32,80,128]{2,1,0:T(8,128)(2,1)S(1)} async-done(((bf16[32,80,128]{2,1,0:T(8,128)(2,1)}), bf16[32,80,128]{2,1,0:T(8,128)(2,1)S(1)}, u32[]{:S(2)}, u32[]{:S(2)}) %all-to-all-start) | async-done | bytes 655392 | tf_op jit(solution)/shard_map/all_to_all | solution.py:370
  27.6 0.0 copy-done.3
  27.6 0.0 copy-done.4
  27.6 0.0 copy-done.2
  27.6 29.7 %correlate.1 = (f32[32,1024]{1,0:T(8,128)}, f32[256,128]{1,0:T(8,128)}) custom-call(bf16[32,80,128]{2,1,0:T(8,128)(2,1)S(1)} %all-to-all-done.data_ref, bf16[512,1536]{1,0:T(8,128)(2,1)S(1)} %get-tuple-element.7.sorted_ref, f32[512,128]{1,0:T(8,128)S(1)} %get-tuple-element.8.scale_ref, bf16[512,32]{1,0:T(8,128)(2,1)S(1)} %get-tuple-element.9.owner_ref, ...), custom_call_target="tpu_custom_call" | custom-call | tf_op jit(solution)/shard_map/correlate/pallas_call | solution.py:383
Async XLA Ops:
  0.6 26.9 %copy-start.3 = (s32[64]{0:T(128)S(1)}, s32[64]{0:T(128)}, u32[]{:S(2)}) copy-start(s32[64]{0:T(128)} %param.10) | copy-start | bytes 772
  0.6 26.9 %copy-start.4 = (s32[64]{0:T(128)S(1)}, s32[64]{0:T(128)}, u32[]{:S(2)}) copy-start(s32[64]{0:T(128)} %param.9) | copy-start | bytes 772
  0.7 8.8 %copy-start.1 = (s32[32,8]{0,1:T(8,128)S(1)}, s32[32,8]{0,1:T(8,128)}, u32[]{:S(2)}) copy-start(s32[32,8]{0,1:T(8,128)} %param.8) | copy-start | bytes 3076
  0.7 8.8 %copy-start = (bf16[32,8,1536]{2,1,0:T(8,128)(2,1)S(1)}, bf16[32,8,1536]{2,1,0:T(8,128)(2,1)}, u32[]{:S(2)}) copy-start(bf16[32,8,1536]{2,1,0:T(8,128)(2,1)} %tiles_ref.1) | copy-start | bytes 2359300
  0.7 26.9 %copy-start.2 = (s32[64,4]{0,1:T(4,128)S(1)}, s32[64,4]{0,1:T(4,128)}, u32[]{:S(2)}) copy-start(s32[64,4]{0,1:T(4,128)} %param.11) | copy-start | bytes 3076
  2.4 25.2 %all-to-all-start = ((bf16[32,80,128]{2,1,0:T(8,128)(2,1)}), bf16[32,80,128]{2,1,0:T(8,128)(2,1)S(1)}, u32[]{:S(2)}, u32[]{:S(2)}) async-start(bf16[32,80,128]{2,1,0:T(8,128)(2,1)} %pack.1), calls=%async_computation | async-start | bytes 1310720 | tf_op jit(solution)/shard_map/all_to_all | solution.py:370

commit v2 on v0

v2 whole, which is shorter than its diff:
```python
import functools

import jax
import jax.numpy as jnp
from jax import lax
from jax.experimental import pallas as pl
from jax.experimental.pallas import tpu as pltpu
from jax.sharding import PartitionSpec as P

LANES = 128
CHANNELS = 3
STATIONS = 2
BLOCKS = 12
TAPS = 4
LAG_BLOCKS = BLOCKS - TAPS
SLOTS = 8
FINE = 8
COARSE = LANES // FINE
DET_FINE = 16
DET_COARSE = LANES // DET_FINE
DET_ROWS = 16
W = 256
DTLAG = 128
HALF = DTLAG // 2
KEEP = W // LANES
DET_DEPTH = CHANNELS * KEEP * LANES + LANES
SPAN = STATIONS * BLOCKS
ROWS = CHANNELS * SPAN
PACKED = ROWS + 8
EPS = 1e-06
F32 = jnp.float32
BF16 = jnp.bfloat16
NT = (((1,), (1,)), ((), ()))


def iota(shape, axis):
    return lax.broadcasted_iota(jnp.int32, shape, axis)


def rot(value, shift, axis=1):
    shift = shift % value.shape[axis]
    return pltpu.roll(value, shift, axis) if shift else value


def dot(a, b):
    return jnp.dot(a, b, preferred_element_type=F32)


def dot_nt(a, b):
    return lax.dot_general(a, b, NT, preferred_element_type=F32)


def ones_where(mask):
    return jnp.where(mask, 1.0, 0.0).astype(BF16)


def pieces(value, count):
    out = []
    for _ in range(count - 1):
        high = value.astype(BF16)
        out.append(high)
        value = value - high.astype(F32)
    out.append(value.astype(BF16))
    return out


def column(row):
    n = row.shape[1]
    diagonal = iota((n, n), 0) == iota((n, n), 1)
    return jnp.sum(jnp.where(diagonal, row, 0), axis=1, keepdims=True)


def pack_kernel(wave_ref, time_ref, station_ref, out_ref, rows_ref):
    start = time_ref[...] - HALF
    row = BLOCKS * station_ref[...] + start // LANES
    shift = start % LANES
    pad = jnp.zeros((1, LANES - row.shape[1]), F32)
    for c in range(CHANNELS):
        series = wave_ref[c].astype(F32)
        for s in range(STATIONS):
            for block in range(BLOCKS):
                at = c * SPAN + s * BLOCKS + block
                rows_ref[at : at + 1, :] = series[s : s + 1, block * LANES : (block + 1) * LANES]
    rows_ref[ROWS : ROWS + 1, :] = jnp.concatenate([row.astype(F32), pad], axis=1)
    rows_ref[ROWS + 1 : ROWS + 2, :] = jnp.concatenate([shift.astype(F32), pad], axis=1)
    rows_ref[ROWS + 2 : PACKED, :] = jnp.zeros((PACKED - ROWS - 2, LANES), F32)
    out_ref[...] = jnp.broadcast_to(rows_ref[...].astype(BF16)[None], out_ref.shape)


def tile_kernel(ngx, ngy, tiles_ref, station_ref, sorted_ref, scale_ref, owner_ref):
    tpl_dev, k_slots, row_len = tiles_ref.shape
    count = tpl_dev * k_slots
    total = sorted_ref.shape[0]
    station = station_ref[...].astype(F32).astype(BF16)
    home = ones_where(iota((count, tpl_dev), 0) // k_slots == iota((count, tpl_dev), 1))
    home_t = ones_where(iota((tpl_dev, count), 1) // k_slots == iota((tpl_dev, count), 0))
    by_row = dot_nt(home, station)
    by_col = dot(station, home_t)
    own_col = iota((count, k_slots), 0) % k_slots == iota((count, k_slots), 1)
    own_row = iota((k_slots, count), 1) % k_slots == iota((k_slots, count), 0)
    st_col = jnp.sum(jnp.where(own_col, by_row, 0.0), axis=1, keepdims=True)
    st_row = jnp.sum(jnp.where(own_row, by_col, 0.0), axis=0, keepdims=True)
    earlier = iota((count, count), 0) < iota((count, count), 1)
    rank = jnp.sum(jnp.where((st_col == st_row) & earlier, 1.0, 0.0), axis=0, keepdims=True)
    st = st_row.astype(jnp.int32)
    group = st // STATIONS
    x, y = group // ngy, group % ngy
    away = (x + lax.axis_index("gx")) % 2
    place_of = away * (ngx * ngy // 2) + x // 2 * ngy + y
    slot = (place_of * STATIONS + st % STATIONS) * SLOTS + rank.astype(jnp.int32)
    tiles = tiles_ref[...].reshape(count, row_len)
    step = 128
    for first in range(0, total, step):
        place = ones_where(iota((step, count), 0) + first == slot)
        moved = dot(place, tiles)
        sorted_ref[first : first + step, :] = moved.astype(BF16)
        mean = jnp.sum(moved * moved, axis=1, keepdims=True) / row_len
        scale = lax.rsqrt(row_len * (mean + EPS))
        scale_ref[first : first + step, :] = jnp.broadcast_to(scale, (step, LANES))
        owner_ref[:, first : first + step] = dot_nt(home_t, place).astype(BF16)


def window_scales(data_ref, rows_ref, win_ref):
    groups = data_ref.shape[0]
    step = min(8, groups)
    column_of = iota((LANES, LANES), 1)
    sample = FINE * (COARSE - 1 - column_of % COARSE) + column_of // COARSE
    row = iota((LANES, LANES), 0)
    sums_of = ones_where(jnp.concatenate([row >= sample, row < sample, row >= 0], axis=1))
    major, chunk = iota((step, FINE, LANES), 1), iota((step, FINE, LANES), 2) // COARSE

    def body(q, carry):
        x = data_ref[pl.ds(q * step, step)].astype(F32)
        rows_ref[pl.ds(q * step, step)] = x
        energy = sum(x[:, SPAN * c : SPAN * (c + 1)] * x[:, SPAN * c : SPAN * (c + 1)] for c in range(CHANNELS))
        sums = sum(dot(part, sums_of) for part in pieces(energy.reshape(step * SPAN, LANES), 3))
        sums = sums.reshape(step, SPAN, 3 * LANES)
        for s in range(STATIONS):
            at = BLOCKS * s
            mean = sums[:, at : at + LAG_BLOCKS, 0:LANES]
            for j in range(1, TAPS):
                mean = mean + sums[:, at + j : at + j + LAG_BLOCKS, 2 * LANES :]
            mean = (mean + sums[:, at + TAPS : at + TAPS + LAG_BLOCKS, LANES : 2 * LANES]) / (
                CHANNELS * TAPS * LANES
            )
            value = lax.rsqrt(mean + EPS)
            for bit in range(3):
                size = 1 << bit
                up = (major // size) % 2
                other = (chunk // size) % 2
                later = rot(rot(value, -size, 1), size * COARSE, 2)
                earlier = rot(rot(value, size, 1), -size * COARSE, 2)
                value = jnp.where(up == other, value, jnp.where(up == 0, later, earlier))
            win_ref[pl.ds(q * step, step), s] = value
        return carry

    lax.fori_loop(0, groups // step, body, 0)


def build_data(rows_ref, g, s, out_ref):
    lane = iota((COARSE, LANES), 1)
    bound = FINE * (iota((COARSE, LANES), 0) + 1)
    for c in range(CHANNELS):
        now = None
        for block in range(BLOCKS):
            at = SPAN * c + BLOCKS * s + block
            row = jnp.broadcast_to(rows_ref[g, at : at + 1, :], (COARSE, LANES))
            later = pltpu.roll(row, FINE, 1, stride=FINE, stride_axis=0).astype(BF16)
            if block:
                out_ref[(block - 1) * COARSE : block * COARSE, c * LANES : (c + 1) * LANES] = jnp.where(
                    lane < bound, now, later
                )
            now = later
        out_ref[(BLOCKS - 1) * COARSE : BLOCKS * COARSE, c * LANES : (c + 1) * LANES] = now


def build_taps(blocks_of, fine, height, out_ref, first, step):
    lane = iota((height, LANES), 1)
    zero = jnp.zeros((height, LANES), BF16)
    for b in range(fine):
        rows = slice(first + step * b, first + step * b + height)
        tail = zero
        at = 0
        for c, blocks in enumerate(blocks_of):
            before = zero
            for block in blocks:
                moved = rot(block, b)
                out_ref[rows, at : at + LANES] = jnp.where(lane < b, before, moved) if b else moved
                before = moved
                at += LANES
            if b:
                end = rot(blocks[-1], b + fine * c)
                tail = jnp.where((lane >= fine * c) & (lane < fine * c + b), end, tail)
        out_ref[rows, at : at + LANES] = tail


def taps_kernel(sorted_ref, out_ref):
    height = FINE * STATIONS * SLOTS
    per_step = out_ref.shape[0] // height
    rows = STATIONS * SLOTS
    lane = iota((rows, LANES), 1)
    zero = jnp.zeros((rows, LANES), BF16)

    def body(i, carry):
        at = (pl.program_id(0) * per_step + i) * rows
        tiles = sorted_ref[pl.ds(pl.multiple_of(at, rows), rows), :]
        out = out_ref.at[pl.ds(pl.multiple_of(i * height, height), height), :]
        for c in range(CHANNELS):
            blocks = [tiles[:, (TAPS * c + j) * LANES : (TAPS * c + j + 1) * LANES] for j in range(TAPS)]
            for b in range(FINE):
                before = zero
                for j in range(TAPS + 1):
                    moved = rot(blocks[j], b) if j < TAPS else zero
                    lanes = slice((c * (TAPS + 1) + j) * LANES, (c * (TAPS + 1) + j + 1) * LANES)
                    out[b * rows : (b + 1) * rows, lanes] = jnp.where(lane < b, before, moved) if b else moved
                    before = moved
        return carry

    lax.fori_loop(0, per_step, body, 0)


def correlate_kernel(call, data_ref, taps_ref, scale_ref, *refs):
    if call:
        owner_ref, first_high_ref, first_low_ref, stack_ref, high_ref, low_ref = refs[:6]
        refs = refs[6:]
    else:
        high_ref, low_ref = refs[:2]
        refs = refs[2:]
    rows_ref, win_ref = refs[:2]
    x_refs = (refs[2:4], refs[4:6])
    groups = data_ref.shape[0]
    rows = STATIONS * SLOTS
    height = FINE * rows
    per_step = taps_ref.shape[0] // height
    step = pl.program_id(0)

    def build(g, which):
        for s in range(STATIONS):
            build_data(rows_ref, g, s, x_refs[which][s])

    @pl.when(step == 0)
    def _():
        window_scales(data_ref, rows_ref, win_ref)
        build(0, 0)

    def lags(i, which):
        g = step * per_step + i
        taps = taps_ref[pl.ds(pl.multiple_of(i * height, height), height), :]
        data = [
            jnp.concatenate(
                [
                    ref[j * COARSE : j * COARSE + LANES, c * LANES : (c + 1) * LANES]
                    for c in range(CHANNELS)
                    for j in range(TAPS + 1)
                ],
                axis=1,
            )
            for ref in x_refs[which]
        ]
        raw = dot_nt(taps, jnp.concatenate(data, axis=0))
        scale = scale_ref[pl.ds(pl.multiple_of((call * groups + g) * rows, rows), rows), :]
        at = pl.ds(pl.multiple_of(g * rows, rows), rows)
        for b in range(FINE):
            value, window = [], []
            for s in range(STATIONS):
                first = b * rows + s * SLOTS
                value.append(raw[first : first + SLOTS, s * LANES : (s + 1) * LANES])
                window.append(jnp.broadcast_to(win_ref[g, s, b : b + 1, :], (SLOTS, LANES)))
            value = jnp.concatenate(value, axis=0) * scale * jnp.concatenate(window, axis=0)
            high, low = pieces(value, 2)
            high_ref[at, b * LANES : (b + 1) * LANES] = high
            low_ref[at, b * LANES : (b + 1) * LANES] = low

    def body(i, carry):
        g = step * per_step + 2 * i
        lags(2 * i, 0)
        build(g + 1, 1)
        lags(2 * i + 1, 1)
        build(jnp.minimum(g + 2, groups - 1), 0)
        return carry

    lax.fori_loop(0, per_step // 2, body, 0)

    if call:

        @pl.when(step == pl.num_programs(0) - 1)
        def _():
            half = groups * rows
            total = 0.0
            for first, second in ((first_high_ref, high_ref), (first_low_ref, low_ref)):
                total = total + dot(owner_ref[:, 0:half], first[...]) + dot(owner_ref[:, half:], second[...])
            stack_lags(total, stack_ref)


def stack_lags(total, stack_ref):
    tpl_dev = stack_ref.shape[0]
    block_of = iota((tpl_dev, FINE * LANES), 1) % LANES // COARSE
    place = iota((FINE * LANES, LANES), 0)
    spread = iota((FINE * LANES, LANES), 1) == FINE * (COARSE - 1 - place % COARSE) + place // LANES
    spread = ones_where(spread)
    out = 0.0
    for part in pieces(total, 2):
        part = part.astype(F32)
        masked = [jnp.where(block_of == block, part, 0.0) for block in range(LAG_BLOCKS)]
        out = out + dot(jnp.concatenate(masked, axis=0).astype(BF16), spread)
    for block in range(LAG_BLOCKS):
        rows = out[block * tpl_dev : (block + 1) * tpl_dev]
        stack_ref[:, block * LANES : (block + 1) * LANES] = rows * (1.0 / 8.0**0.5)


def cut(data, row, shift, blocks):
    det_dev = row.shape[0]
    row_iota, lane = iota((det_dev, PACKED), 1), iota((det_dev, LANES), 1)
    picks = [row_iota == row + (SPAN * c + j) for c in range(CHANNELS) for j in range(blocks)]
    picks = jnp.concatenate([jnp.where(pick, 1.0, 0.0) for pick in picks], axis=0).astype(BF16)
    found = dot(picks, data).astype(BF16)
    found = [
        [found[(c * blocks + j) * det_dev : (c * blocks + j + 1) * det_dev] for j in range(blocks)]
        for c in range(CHANNELS)
    ]
    shift = jnp.broadcast_to(shift, (det_dev, LANES))
    for bit in range(7):
        size = 1 << bit
        moves = (shift // size) % 2 == 1
        inner = lane < LANES - size
        for c in range(CHANNELS):
            turned = [rot(found[c][j], -size) for j in range(blocks)]
            turned.append(turned[-1])
            found[c] = [
                jnp.where(moves, jnp.where(inner, turned[j], turned[j + 1]), found[c][j]) for j in range(blocks)
            ]
    return [found[c][: blocks - 1] for c in range(CHANNELS)]


def mean_square(blocks):
    total = 0.0
    for block, mask in blocks:
        block = block.astype(F32)
        square = block * block
        total = total + (square if mask is None else jnp.where(mask, square, 0.0))
    return jnp.sum(total, axis=1, keepdims=True) / (CHANNELS * W)


def own_windows(data, time_ref, station_ref):
    start = column(time_ref[...])
    row = column(station_ref[...]) * BLOCKS + start // LANES
    mine = cut(data, row, start % LANES, KEEP + 1)
    scale = lax.rsqrt(CHANNELS * W * (mean_square([(block, None) for blocks in mine for block in blocks]) + EPS))
    return mine, scale


def partner_windows(data, chosen_row):
    det_dev = chosen_row.shape[1]
    lane = iota((det_dev, LANES), 1)
    info = dot_nt(ones_where(lane == column(chosen_row)), data[PACKED - 16 : PACKED, :])
    pieces_of = cut(data, info[:, 8:9].astype(jnp.int32), info[:, 9:10].astype(jnp.int32), KEEP + 2)
    centre = []
    for first, middle, last in pieces_of:
        centre += [(first, lane >= HALF), (middle, None), (last, lane < HALF)]
    return pieces_of, lax.rsqrt(mean_square(centre) + EPS)


def differential(mine, windows, x_ref, w_ref, parts_ref):
    count = len(windows)
    det_dev = mine[0][0].shape[0]
    height = count * DET_ROWS
    lane = iota((DET_ROWS, LANES), 1)
    wide = DET_FINE * DET_ROWS
    diagonal = iota((height, wide), 0) % DET_ROWS == iota((height, wide), 1) % DET_ROWS
    for q in range(det_dev // DET_ROWS):
        rows = slice(q * DET_ROWS, (q + 1) * DET_ROWS)
        build_taps([[block[rows] for block in blocks] for blocks in mine], DET_FINE, DET_ROWS, w_ref, 0, DET_ROWS)
        for d in range(count):
            source = [[block[rows] for block in blocks] for blocks in windows[d]]
            for a in range(DET_COARSE):
                shift = DET_FINE * a
                out = slice((a * count + d) * DET_ROWS, (a * count + d + 1) * DET_ROWS)
                tail = None
                for c in range(CHANNELS):
                    moved = [rot(block, -shift) for block in source[c]]
                    for j in range(KEEP):
                        block = jnp.where(lane < LANES - shift, moved[j], moved[j + 1]) if a else moved[j]
                        at = (c * KEEP + j) * LANES
                        x_ref[out, at : at + LANES] = block
                    end = rot(source[c][KEEP], DET_FINE * c - shift)
                    tail = end if tail is None else jnp.where(lane < DET_FINE * c, tail, end)
                x_ref[out, DET_DEPTH - LANES : DET_DEPTH] = tail
        raw = dot_nt(x_ref[0 : DET_COARSE * height, :], w_ref[...])
        for a in range(DET_COARSE):
            value = jnp.where(diagonal, raw[a * height : (a + 1) * height], 0.0)
            for n, part in enumerate(pieces(value, 2)):
                parts_ref[n, a, q * height : (q + 1) * height, :] = part
    place = iota((wide, LANES), 0)
    out = 0.0
    total = det_dev * count
    for a in range(DET_COARSE):
        spread = ones_where(iota((wide, LANES), 1) == DET_FINE * a + place // DET_ROWS)
        for n in range(2):
            out = out + dot(parts_ref[n, a, 0:total, :], spread)
    return out


def detect_kernel(
    ngx, ngy, near_ref, far_ref, time_ref, station_ref, partner_ref, diff_ref, x_ref, w_ref, parts_ref
):
    gx, gy = lax.axis_index("gx"), lax.axis_index("gy")
    mine, mine_scale = own_windows(near_ref[gx // 2 * ngy + gy], time_ref, station_ref)
    windows, scales = [], []
    for d, (dx, dy) in enumerate(((1, 0), (-1, 0), (0, 1), (0, -1))):
        x, y = gx + dx, gy + dy
        valid = (x >= 0) & (x < ngx) & (y >= 0) & (y < ngy)
        other = jnp.clip(x, 0, ngx - 1) // 2 * ngy + jnp.clip(y, 0, ngy - 1)
        data = (far_ref if dx else near_ref)[other]
        found, scale = partner_windows(data, partner_ref[d : d + 1, :])
        windows.append(found)
        scales.append(jnp.where(valid, mine_scale * scale, 0.0))
    out = differential(mine, windows, x_ref, w_ref, parts_ref)
    for q in range(time_ref.shape[1] // DET_ROWS):
        for d in range(4):
            at = (q * 4 + d) * DET_ROWS
            rows = slice(q * DET_ROWS, (q + 1) * DET_ROWS)
            diff_ref[pl.ds(q * DET_ROWS * 4 + d, DET_ROWS, stride=4), :] = (
                out[at : at + DET_ROWS] * scales[d][rows]
            )


def on_device(ngx, ngy, waveforms, templates, tpl_stations, det_station, det_time, partner):
    tpl_dev, k_slots, row_len = templates.shape
    det_dev = det_station.shape[0]
    groups = ngx * ngy
    half = groups // 2
    rows = STATIONS * SLOTS
    total = groups * rows
    time_row, station_row = det_time.reshape(1, det_dev), det_station.reshape(1, det_dev)
    packed = pl.pallas_call(
        pack_kernel,
        out_shape=jax.ShapeDtypeStruct((half, PACKED, LANES), BF16),
        scratch_shapes=[pltpu.VMEM((PACKED, LANES), F32)],
        name="pack",
    )(waveforms.transpose(1, 0, 2), time_row, station_row)
    members = [[x * ngy + y for x in range(parity, ngx, 2) for y in range(ngy)] for parity in range(2)]
    near = lax.all_to_all(
        packed, ("gx", "gy"), split_axis=0, concat_axis=0, axis_index_groups=members, tiled=True
    )
    tiles, scale, owner = pl.pallas_call(
        functools.partial(tile_kernel, ngx, ngy),
        out_shape=(
            jax.ShapeDtypeStruct((total, row_len), BF16),
            jax.ShapeDtypeStruct((total, LANES), F32),
            jax.ShapeDtypeStruct((tpl_dev, total), BF16),
        ),
        compiler_params=pltpu.CompilerParams(vmem_limit_bytes=24 << 20),
        name="tiles",
    )(templates, tpl_stations.T)
    steps = groups // 4
    height = 4 * FINE * rows
    depth = CHANNELS * (TAPS + 1) * LANES
    taps = pl.pallas_call(
        taps_kernel,
        grid=(steps,),
        in_specs=[pl.BlockSpec((total, row_len), lambda i: (0, 0))],
        out_specs=pl.BlockSpec((height, depth), lambda i: (i, 0)),
        out_shape=pltpu.HBM((steps * height, depth), BF16),
        compiler_params=pltpu.CompilerParams(vmem_limit_bytes=(8 << 20) + total * row_len * 4),
        name="taps",
    )(tiles)
    taps = pltpu.with_memory_space_constraint(taps, pltpu.HBM)
    far = lax.ppermute(near, "gx", [(x, x ^ 1) for x in range(ngx)])

    def whole(*shape):
        return pl.BlockSpec(shape, lambda i: (0,) * len(shape))

    sums = (half * rows, FINE * LANES)
    scratch = [
        pltpu.VMEM((half, PACKED, LANES), F32),
        pltpu.VMEM((half, STATIONS, FINE, LANES), F32),
    ] + [pltpu.VMEM((BLOCKS * COARSE, CHANNELS * LANES), BF16)] * 4
    params = pltpu.CompilerParams(vmem_limit_bytes=(16 << 20) + groups * (1 << 17))

    def specs(call):
        return [
            whole(half, PACKED, LANES),
            pl.BlockSpec((height, depth), lambda i: (call * steps // 2 + i, 0)),
            whole(*scale.shape),
        ]

    high, low = pl.pallas_call(
        functools.partial(correlate_kernel, 0),
        grid=(steps // 2,),
        in_specs=specs(0),
        out_specs=(whole(*sums), whole(*sums)),
        out_shape=(jax.ShapeDtypeStruct(sums, BF16),) * 2,
        scratch_shapes=scratch,
        compiler_params=params,
        name="correlate_near",
    )(near, taps, scale)
    stack = pl.pallas_call(
        functools.partial(correlate_kernel, 1),
        grid=(steps // 2,),
        in_specs=specs(1) + [whole(*owner.shape), whole(*sums), whole(*sums)],
        out_specs=whole(tpl_dev, LAG_BLOCKS * LANES),
        out_shape=jax.ShapeDtypeStruct((tpl_dev, LAG_BLOCKS * LANES), F32),
        scratch_shapes=[pltpu.VMEM(sums, BF16)] * 2 + scratch,
        compiler_params=params,
        name="correlate_far",
    )(far, taps, scale, owner, high, low)
    diff = pl.pallas_call(
        functools.partial(detect_kernel, ngx, ngy),
        out_shape=jax.ShapeDtypeStruct((4 * det_dev, DTLAG), F32),
        scratch_shapes=[
            pltpu.VMEM((4 * DET_COARSE * DET_ROWS, DET_DEPTH), BF16),
            pltpu.VMEM((DET_FINE * DET_ROWS, DET_DEPTH), BF16),
            pltpu.VMEM((2, DET_COARSE, 4 * det_dev, DET_FINE * DET_ROWS), BF16),
        ],
        compiler_params=pltpu.CompilerParams(vmem_limit_bytes=(16 << 20) + groups * (1 << 15)),
        name="detect",
    )(near, far, time_row, station_row, partner.T)
    return stack, diff.reshape(det_dev, 4, DTLAG)


def solution(mesh):
    return jax.shard_map(
        functools.partial(on_device, mesh.shape["gx"], mesh.shape["gy"]),
        mesh=mesh,
        in_specs=(
            P(("gx", "gy"), None, None),
            P(("gx", "gy"), None, None),
            P(("gx", "gy"), None),
            P(("gx", "gy")),
            P(("gx", "gy")),
            P(("gx", "gy"), None),
        ),
        out_specs=(P(("gx", "gy"), None), P(("gx", "gy"), None, None)),
        check_vma=False,
    )
```

time: 1190 us -> 63 us (0.05)
  local copies, waits for them, and re-layouts: 950 us -> 1.84 us
  other arithmetic: 154 us -> 0 us
  matrix products: 46.8 us -> 0 us
  Pallas kernels: 0 us -> 39.8 us
  starting transfers between devices: 23.6 us -> 1.96 us
  blocking collectives: 0 us -> 18.4 us
    reshape x23 -> x0, local copies, waits for them, and re-layouts: 469 us -> none  [the longest x18 463 us: lagged_rows(): tiled = tiled[..., :rows * (length + 1)].reshape(lead + (rows, length + 1))]
    another operation x49 -> x0, local copies, waits for them, and re-layouts: 244 us -> none  [the longest x48 244 us: lagged_rows(): tiled = jnp.tile(series, (1,) * len(lead) + (rows + 1,))]
    slice x20 -> x0, local copies, waits for them, and re-layouts: 143 us -> none  [the longest x18 135 us: lagged_rows(): tiled = tiled[..., :rows * (length + 1)].reshape(lead + (rows, length + 1))]
    another operation x3 -> x0, other arithmetic: 142 us -> none
    gather x7 -> x0, local copies, waits for them, and re-layouts: 51.5 us -> none  [the longest x4 47.3 us: cut(): lax.dynamic_slice(waveforms, (sta, jnp.int32(0), start), (1, 3, size))[0]]
    dot_general x18 -> x0, matrix products: 46.8 us -> none  [the longest x16 39 us: window_block(): jnp.einsum('bct,bctl->bl', mine, lagged, preferred_element_type=jnp.float32)]
    pallas_call x0 -> x6, Pallas kernels: none -> 39.8 us  [the longest x1 10.8 us: on_device(): pl.pallas_call(functools.partial(correlate_kernel, 1), grid=(steps // 2,)...]
    while x8 -> x0, local copies, waits for them, and re-layouts: 34.4 us -> none
  transfers between devices with their start and end apart: 6 -> 1, of which waited for: 0 -> 0; matrix products, arithmetic and copies ran while one was open for 77% -> 0% of each run, Pallas kernels for 0% -> 30%
where the time goes in v2:
time: 63 us; the launch traced here: 62.7 us
  Pallas kernels  39.8 us (63%)
  blocking collectives  18.4 us (29%)
  starting transfers between devices  1.96 us (3%)
  local copies, waits for them, and re-layouts  1.84 us (3%)
  between operations  0.7 us (1%)
    all_to_all x1, blocking collectives, on_device(): lax.all_to_all(packed, ('gx', 'gy'), split_axis=0, concat_axis=0, axis_in...  18.4 us
    pallas_call x1, Pallas kernels, on_device(): pl.pallas_call(functools.partial(correlate_kernel, 1), grid=(steps // 2,)...  10.8 us
    pallas_call x1, Pallas kernels, on_device(): pl.pallas_call(functools.partial(correlate_kernel, 0), grid=(steps // 2,)...  9.27 us
    pallas_call x1, Pallas kernels, on_device(): pl.pallas_call(functools.partial(detect_kernel, ngx, ngy), out_shape=jax....  8.67 us
    pallas_call x1, Pallas kernels, on_device(): pl.pallas_call(taps_kernel, grid=(steps,), in_specs=[pl.BlockSpec((total,...  8.55 us
    ppermute x1, starting transfers between devices, on_device(): far = lax.ppermute(near, 'gx', [(x, x ^ 1) for x in range(ngx)])  1.96 us
    unnamed x10, local copies, waits for them, and re-layouts  1.84 us
    pallas_call x1, Pallas kernels, on_device(): pl.pallas_call(pack_kernel, out_shape=jax.ShapeDtypeStruct((half, PACKED,...  1.52 us
  transfers between devices with their start and end apart: 1, of which 0 were waited for; matrix products, arithmetic and copies ran while one was open for 0% of the time, Pallas kernels for 30%

profile of v2, /device:TPU:1, one launch (start us, length us, event | category | flops | bytes accessed | tf_op | source)
XLA Modules:
  0.0 62.7 jit_solution(8995414041516122622)
XLA Ops:
  0.6 1.5 %pack.1 = bf16[16,80,128]{2,1,0:T(8,128)(2,1)} custom-call(bf16[3,2,1536]{2,1,0:T(2,128)(2,1)} %bitcast.13, s32[1,64]{1,0:T(1,128)} %bitcast.8, s32[1,64]{1,0:T(1,128)} %bitcast.10), custom_call_target="tpu_custom_call" | custom-call | tf_op jit(solution)/shard_map/pack/pallas_call | solution.py:435
  2.1 18.4 %all_to_all.5.data_ref.near_ref = bf16[16,80,128]{2,1,0:T(8,128)(2,1)S(1)} all-to-all(bf16[16,80,128]{2,1,0:T(8,128)(2,1)} %pack.1), channel_id=1, replica_groups={{0,1,2,3,8,9,10,11,16,17,18,19,24,25,26,27},{4,5,6,7,12,13,14,15,20,21,..., dimensions={0} | all-to-all | bytes 655360 | tf_op jit(solution)/shard_map/all_to_all | solution.py:442
  20.5 2.0 %collective-permute-start = (bf16[16,80,128]{2,1,0:T(8,128)(2,1)S(1)}, bf16[16,80,128]{2,1,0:T(8,128)(2,1)S(1)}, u32[]{:S(2)}, u32[]{:S(2)}) collective-permute-start(bf16[16,80,128]{2,1,0:T(8,128)(2,1)S(1)} %all_to_all.5.data_ref.near_ref), channel_id=1, source_target_pairs={{0,4},{4,0},{8,12},{12,8},{16,20},{20,16},{24,28},{28,24},{1,5},{5... | collective-permute-start | bytes 983048 | tf_op jit(solution)/shard_map/ppermute | solution.py:468
  22.5 0.0 copy-start
  22.5 1.1 %copy-done = bf16[32,8,1536]{2,1,0:T(8,128)(2,1)S(1)} copy-done((bf16[32,8,1536]{2,1,0:T(8,128)(2,1)S(1)}, bf16[32,8,1536]{2,1,0:T(8,128)(2,1)}, u32[]{:S(2)}) %copy-start) | copy-done | bytes 786456
  23.6 0.0 copy-start.1
  23.6 0.7 %copy-done.1 = s32[32,8]{0,1:T(8,128)S(1)} copy-done((s32[32,8]{0,1:T(8,128)S(1)}, s32[32,8]{0,1:T(8,128)}, u32[]{:S(2)}) %copy-start.1) | copy-done | bytes 1048
  24.3 1.0 %tiles.1 = (bf16[512,1536]{1,0:T(8,128)(2,1)S(1)}, f32[512,128]{1,0:T(8,128)S(1)}, bf16[32,512]{1,0:T(8,128)(2,1)S(1)}) custom-call(bf16[32,8,1536]{2,1,0:T(8,128)(2,1)S(1)} %copy-done, s32[8,32]{1,0:T(8,128)S(1)} %bitcast.6), custom_call_target="tpu_custom_call" | custom-call | tf_op jit(solution)/shard_map/tiles/pallas_call | solution.py:445
  25.3 0.0 copy-start.2
  25.3 0.0 copy-start.3
  25.3 0.0 copy-start.4
  25.3 8.5 %taps.1.taps_ref = bf16[4096,1920]{1,0:T(8,128)(2,1)} custom-call(bf16[512,1536]{1,0:T(8,128)(2,1)S(1)} %get-tuple-element.7.sorted_ref), custom_call_target="tpu_custom_call" | custom-call | tf_op jit(solution)/shard_map/taps/pallas_call | solution.py:458
  33.9 9.3 %correlate_near.1 = (bf16[256,1024]{1,0:T(8,128)(2,1)S(1)}, bf16[256,1024]{1,0:T(8,128)(2,1)S(1)}) custom-call(bf16[16,80,128]{2,1,0:T(8,128)(2,1)S(1)} %all_to_all.5.data_ref.near_ref, bf16[4096,1920]{1,0:T(8,128)(2,1)} %taps.1.taps_ref, f32[512,128]{1,0:T(8,128)S(1)} %get-tuple-element.8.scale_ref), custom_call_target="tpu_custom_call" | custom-call | tf_op jit(solution)/shard_map/correlate_near/pallas_call | solution.py:487
  43.2 0.0 collective-permute-done.data_ref.far_ref
  43.2 0.0 copy-done.2
  43.2 0.0 copy-done.3
  43.2 0.0 copy-done.4
  43.2 8.7 %detect.1 = f32[256,128]{1,0:T(8,128)} custom-call(bf16[16,80,128]{2,1,0:T(8,128)(2,1)S(1)} %all_to_all.5.data_ref.near_ref, bf16[16,80,128]{2,1,0:T(8,128)(2,1)S(1)} %collective-permute-done.data_ref.far_ref, s32[1,64]{1,0:T(1,128)S(1)} %bitcast.9, s32[1,64]{1,0:T(1,128)S(1)} %bitcast.11, s32[4,64]{1,0:T(4,128)S(1)} %bitcast.7), custom_call_target="tpu_custom_call" | custom-call | tf_op jit(solution)/shard_map/detect/pallas_call | solution.py:507
  51.9 10.8 %correlate_far.1 = f32[32,1024]{1,0:T(8,128)} custom-call(bf16[16,80,128]{2,1,0:T(8,128)(2,1)S(1)} %collective-permute-done.data_ref.far_ref, bf16[4096,1920]{1,0:T(8,128)(2,1)} %taps.1.taps_ref, f32[512,128]{1,0:T(8,128)S(1)} %get-tuple-element.8.scale_ref, bf16[32,512]{1,0:T(8,128)(2,1)S(1)} %get-tuple-element.9.refs_0_, ...), custom_call_target="tpu_custom_call" | custom-call | tf_op jit(solution)/shard_map/correlate_far/pallas_call | solution.py:497
Async XLA Ops:
  20.5 22.6 %collective-permute-start = (bf16[16,80,128]{2,1,0:T(8,128)(2,1)S(1)}, bf16[16,80,128]{2,1,0:T(8,128)(2,1)S(1)}, u32[]{:S(2)}, u32[]{:S(2)}) collective-permute-start(bf16[16,80,128]{2,1,0:T(8,128)(2,1)S(1)} %all_to_all.5.data_ref.near_ref), channel_id=1, source_target_pairs={{0,4},{4,0},{8,12},{12,8},{16,20},{20,16},{24,28},{28,24},{1,5},{5... | collective-permute-start | bytes 983048 | tf_op jit(solution)/shard_map/ppermute | solution.py:468
  22.5 1.1 %copy-start = (bf16[32,8,1536]{2,1,0:T(8,128)(2,1)S(1)}, bf16[32,8,1536]{2,1,0:T(8,128)(2,1)}, u32[]{:S(2)}) copy-start(bf16[32,8,1536]{2,1,0:T(8,128)(2,1)} %tiles_ref.1) | copy-start | bytes 2359300
  23.6 0.7 %copy-start.1 = (s32[32,8]{0,1:T(8,128)S(1)}, s32[32,8]{0,1:T(8,128)}, u32[]{:S(2)}) copy-start(s32[32,8]{0,1:T(8,128)} %param.8) | copy-start | bytes 3076
  25.3 17.9 %copy-start.2 = (s32[64,4]{0,1:T(4,128)S(1)}, s32[64,4]{0,1:T(4,128)}, u32[]{:S(2)}) copy-start(s32[64,4]{0,1:T(4,128)} %param.11) | copy-start | bytes 3076
  25.3 17.9 %copy-start.3 = (s32[64]{0:T(128)S(1)}, s32[64]{0:T(128)}, u32[]{:S(2)}) copy-start(s32[64]{0:T(128)} %param.10) | copy-start | bytes 772
  25.3 17.9 %copy-start.4 = (s32[64]{0:T(128)S(1)}, s32[64]{0:T(128)}, u32[]{:S(2)}) copy-start(s32[64]{0:T(128)} %param.9) | copy-start | bytes 772

commit v3 on v2

--- a/solution.py
+++ b/solution.py
@@ -27,6 +27,9 @@
 SPAN = STATIONS * BLOCKS
 ROWS = CHANNELS * SPAN
 PACKED = ROWS + 8
+MXU = 256
+PASSES = (CHANNELS * (TAPS + 1) + 1) // 2
+SENT = 128
 EPS = 1e-06
 F32 = jnp.float32
 BF16 = jnp.bfloat16
@@ -84,7 +87,9 @@
     rows_ref[ROWS : ROWS + 1, :] = jnp.concatenate([row.astype(F32), pad], axis=1)
     rows_ref[ROWS + 1 : ROWS + 2, :] = jnp.concatenate([shift.astype(F32), pad], axis=1)
     rows_ref[ROWS + 2 : PACKED, :] = jnp.zeros((PACKED - ROWS - 2, LANES), F32)
-    out_ref[...] = jnp.broadcast_to(rows_ref[...].astype(BF16)[None], out_ref.shape)
+    count = out_ref.shape[0]
+    out_ref[:, 0:PACKED] = jnp.broadcast_to(rows_ref[...].astype(BF16)[None], (count, PACKED, LANES))
+    out_ref[:, PACKED:] = jnp.zeros((count, SENT - PACKED, LANES), BF16)
 
 
 def tile_kernel(ngx, ngy, tiles_ref, station_ref, sorted_ref, scale_ref, owner_ref):
@@ -120,7 +125,7 @@
         owner_ref[:, first : first + step] = dot_nt(home_t, place).astype(BF16)
 
 
-def window_scales(data_ref, rows_ref, win_ref):
+def windows_kernel(data_ref, rows_ref, win_ref):
     groups = data_ref.shape[0]
     step = min(8, groups)
     column_of = iota((LANES, LANES), 1)
@@ -130,7 +135,7 @@
     major, chunk = iota((step, FINE, LANES), 1), iota((step, FINE, LANES), 2) // COARSE
 
     def body(q, carry):
-        x = data_ref[pl.ds(q * step, step)].astype(F32)
+        x = data_ref[pl.ds(q * step, step), 0:PACKED].astype(F32)
         rows_ref[pl.ds(q * step, step)] = x
         energy = sum(x[:, SPAN * c : SPAN * (c + 1)] * x[:, SPAN * c : SPAN * (c + 1)] for c in range(CHANNELS))
         sums = sum(dot(part, sums_of) for part in pieces(energy.reshape(step * SPAN, LANES), 3))
@@ -157,21 +162,20 @@
     lax.fori_loop(0, groups // step, body, 0)
 
 
-def build_data(rows_ref, g, s, out_ref):
+def build_data(rows_ref, g, s, c, out_ref):
     lane = iota((COARSE, LANES), 1)
     bound = FINE * (iota((COARSE, LANES), 0) + 1)
-    for c in range(CHANNELS):
-        now = None
-        for block in range(BLOCKS):
-            at = SPAN * c + BLOCKS * s + block
-            row = jnp.broadcast_to(rows_ref[g, at : at + 1, :], (COARSE, LANES))
-            later = pltpu.roll(row, FINE, 1, stride=FINE, stride_axis=0).astype(BF16)
-            if block:
-                out_ref[(block - 1) * COARSE : block * COARSE, c * LANES : (c + 1) * LANES] = jnp.where(
-                    lane < bound, now, later
-                )
-            now = later
-        out_ref[(BLOCKS - 1) * COARSE : BLOCKS * COARSE, c * LANES : (c + 1) * LANES] = now
+    now = None
+    for block in range(BLOCKS):
+        at = SPAN * c + BLOCKS * s + block
+        row = jnp.broadcast_to(rows_ref[g, at : at + 1, :], (COARSE, LANES))
+        later = pltpu.roll(row, FINE, 1, stride=FINE, stride_axis=0).astype(BF16)
+        if block:
+            out_ref[(block - 1) * COARSE : block * COARSE, c * LANES : (c + 1) * LANES] = jnp.where(
+                lane < bound, now, later
+            )
+        now = later
+    out_ref[(BLOCKS - 1) * COARSE : BLOCKS * COARSE, c * LANES : (c + 1) * LANES] = now
 
 
 def build_taps(blocks_of, fine, height, out_ref, first, step):
@@ -214,50 +218,34 @@
                     lanes = slice((c * (TAPS + 1) + j) * LANES, (c * (TAPS + 1) + j + 1) * LANES)
                     out[b * rows : (b + 1) * rows, lanes] = jnp.where(lane < b, before, moved) if b else moved
                     before = moved
+        out[:, CHANNELS * (TAPS + 1) * LANES :] = jnp.zeros((height, LANES), BF16)
         return carry
 
     lax.fori_loop(0, per_step, body, 0)
 
 
-def correlate_kernel(call, data_ref, taps_ref, scale_ref, *refs):
-    if call:
-        owner_ref, first_high_ref, first_low_ref, stack_ref, high_ref, low_ref = refs[:6]
-        refs = refs[6:]
-    else:
-        high_ref, low_ref = refs[:2]
-        refs = refs[2:]
-    rows_ref, win_ref = refs[:2]
-    x_refs = (refs[2:4], refs[4:6])
-    groups = data_ref.shape[0]
+def correlate_kernel(call, rows_ref, win_ref, taps_ref, scale_ref, high_ref, low_ref, *refs):
+    x_refs = [[refs[4 * bank + 2 * n : 4 * bank + 2 * n + 2] for n in range(2)] for bank in range(2)]
+    groups = rows_ref.shape[0]
     rows = STATIONS * SLOTS
     height = FINE * rows
-    per_step = taps_ref.shape[0] // height
     step = pl.program_id(0)
-
-    def build(g, which):
-        for s in range(STATIONS):
-            build_data(rows_ref, g, s, x_refs[which][s])
+    parts = [(c, j) for c in range(CHANNELS) for j in range(TAPS + 1)]
+    parts = parts + parts[:1]
+
+    def builds(first, bank):
+        for n in range(2):
+            for s in range(STATIONS):
+                for c in range(CHANNELS):
+                    yield lambda n=n, s=s, c=c: build_data(rows_ref, first + n, s, c, x_refs[bank][n][s])
 
     @pl.when(step == 0)
     def _():
-        window_scales(data_ref, rows_ref, win_ref)
-        build(0, 0)
-
-    def lags(i, which):
-        g = step * per_step + i
-        taps = taps_ref[pl.ds(pl.multiple_of(i * height, height), height), :]
-        data = [
-            jnp.concatenate(
-                [
-                    ref[j * COARSE : j * COARSE + LANES, c * LANES : (c + 1) * LANES]
-                    for c in range(CHANNELS)
-                    for j in range(TAPS + 1)
-                ],
-                axis=1,
-            )
-            for ref in x_refs[which]
-        ]
-        raw = dot_nt(taps, jnp.concatenate(data, axis=0))
+        for write in builds(0, 0):
+            write()
+
+    def store_lags(i, raw):
+        g = step * 4 + i
         scale = scale_ref[pl.ds(pl.multiple_of((call * groups + g) * rows, rows), rows), :]
         at = pl.ds(pl.multiple_of(g * rows, rows), rows)
         for b in range(FINE):
@@ -271,28 +259,38 @@
             high_ref[at, b * LANES : (b + 1) * LANES] = high
             low_ref[at, b * LANES : (b + 1) * LANES] = low
 
-    def body(i, carry):
-        g = step * per_step + 2 * i
-        lags(2 * i, 0)
-        build(g + 1, 1)
-        lags(2 * i + 1, 1)
-        build(jnp.minimum(g + 2, groups - 1), 0)
-        return carry
-
-    lax.fori_loop(0, per_step // 2, body, 0)
-
-    if call:
-
-        @pl.when(step == pl.num_programs(0) - 1)
-        def _():
-            half = groups * rows
-            total = 0.0
-            for first, second in ((first_high_ref, high_ref), (first_low_ref, low_ref)):
-                total = total + dot(owner_ref[:, 0:half], first[...]) + dot(owner_ref[:, half:], second[...])
-            stack_lags(total, stack_ref)
-
-
-def stack_lags(total, stack_ref):
+    def multiply(accs, bank, writes):
+        for t in range(PASSES):
+            for n in range(2):
+                data = [
+                    jnp.concatenate(
+                        [ref[j * COARSE : j * COARSE + LANES, c * LANES : (c + 1) * LANES] for c, j in parts[2 * t : 2 * t + 2]],
+                        axis=1,
+                    )
+                    for ref in x_refs[bank][n]
+                ]
+                pltpu.matmul_push_rhs(jnp.concatenate(data, axis=0), t % 2, n, transpose=True)
+                first = (2 * bank + n) * height
+                taps = taps_ref[first : first + height, t * MXU : (t + 1) * MXU]
+                pltpu.matmul_acc_lhs(accs[n], taps, load_staged_rhs=t % 2)
+            for write in writes[t::PASSES]:
+                write()
+
+    def four_groups(*accs):
+        multiply(accs[:2], 0, list(builds(step * 4 + 2, 1)))
+        finish = [lambda n=n: store_lags(n, pltpu.matmul_pop(accs[n])) for n in range(2)]
+        multiply(accs[2:], 1, list(builds(jnp.minimum(step * 4 + 4, groups - 2), 0)) + finish)
+        for n in range(2):
+            store_lags(2 + n, pltpu.matmul_pop(accs[2 + n]))
+
+    pl.run_scoped(four_groups, *[pltpu.ACC(n % 2)((height, MXU), F32) for n in range(4)])
+
+
+def stack_kernel(owner_ref, near_high_ref, near_low_ref, far_high_ref, far_low_ref, stack_ref):
+    half = near_high_ref.shape[0]
+    total = 0.0
+    for near, far in ((near_high_ref, far_high_ref), (near_low_ref, far_low_ref)):
+        total = total + dot(owner_ref[:, 0:half], near[...]) + dot(owner_ref[:, half:], far[...])
     tpl_dev = stack_ref.shape[0]
     block_of = iota((tpl_dev, FINE * LANES), 1) % LANES // COARSE
     place = iota((FINE * LANES, LANES), 0)
@@ -360,16 +358,21 @@
     return pieces_of, lax.rsqrt(mean_square(centre) + EPS)
 
 
+def turn_over(block):
+    n = block.shape[0]
+    return dot(ones_where(iota((n, n), 0) + iota((n, n), 1) == n - 1), block).astype(BF16)
+
+
 def differential(mine, windows, x_ref, w_ref, parts_ref):
     count = len(windows)
     det_dev = mine[0][0].shape[0]
     height = count * DET_ROWS
     lane = iota((DET_ROWS, LANES), 1)
     wide = DET_FINE * DET_ROWS
-    diagonal = iota((height, wide), 0) % DET_ROWS == iota((height, wide), 1) % DET_ROWS
+    sub_lane = iota((8, LANES), 1) % DET_ROWS
     for q in range(det_dev // DET_ROWS):
         rows = slice(q * DET_ROWS, (q + 1) * DET_ROWS)
-        build_taps([[block[rows] for block in blocks] for blocks in mine], DET_FINE, DET_ROWS, w_ref, 0, DET_ROWS)
+        build_taps([[turn_over(block[rows]) for block in blocks] for blocks in mine], DET_FINE, DET_ROWS, w_ref, 0, DET_ROWS)
         for d in range(count):
             source = [[block[rows] for block in blocks] for blocks in windows[d]]
             for a in range(DET_COARSE):
@@ -386,31 +389,32 @@
                     tail = end if tail is None else jnp.where(lane < DET_FINE * c, tail, end)
                 x_ref[out, DET_DEPTH - LANES : DET_DEPTH] = tail
         raw = dot_nt(x_ref[0 : DET_COARSE * height, :], w_ref[...])
-        for a in range(DET_COARSE):
-            value = jnp.where(diagonal, raw[a * height : (a + 1) * height], 0.0)
-            for n, part in enumerate(pieces(value, 2)):
-                parts_ref[n, a, q * height : (q + 1) * height, :] = part
-    place = iota((wide, LANES), 0)
-    out = 0.0
-    total = det_dev * count
-    for a in range(DET_COARSE):
-        spread = ones_where(iota((wide, LANES), 1) == DET_FINE * a + place // DET_ROWS)
-        for n in range(2):
-            out = out + dot(parts_ref[n, a, 0:total, :], spread)
-    return out
+        for half in range(2):
+            for row in range(0, height, 8):
+                upper = row % DET_ROWS // 8
+                total = jnp.zeros((8, LANES), F32)
+                for a in range(DET_COARSE):
+                    part = raw[a * height + row : a * height + row + 8, half * LANES : (half + 1) * LANES]
+                    base = a + 1 if upper else a + LANES - DET_ROWS + 1
+                    part = pltpu.roll(part, base, 1, stride=1, stride_axis=0)
+                    total = jnp.where(sub_lane == 8 * upper + a, part, total)
+                parts_ref[q * height + row : q * height + row + 8, half * LANES : (half + 1) * LANES] = total
+    place, to = iota((wide, LANES), 0), iota((wide, LANES), 1)
+    order = ones_where((to // DET_FINE == place % DET_COARSE) & (to % DET_FINE == place // DET_ROWS))
+    return sum(dot(part, order) for part in pieces(parts_ref[...], 2))
 
 
 def detect_kernel(
     ngx, ngy, near_ref, far_ref, time_ref, station_ref, partner_ref, diff_ref, x_ref, w_ref, parts_ref
 ):
     gx, gy = lax.axis_index("gx"), lax.axis_index("gy")
-    mine, mine_scale = own_windows(near_ref[gx // 2 * ngy + gy], time_ref, station_ref)
+    mine, mine_scale = own_windows(near_ref[gx // 2 * ngy + gy, 0:PACKED], time_ref, station_ref)
     windows, scales = [], []
     for d, (dx, dy) in enumerate(((1, 0), (-1, 0), (0, 1), (0, -1))):
         x, y = gx + dx, gy + dy
         valid = (x >= 0) & (x < ngx) & (y >= 0) & (y < ngy)
         other = jnp.clip(x, 0, ngx - 1) // 2 * ngy + jnp.clip(y, 0, ngy - 1)
-        data = (far_ref if dx else near_ref)[other]
+        data = (far_ref if dx else near_ref)[other, 0:PACKED]
         found, scale = partner_windows(data, partner_ref[d : d + 1, :])
         windows.append(found)
         scales.append(jnp.where(valid, mine_scale * scale, 0.0))
@@ -434,7 +438,7 @@
     time_row, station_row = det_time.reshape(1, det_dev), det_station.reshape(1, det_dev)
     packed = pl.pallas_call(
         pack_kernel,
-        out_shape=jax.ShapeDtypeStruct((half, PACKED, LANES), BF16),
+        out_shape=jax.ShapeDtypeStruct((half, SENT, LANES), BF16),
         scratch_shapes=[pltpu.VMEM((PACKED, LANES), F32)],
         name="pack",
     )(waveforms.transpose(1, 0, 2), time_row, station_row)
@@ -454,7 +458,7 @@
     )(templates, tpl_stations.T)
     steps = groups // 4
     height = 4 * FINE * rows
-    depth = CHANNELS * (TAPS + 1) * LANES
+    depth = MXU * PASSES
     taps = pl.pallas_call(
         taps_kernel,
         grid=(steps,),
@@ -471,46 +475,48 @@
         return pl.BlockSpec(shape, lambda i: (0,) * len(shape))
 
     sums = (half * rows, FINE * LANES)
-    scratch = [
-        pltpu.VMEM((half, PACKED, LANES), F32),
-        pltpu.VMEM((half, STATIONS, FINE, LANES), F32),
-    ] + [pltpu.VMEM((BLOCKS * COARSE, CHANNELS * LANES), BF16)] * 4
     params = pltpu.CompilerParams(vmem_limit_bytes=(16 << 20) + groups * (1 << 17))
 
-    def specs(call):
-        return [
-            whole(half, PACKED, LANES),
-            pl.BlockSpec((height, depth), lambda i: (call * steps // 2 + i, 0)),
-            whole(*scale.shape),
-        ]
-
-    high, low = pl.pallas_call(
-        functools.partial(correlate_kernel, 0),
-        grid=(steps // 2,),
-        in_specs=specs(0),
-        out_specs=(whole(*sums), whole(*sums)),
-        out_shape=(jax.ShapeDtypeStruct(sums, BF16),) * 2,
-        scratch_shapes=scratch,
+    def correlate(call, data):
+        series, win = pl.pallas_call(
+            windows_kernel,
+            out_shape=(
+                jax.ShapeDtypeStruct((half, PACKED, LANES), F32),
+                jax.ShapeDtypeStruct((half, STATIONS, FINE, LANES), F32),
+            ),
+            compiler_params=params,
+            name="windows",
+        )(data)
+        return pl.pallas_call(
+            functools.partial(correlate_kernel, call),
+            grid=(steps // 2,),
+            in_specs=[
+                whole(*series.shape),
+                whole(*win.shape),
+                pl.BlockSpec((height, depth), lambda i: (call * steps // 2 + i, 0)),
+                whole(*scale.shape),
+            ],
+            out_specs=(whole(*sums), whole(*sums)),
+            out_shape=(jax.ShapeDtypeStruct(sums, BF16),) * 2,
+            scratch_shapes=[pltpu.VMEM((BLOCKS * COARSE, CHANNELS * LANES), BF16)] * 8,
+            compiler_params=params,
+            name="correlate",
+        )(series, win, taps, scale)
+
+    near_sums, far_sums = correlate(0, near), correlate(1, far)
+    stack = pl.pallas_call(
+        stack_kernel,
+        out_shape=jax.ShapeDtypeStruct((tpl_dev, LAG_BLOCKS * LANES), F32),
         compiler_params=params,
-        name="correlate_near",
-    )(near, taps, scale)
-    stack = pl.pallas_call(
-        functools.partial(correlate_kernel, 1),
-        grid=(steps // 2,),
-        in_specs=specs(1) + [whole(*owner.shape), whole(*sums), whole(*sums)],
-        out_specs=whole(tpl_dev, LAG_BLOCKS * LANES),
-        out_shape=jax.ShapeDtypeStruct((tpl_dev, LAG_BLOCKS * LANES), F32),
-        scratch_shapes=[pltpu.VMEM(sums, BF16)] * 2 + scratch,
-        compiler_params=params,
-        name="correlate_far",
-    )(far, taps, scale, owner, high, low)
+        name="stack",
+    )(owner, *near_sums, *far_sums)
     diff = pl.pallas_call(
         functools.partial(detect_kernel, ngx, ngy),
         out_shape=jax.ShapeDtypeStruct((4 * det_dev, DTLAG), F32),
         scratch_shapes=[
             pltpu.VMEM((4 * DET_COARSE * DET_ROWS, DET_DEPTH), BF16),
             pltpu.VMEM((DET_FINE * DET_ROWS, DET_DEPTH), BF16),
-            pltpu.VMEM((2, DET_COARSE, 4 * det_dev, DET_FINE * DET_ROWS), BF16),
+            pltpu.VMEM((4 * det_dev, DET_FINE * DET_ROWS), F32),
         ],
         compiler_params=pltpu.CompilerParams(vmem_limit_bytes=(16 << 20) + groups * (1 << 15)),
         name="detect",

time: 63 us -> 67.4 us (1.070)
  blocking collectives: 18.4 us -> 22.8 us
    all_to_all x1, blocking collectives: 18.4 us -> 22.8 us  [on_device(): lax.all_to_all(packed, ('gx', 'gy'), split_axis=0, concat_axis=0, axis_in...]
    pallas_call x3 -> x6, Pallas kernels: 21.6 us -> 21 us  [the longest x2 15.6 us: correlate(): pl.pallas_call(functools.partial(correlate_kernel, call), grid=(steps //...]
  transfers between devices with their start and end apart: 1 -> 1, of which waited for: 0 -> 0; matrix products, arithmetic and copies ran while one was open for 0% -> 0% of each run, Pallas kernels for 30% -> 28%
where the time goes in v3:
time: 67.4 us; the launch traced here: 66.9 us
  Pallas kernels  39.9 us (59%)
  blocking collectives  22.8 us (34%)
  local copies, waits for them, and re-layouts  1.84 us (3%)
  starting transfers between devices  1.74 us (3%)
  between operations  0.69 us (1%)
    all_to_all x1, blocking collectives, on_device(): lax.all_to_all(packed, ('gx', 'gy'), split_axis=0, concat_axis=0, axis_in...  22.8 us
    pallas_call x2, Pallas kernels, correlate(): pl.pallas_call(functools.partial(correlate_kernel, call), grid=(steps //...  15.6 us
    pallas_call x1, Pallas kernels, on_device(): pl.pallas_call(functools.partial(detect_kernel, ngx, ngy), out_shape=jax....  9.23 us
    pallas_call x1, Pallas kernels, on_device(): pl.pallas_call(taps_kernel, grid=(steps,), in_specs=[pl.BlockSpec((total,...  8.67 us
    pallas_call x2, Pallas kernels, correlate(): pl.pallas_call(windows_kernel, out_shape=(jax.ShapeDtypeStruct((half, PAC...  2.21 us
    unnamed x10, local copies, waits for them, and re-layouts  1.84 us
    ppermute x1, starting transfers between devices, on_device(): far = lax.ppermute(near, 'gx', [(x, x ^ 1) for x in range(ngx)])  1.74 us
    pallas_call x1, Pallas kernels, on_device(): pl.pallas_call(pack_kernel, out_shape=jax.ShapeDtypeStruct((half, SENT, L...  1.62 us
  transfers between devices with their start and end apart: 1, of which 0 were waited for; matrix products, arithmetic and copies ran while one was open for 0% of the time, Pallas kernels for 28%

profile of v3, /device:TPU:1, one launch (start us, length us, event | category | flops | bytes accessed | tf_op | source)
XLA Modules:
  0.0 66.9 jit_solution(13985859334525474107)
XLA Ops:
  0.6 1.6 %pack.1 = bf16[16,128,128]{2,1,0:T(8,128)(2,1)} custom-call(bf16[3,2,1536]{2,1,0:T(2,128)(2,1)} %bitcast.13, s32[1,64]{1,0:T(1,128)} %bitcast.8, s32[1,64]{1,0:T(1,128)} %bitcast.10), custom_call_target="tpu_custom_call" | custom-call | tf_op jit(solution)/shard_map/pack/pallas_call | solution.py:439
  2.2 22.8 %all_to_all.5.data_ref.near_ref = bf16[16,128,128]{2,1,0:T(8,128)(2,1)S(1)} all-to-all(bf16[16,128,128]{2,1,0:T(8,128)(2,1)} %pack.1), channel_id=1, replica_groups={{0,1,2,3,8,9,10,11,16,17,18,19,24,25,26,27},{4,5,6,7,12,13,14,15,20,21,..., dimensions={0} | all-to-all | bytes 1048576 | tf_op jit(solution)/shard_map/all_to_all | solution.py:446
  25.1 1.7 %collective-permute-start = (bf16[16,128,128]{2,1,0:T(8,128)(2,1)S(1)}, bf16[16,128,128]{2,1,0:T(8,128)(2,1)S(1)}, u32[]{:S(2)}, u32[]{:S(2)}) collective-permute-start(bf16[16,128,128]{2,1,0:T(8,128)(2,1)S(1)} %all_to_all.5.data_ref.near_ref), channel_id=1, source_target_pairs={{0,4},{4,0},{8,12},{12,8},{16,20},{20,16},{24,28},{28,24},{1,5},{5... | collective-permute-start | bytes 1572872 | tf_op jit(solution)/shard_map/ppermute | solution.py:472
  26.8 0.0 copy-start
  26.8 1.1 %copy-done = bf16[32,8,1536]{2,1,0:T(8,128)(2,1)S(1)} copy-done((bf16[32,8,1536]{2,1,0:T(8,128)(2,1)S(1)}, bf16[32,8,1536]{2,1,0:T(8,128)(2,1)}, u32[]{:S(2)}) %copy-start) | copy-done | bytes 786456
  27.9 0.0 copy-start.1
  27.9 0.7 %copy-done.1 = s32[32,8]{0,1:T(8,128)S(1)} copy-done((s32[32,8]{0,1:T(8,128)S(1)}, s32[32,8]{0,1:T(8,128)}, u32[]{:S(2)}) %copy-start.1) | copy-done | bytes 1048
  28.6 1.0 %tiles.1 = (bf16[512,1536]{1,0:T(8,128)(2,1)S(1)}, f32[512,128]{1,0:T(8,128)S(1)}, bf16[32,512]{1,0:T(8,128)(2,1)S(1)}) custom-call(bf16[32,8,1536]{2,1,0:T(8,128)(2,1)S(1)} %copy-done, s32[8,32]{1,0:T(8,128)S(1)} %bitcast.6), custom_call_target="tpu_custom_call" | custom-call | tf_op jit(solution)/shard_map/tiles/pallas_call | solution.py:449
  29.6 8.7 %taps.1.taps_ref = bf16[4096,2048]{1,0:T(8,128)(2,1)} custom-call(bf16[512,1536]{1,0:T(8,128)(2,1)S(1)} %get-tuple-element.16.sorted_ref), custom_call_target="tpu_custom_call" | custom-call | tf_op jit(solution)/shard_map/taps/pallas_call | solution.py:462
  38.3 1.1 %windows.2 = (f32[16,80,128]{2,1,0:T(8,128)S(1)}, f32[16,2,8,128]{3,2,1,0:T(8,128)S(1)}) custom-call(bf16[16,128,128]{2,1,0:T(8,128)(2,1)S(1)} %all_to_all.5.data_ref.near_ref), custom_call_target="tpu_custom_call" | custom-call | tf_op jit(solution)/shard_map/windows/pallas_call | solution.py:481
  39.4 0.0 copy-start.2
  39.4 0.0 copy-start.3
  39.4 0.0 copy-start.4
  39.4 7.8 %correlate.2 = (bf16[256,1024]{1,0:T(8,128)(2,1)S(1)}, bf16[256,1024]{1,0:T(8,128)(2,1)S(1)}) custom-call(f32[16,80,128]{2,1,0:T(8,128)S(1)} %get-tuple-element.14.rows_ref, f32[16,2,8,128]{3,2,1,0:T(8,128)S(1)} %get-tuple-element.15.win_ref, bf16[4096,2048]{1,0:T(8,128)(2,1)} %taps.1.taps_ref, f32[512,128]{1,0:T(8,128)S(1)} %get-tuple-element.17.scale_ref), custom_call_target="tpu_custom_call" | custom-call | tf_op jit(solution)/shard_map/correlate/pallas_call | solution.py:490
  47.2 0.0 collective-permute-done.data_ref.far_ref
  47.3 1.1 %windows.3 = (f32[16,80,128]{2,1,0:T(8,128)S(1)}, f32[16,2,8,128]{3,2,1,0:T(8,128)S(1)}) custom-call(bf16[16,128,128]{2,1,0:T(8,128)(2,1)S(1)} %collective-permute-done.data_ref.far_ref), custom_call_target="tpu_custom_call" | custom-call | tf_op jit(solution)/shard_map/windows/pallas_call | solution.py:481
  48.4 7.8 %correlate.3 = (bf16[256,1024]{1,0:T(8,128)(2,1)S(1)}, bf16[256,1024]{1,0:T(8,128)(2,1)S(1)}) custom-call(f32[16,80,128]{2,1,0:T(8,128)S(1)} %get-tuple-element.20.rows_ref, f32[16,2,8,128]{3,2,1,0:T(8,128)S(1)} %get-tuple-element.21.win_ref, bf16[4096,2048]{1,0:T(8,128)(2,1)} %taps.1.taps_ref, f32[512,128]{1,0:T(8,128)S(1)} %get-tuple-element.17.scale_ref), custom_call_target="tpu_custom_call" | custom-call | tf_op jit(solution)/shard_map/correlate/pallas_call | solution.py:490
  56.2 1.5 %stack.1 = f32[32,1024]{1,0:T(8,128)} custom-call(bf16[32,512]{1,0:T(8,128)(2,1)S(1)} %get-tuple-element.13.owner_ref, bf16[256,1024]{1,0:T(8,128)(2,1)S(1)} %get-tuple-element.18.near_high_ref, bf16[256,1024]{1,0:T(8,128)(2,1)S(1)} %get-tuple-element.19.near_low_ref, bf16[256,1024]{1,0:T(8,128)(2,1)S(1)} %get-tuple-element.22.far_high_ref, ...), custom_call_target="tpu_custom_call" | custom-call | tf_op jit(solution)/shard_map/stack/pallas_call | solution.py:507
  57.7 0.0 copy-done.2
  57.7 0.0 copy-done.3
  57.7 0.0 copy-done.4
  57.7 9.2 %detect.1 = f32[256,128]{1,0:T(8,128)} custom-call(bf16[16,128,128]{2,1,0:T(8,128)(2,1)S(1)} %all_to_all.5.data_ref.near_ref, bf16[16,128,128]{2,1,0:T(8,128)(2,1)S(1)} %collective-permute-done.data_ref.far_ref, s32[1,64]{1,0:T(1,128)S(1)} %bitcast.9, s32[1,64]{1,0:T(1,128)S(1)} %bitcast.11, s32[4,64]{1,0:T(4,128)S(1)} %bitcast.7), custom_call_target="tpu_custom_call" | custom-call | tf_op jit(solution)/shard_map/detect/pallas_call | solution.py:513
Async XLA Ops:
  25.1 22.2 %collective-permute-start = (bf16[16,128,128]{2,1,0:T(8,128)(2,1)S(1)}, bf16[16,128,128]{2,1,0:T(8,128)(2,1)S(1)}, u32[]{:S(2)}, u32[]{:S(2)}) collective-permute-start(bf16[16,128,128]{2,1,0:T(8,128)(2,1)S(1)} %all_to_all.5.data_ref.near_ref), channel_id=1, source_target_pairs={{0,4},{4,0},{8,12},{12,8},{16,20},{20,16},{24,28},{28,24},{1,5},{5... | collective-permute-start | bytes 1572872 | tf_op jit(solution)/shard_map/ppermute | solution.py:472
  26.8 1.1 %copy-start = (bf16[32,8,1536]{2,1,0:T(8,128)(2,1)S(1)}, bf16[32,8,1536]{2,1,0:T(8,128)(2,1)}, u32[]{:S(2)}) copy-start(bf16[32,8,1536]{2,1,0:T(8,128)(2,1)} %tiles_ref.1) | copy-start | bytes 2359300
  27.9 0.7 %copy-start.1 = (s32[32,8]{0,1:T(8,128)S(1)}, s32[32,8]{0,1:T(8,128)}, u32[]{:S(2)}) copy-start(s32[32,8]{0,1:T(8,128)} %param.8) | copy-start | bytes 3076
  39.4 18.3 %copy-start.2 = (s32[64,4]{0,1:T(4,128)S(1)}, s32[64,4]{0,1:T(4,128)}, u32[]{:S(2)}) copy-start(s32[64,4]{0,1:T(4,128)} %param.11) | copy-start | bytes 3076
  39.4 18.3 %copy-start.3 = (s32[64]{0:T(128)S(1)}, s32[64]{0:T(128)}, u32[]{:S(2)}) copy-start(s32[64]{0:T(128)} %param.10) | copy-start | bytes 772
  39.4 18.3 %copy-start.4 = (s32[64]{0:T(128)S(1)}, s32[64]{0:T(128)}, u32[]{:S(2)}) copy-start(s32[64]{0:T(128)} %param.9) | copy-start | bytes 772

commit v4 on v3

v4 whole, which is shorter than its diff:
```python
import functools

import jax
import jax.numpy as jnp
from jax import lax
from jax.experimental import pallas as pl
from jax.experimental.pallas import tpu as pltpu
from jax.sharding import PartitionSpec as P

LANES = 128
CHANNELS = 3
STATIONS = 2
BLOCKS = 12
TAPS = 4
LAG_BLOCKS = BLOCKS - TAPS
SLOTS = 8
FINE = 8
COARSE = LANES // FINE
DET_FINE = 16
DET_COARSE = LANES // DET_FINE
DET_ROWS = 16
W = 256
DTLAG = 128
HALF = DTLAG // 2
KEEP = W // LANES
DET_DEPTH = CHANNELS * KEEP * LANES + LANES
SPAN = STATIONS * BLOCKS
ROWS = CHANNELS * SPAN
PACKED = ROWS + 8
MXU = 256
RUNS = BLOCKS - 1
DEPTH = CHANNELS * LANES + LANES
EPS = 1e-06
F32 = jnp.float32
BF16 = jnp.bfloat16
NT = (((1,), (1,)), ((), ()))


def iota(shape, axis):
    return lax.broadcasted_iota(jnp.int32, shape, axis)


def rot(value, shift, axis=1):
    shift = shift % value.shape[axis]
    return pltpu.roll(value, shift, axis) if shift else value


def dot(a, b):
    return jnp.dot(a, b, preferred_element_type=F32)


def dot_nt(a, b):
    return lax.dot_general(a, b, NT, preferred_element_type=F32)


def ones_where(mask):
    return jnp.where(mask, 1.0, 0.0).astype(BF16)


def pieces(value, count):
    out = []
    for _ in range(count - 1):
        high = value.astype(BF16)
        out.append(high)
        value = value - high.astype(F32)
    out.append(value.astype(BF16))
    return out


def column(row):
    n = row.shape[1]
    diagonal = iota((n, n), 0) == iota((n, n), 1)
    return jnp.sum(jnp.where(diagonal, row, 0), axis=1, keepdims=True)


def pack_kernel(wave_ref, time_ref, station_ref, out_ref, rows_ref):
    start = time_ref[...] - HALF
    row = BLOCKS * station_ref[...] + start // LANES
    shift = start % LANES
    pad = jnp.zeros((1, LANES - row.shape[1]), F32)
    for c in range(CHANNELS):
        series = wave_ref[c].astype(F32)
        for s in range(STATIONS):
            for block in range(BLOCKS):
                at = c * SPAN + s * BLOCKS + block
                rows_ref[at : at + 1, :] = series[s : s + 1, block * LANES : (block + 1) * LANES]
    rows_ref[ROWS : ROWS + 1, :] = jnp.concatenate([row.astype(F32), pad], axis=1)
    rows_ref[ROWS + 1 : ROWS + 2, :] = jnp.concatenate([shift.astype(F32), pad], axis=1)
    rows_ref[ROWS + 2 : PACKED, :] = jnp.zeros((PACKED - ROWS - 2, LANES), F32)
    out_ref[...] = jnp.broadcast_to(rows_ref[...].astype(BF16)[None], out_ref.shape)


def tile_kernel(tiles_ref, station_ref, sorted_ref, scale_ref, owner_ref):
    tpl_dev, k_slots, row_len = tiles_ref.shape
    count = tpl_dev * k_slots
    total = scale_ref.shape[0]
    station = station_ref[...].astype(F32).astype(BF16)
    home = ones_where(iota((count, tpl_dev), 0) // k_slots == iota((count, tpl_dev), 1))
    home_t = ones_where(iota((tpl_dev, count), 1) // k_slots == iota((tpl_dev, count), 0))
    by_row = dot_nt(home, station)
    by_col = dot(station, home_t)
    own_col = iota((count, k_slots), 0) % k_slots == iota((count, k_slots), 1)
    own_row = iota((k_slots, count), 1) % k_slots == iota((k_slots, count), 0)
    st_col = jnp.sum(jnp.where(own_col, by_row, 0.0), axis=1, keepdims=True)
    st_row = jnp.sum(jnp.where(own_row, by_col, 0.0), axis=0, keepdims=True)
    earlier = iota((count, count), 0) < iota((count, count), 1)
    rank = jnp.sum(jnp.where((st_col == st_row) & earlier, 1.0, 0.0), axis=0, keepdims=True)
    slot = (st_row * SLOTS + rank).astype(jnp.int32)
    tiles = tiles_ref[...].reshape(count, row_len)
    step = 128
    for first in range(0, total, step):
        place = ones_where(iota((step, count), 0) + first == slot)
        moved = dot(place, tiles)
        mean = jnp.sum(moved * moved, axis=1, keepdims=True) / row_len
        scale = lax.rsqrt(row_len * (mean + EPS))
        scale_ref[first : first + step, :] = jnp.broadcast_to(scale, (step, LANES))
        owner_ref[:, first : first + step] = dot_nt(home_t, place).astype(BF16)
        moved = moved.reshape(step // SLOTS, SLOTS, row_len)
        for c in range(CHANNELS):
            parts = [moved[:, :, (TAPS * c + h) * LANES : (TAPS * c + h + 1) * LANES] for h in range(TAPS)]
            block = jnp.stack(parts, axis=1).reshape(step * TAPS, LANES)
            sorted_ref[first * TAPS : (first + step) * TAPS, c * LANES : (c + 1) * LANES] = block.astype(BF16)


def windows_kernel(data_ref, rows_ref, win_ref):
    groups = data_ref.shape[0]
    step = min(8, groups)
    column_of = iota((LANES, LANES), 1)
    sample = FINE * (COARSE - 1 - column_of % COARSE) + column_of // COARSE
    row = iota((LANES, LANES), 0)
    sums_of = ones_where(jnp.concatenate([row >= sample, row < sample, row >= 0], axis=1))
    major, chunk = iota((step, FINE, LANES), 1), iota((step, FINE, LANES), 2) // COARSE

    def body(q, carry):
        x = data_ref[pl.ds(q * step, step)].astype(F32)
        rows_ref[pl.ds(q * step, step)] = x
        energy = sum(x[:, SPAN * c : SPAN * (c + 1)] * x[:, SPAN * c : SPAN * (c + 1)] for c in range(CHANNELS))
        sums = sum(dot(part, sums_of) for part in pieces(energy.reshape(step * SPAN, LANES), 3))
        sums = sums.reshape(step, SPAN, 3 * LANES)
        for s in range(STATIONS):
            at = BLOCKS * s
            mean = sums[:, at : at + LAG_BLOCKS, 0:LANES]
            for j in range(1, TAPS):
                mean = mean + sums[:, at + j : at + j + LAG_BLOCKS, 2 * LANES :]
            mean = (mean + sums[:, at + TAPS : at + TAPS + LAG_BLOCKS, LANES : 2 * LANES]) / (
                CHANNELS * TAPS * LANES
            )
            value = lax.rsqrt(mean + EPS)
            for bit in range(3):
                size = 1 << bit
                up = (major // size) % 2
                other = (chunk // size) % 2
                later = rot(rot(value, -size, 1), size * COARSE, 2)
                earlier = rot(rot(value, size, 1), -size * COARSE, 2)
                value = jnp.where(up == other, value, jnp.where(up == 0, later, earlier))
            win_ref[pl.ds(q * step, step), s] = value
        return carry

    lax.fori_loop(0, groups // step, body, 0)


def build_data(rows_ref, group, s, out_ref):
    lane = iota((COARSE, LANES), 1)
    bound = FINE * (iota((COARSE, LANES), 0) + 1)

    def turned(c, block):
        at = SPAN * c + BLOCKS * s + block
        row = jnp.broadcast_to(rows_ref[group, at : at + 1, :], (COARSE, LANES))
        return pltpu.roll(row, FINE, 1, stride=FINE, stride_axis=0).astype(BF16)

    now = [turned(c, 0) for c in range(CHANNELS)]
    for run in range(RUNS):
        later = [turned(c, run + 1) for c in range(CHANNELS)]
        rows = slice(run * COARSE, (run + 1) * COARSE)
        for c in range(CHANNELS):
            out_ref[rows, c * LANES : (c + 1) * LANES] = jnp.where(lane < bound, now[c], later[c])
        tail = later[0]
        for c in range(1, CHANNELS):
            tail = jnp.where(lane < FINE * c, tail, rot(later[c], FINE * c))
        out_ref[rows, CHANNELS * LANES :] = tail
        now = later


def build_taps(blocks_of, fine, height, out_ref, first, step):
    lane = iota((height, LANES), 1)
    zero = jnp.zeros((height, LANES), BF16)
    for b in range(fine):
        rows = slice(first + step * b, first + step * b + height)
        tail = zero
        at = 0
        for c, blocks in enumerate(blocks_of):
            before = zero
            for block in blocks:
                moved = rot(block, b)
                out_ref[rows, at : at + LANES] = jnp.where(lane < b, before, moved) if b else moved
                before = moved
                at += LANES
            if b:
                end = rot(blocks[-1], b + fine * c)
                tail = jnp.where((lane >= fine * c) & (lane < fine * c + b), end, tail)
        out_ref[rows, at : at + LANES] = tail


def taps_kernel(sorted_ref, out_ref):
    height = FINE * TAPS * SLOTS
    stations = out_ref.shape[0] // height

    def body(i, carry):
        station = pl.program_id(0) * stations + i
        out = out_ref.at[pl.ds(pl.multiple_of(i * height, height), height), :]
        for pair in range(TAPS // 2):
            at = station * TAPS * SLOTS + pair * 2 * SLOTS
            tiles = sorted_ref[pl.ds(pl.multiple_of(at, 2 * SLOTS), 2 * SLOTS), :]
            blocks = [[tiles[:, c * LANES : (c + 1) * LANES]] for c in range(CHANNELS)]
            build_taps(blocks, FINE, 2 * SLOTS, out, pair * 2 * SLOTS, TAPS * SLOTS)
        return carry

    lax.fori_loop(0, stations, body, 0)


def correlate_kernel(rows_ref, win_ref, taps_ref, scale_ref, high_ref, low_ref, *x_refs):
    stations = rows_ref.shape[0] * STATIONS
    height = FINE * TAPS * SLOTS
    per_step = taps_ref.shape[0] // height
    base = pl.program_id(0) * per_step
    lane = iota((SLOTS, LANES), 1)

    def build(k):
        group = jnp.minimum((base + k) // STATIONS, stations // STATIONS - 1)
        build_data(rows_ref, group, k % STATIONS, x_refs[k % len(x_refs)])

    @pl.when(pl.program_id(0) == 0)
    def _():
        for ref in x_refs:
            ref[RUNS * COARSE :, :] = jnp.zeros((MXU - RUNS * COARSE, DEPTH), BF16)
        for k in range(2):
            build(k)

    def multiply(k, acc):
        data_ref = x_refs[k % len(x_refs)]
        for t in range(DEPTH // MXU):
            lanes = slice(t * MXU, (t + 1) * MXU)
            pltpu.matmul_push_rhs(data_ref[:, lanes], t % 2, k % 2, transpose=True)
            pltpu.matmul_acc_lhs(acc, taps_ref[k * height : (k + 1) * height, lanes], load_staged_rhs=t % 2)

    def lags(k, acc):
        raw = pltpu.matmul_pop(acc)
        st = base + k
        scale = scale_ref[pl.ds(pl.multiple_of(st * SLOTS, SLOTS), SLOTS), :]
        out = []
        for b in range(FINE):
            total = None
            for h in reversed(range(TAPS)):
                row = (b * TAPS + h) * SLOTS
                part = raw[row : row + SLOTS, 0:LANES]
                if h:
                    part = jnp.where(lane < h * COARSE, raw[row : row + SLOTS, LANES:], part)
                total = part if total is None else part + rot(total, -COARSE)
            out.append(total * scale * win_ref[st // STATIONS, k % STATIONS, b : b + 1, :])
        return out

    def run(*accs):
        done = []
        for k in range(per_step + 1):
            if k < per_step:
                multiply(k, accs[k % len(accs)])
                build(k + 2)
            if k:
                done.append(lags(k - 1, accs[(k - 1) % len(accs)]))
            if len(done) == STATIONS:
                at = pl.multiple_of((base + k - STATIONS) * SLOTS, STATIONS * SLOTS)
                for b in range(FINE):
                    high, low = pieces(jnp.concatenate([value[b] for value in done], axis=0), 2)
                    rows = pl.ds(at, STATIONS * SLOTS)
                    high_ref[rows, b * LANES : (b + 1) * LANES] = high
                    low_ref[rows, b * LANES : (b + 1) * LANES] = low
                done = []

    pl.run_scoped(run, *[pltpu.ACC(n % 2)((height, MXU), F32) for n in range(4)])


def stack_kernel(owner_ref, high_ref, low_ref, stack_ref):
    total = dot(owner_ref[...], high_ref[...]) + dot(owner_ref[...], low_ref[...])
    tpl_dev = stack_ref.shape[0]
    block_of = iota((tpl_dev, FINE * LANES), 1) % LANES // COARSE
    place = iota((FINE * LANES, LANES), 0)
    spread = iota((FINE * LANES, LANES), 1) == FINE * (COARSE - 1 - place % COARSE) + place // LANES
    spread = ones_where(spread)
    out = 0.0
    for part in pieces(total, 2):
        part = part.astype(F32)
        masked = [jnp.where(block_of == block, part, 0.0) for block in range(LAG_BLOCKS)]
        out = out + dot(jnp.concatenate(masked, axis=0).astype(BF16), spread)
    for block in range(LAG_BLOCKS):
        rows = out[block * tpl_dev : (block + 1) * tpl_dev]
        stack_ref[:, block * LANES : (block + 1) * LANES] = rows * (1.0 / 8.0**0.5)


def cut(data, row, shift, blocks):
    det_dev = row.shape[0]
    row_iota, lane = iota((det_dev, PACKED), 1), iota((det_dev, LANES), 1)
    picks = [row_iota == row + (SPAN * c + j) for c in range(CHANNELS) for j in range(blocks)]
    picks = jnp.concatenate([jnp.where(pick, 1.0, 0.0) for pick in picks], axis=0).astype(BF16)
    found = dot(picks, data).astype(BF16)
    found = [
        [found[(c * blocks + j) * det_dev : (c * blocks + j + 1) * det_dev] for j in range(blocks)]
        for c in range(CHANNELS)
    ]
    shift = jnp.broadcast_to(shift, (det_dev, LANES))
    for bit in range(7):
        size = 1 << bit
        moves = (shift & size) > 0
        found = [[jnp.where(moves, rot(block, -size), block) for block in row] for row in found]
    inside = lane < LANES - shift
    return [[jnp.where(inside, row[j], row[j + 1]) for j in range(blocks - 1)] for row in found]


def mean_square(blocks):
    total = 0.0
    for block, mask in blocks:
        block = block.astype(F32)
        square = block * block
        total = total + (square if mask is None else jnp.where(mask, square, 0.0))
    return jnp.sum(total, axis=1, keepdims=True) / (CHANNELS * W)


def own_windows(data, time_ref, station_ref):
    n = time_ref.shape[1]
    turned = iota((n, n), 0) ^ (DET_ROWS - 1) == iota((n, n), 1)
    start = jnp.sum(jnp.where(turned, time_ref[...], 0), axis=1, keepdims=True)
    station = jnp.sum(jnp.where(turned, station_ref[...], 0), axis=1, keepdims=True)
    mine = cut(data, station * BLOCKS + start // LANES, start % LANES, KEEP + 1)
    scale = lax.rsqrt(CHANNELS * W * (mean_square([(block, None) for blocks in mine for block in blocks]) + EPS))
    scale = jnp.sum(jnp.where(turned, scale, 0.0), axis=0, keepdims=True)
    return mine, column(scale)


def partner_windows(data, chosen_row):
    det_dev = chosen_row.shape[1]
    lane = iota((det_dev, LANES), 1)
    info = dot_nt(ones_where(lane == column(chosen_row)), data[PACKED - 16 : PACKED, :])
    pieces_of = cut(data, info[:, 8:9].astype(jnp.int32), info[:, 9:10].astype(jnp.int32), KEEP + 2)
    centre = []
    for first, middle, last in pieces_of:
        centre += [(first, lane >= HALF), (middle, None), (last, lane < HALF)]
    return pieces_of, lax.rsqrt(mean_square(centre) + EPS)


def differential(mine, windows, x_ref, w_ref, parts_ref):
    count = len(windows)
    det_dev = mine[0][0].shape[0]
    height = count * DET_ROWS
    lane = iota((DET_ROWS, LANES), 1)
    wide = DET_FINE * DET_ROWS
    sub_lane = iota((8, LANES), 1) % DET_ROWS
    for q in range(det_dev // DET_ROWS):
        rows = slice(q * DET_ROWS, (q + 1) * DET_ROWS)
        build_taps([[block[rows] for block in blocks] for blocks in mine], DET_FINE, DET_ROWS, w_ref, 0, DET_ROWS)
        for d in range(count):
            source = [[block[rows] for block in blocks] for blocks in windows[d]]
            ends = {}
            for a in range(DET_COARSE):
                shift = DET_FINE * a
                out = slice((a * count + d) * DET_ROWS, (a * count + d + 1) * DET_ROWS)
                tail = None
                for c in range(CHANNELS):
                    moved = [rot(block, -shift) for block in source[c]]
                    ends[c, a] = moved[KEEP]
                    for j in range(KEEP):
                        block = jnp.where(lane < LANES - shift, moved[j], moved[j + 1]) if a else moved[j]
                        at = (c * KEEP + j) * LANES
                        x_ref[out, at : at + LANES] = block
                    end = ends[c, a - c] if a >= c else rot(source[c][KEEP], DET_FINE * c - shift)
                    tail = end if tail is None else jnp.where(lane < DET_FINE * c, tail, end)
                x_ref[out, DET_DEPTH - LANES : DET_DEPTH] = tail
        raw = dot_nt(x_ref[0 : DET_COARSE * height, :], w_ref[...])
        for half in range(2):
            for row in range(0, height, 8):
                upper = row % DET_ROWS // 8
                total = jnp.zeros((8, LANES), F32)
                for a in range(DET_COARSE):
                    part = raw[a * height + row : a * height + row + 8, half * LANES : (half + 1) * LANES]
                    base = a + 1 if upper else a + LANES - DET_ROWS + 1
                    part = pltpu.roll(part, base, 1, stride=1, stride_axis=0)
                    total = jnp.where(sub_lane == 8 * upper + a, part, total)
                parts_ref[q * height + row : q * height + row + 8, half * LANES : (half + 1) * LANES] = total
    place, to = iota((wide, LANES), 0), iota((wide, LANES), 1)
    order = ones_where((to // DET_FINE == place % DET_COARSE) & (to % DET_FINE == place // DET_ROWS))
    return sum(dot(part, order) for part in pieces(parts_ref[...], 2))


def detect_kernel(
    ngx, ngy, data_ref, time_ref, station_ref, partner_ref, diff_ref, x_ref, w_ref, parts_ref
):
    gx, gy = lax.axis_index("gx"), lax.axis_index("gy")
    mine, mine_scale = own_windows(data_ref[gx * ngy + gy], time_ref, station_ref)
    windows, scales = [], []
    for d, (dx, dy) in enumerate(((1, 0), (-1, 0), (0, 1), (0, -1))):
        x, y = gx + dx, gy + dy
        valid = (x >= 0) & (x < ngx) & (y >= 0) & (y < ngy)
        data = data_ref[jnp.clip(x, 0, ngx - 1) * ngy + jnp.clip(y, 0, ngy - 1)]
        found, scale = partner_windows(data, partner_ref[d : d + 1, :])
        windows.append(found)
        scales.append(jnp.where(valid, mine_scale * scale, 0.0))
    out = differential(mine, windows, x_ref, w_ref, parts_ref)
    for q in range(time_ref.shape[1] // DET_ROWS):
        for d in range(4):
            at = (q * 4 + d) * DET_ROWS
            rows = slice(q * DET_ROWS, (q + 1) * DET_ROWS)
            diff_ref[pl.ds(q * DET_ROWS * 4 + d, DET_ROWS, stride=4), :] = (
                out[at : at + DET_ROWS] * scales[d][rows]
            )


def on_device(ngx, ngy, waveforms, templates, tpl_stations, det_station, det_time, partner):
    tpl_dev, k_slots, row_len = templates.shape
    det_dev = det_station.shape[0]
    groups = ngx * ngy
    stations = groups * STATIONS
    total = stations * SLOTS
    time_row, station_row = det_time.reshape(1, det_dev), det_station.reshape(1, det_dev)
    params = pltpu.CompilerParams(vmem_limit_bytes=(16 << 20) + groups * (1 << 17))
    packed = pl.pallas_call(
        pack_kernel,
        out_shape=jax.ShapeDtypeStruct((groups, PACKED, LANES), BF16),
        scratch_shapes=[pltpu.VMEM((PACKED, LANES), F32)],
        name="pack",
    )(waveforms.transpose(1, 0, 2), time_row, station_row)
    data = lax.all_to_all(packed, ("gx", "gy"), split_axis=0, concat_axis=0, tiled=True)
    tiles, scale, owner = pl.pallas_call(
        tile_kernel,
        out_shape=(
            jax.ShapeDtypeStruct((total * TAPS, CHANNELS * LANES), BF16),
            jax.ShapeDtypeStruct((total, LANES), F32),
            jax.ShapeDtypeStruct((tpl_dev, total), BF16),
        ),
        compiler_params=params,
        name="tiles",
    )(templates, tpl_stations.T)
    steps = groups // 4
    height = 4 * STATIONS * FINE * TAPS * SLOTS

    def whole(*shape):
        return pl.BlockSpec(shape, lambda i: (0,) * len(shape))

    def piece(*shape):
        return pl.BlockSpec(shape, lambda i: (i,) + (0,) * (len(shape) - 1))

    taps = pl.pallas_call(
        taps_kernel,
        grid=(steps,),
        in_specs=[whole(*tiles.shape)],
        out_specs=piece(height, DEPTH),
        out_shape=pltpu.HBM((steps * height, DEPTH), BF16),
        compiler_params=params,
        name="taps",
    )(tiles)
    taps = pltpu.with_memory_space_constraint(taps, pltpu.HBM)
    series, win = pl.pallas_call(
        windows_kernel,
        out_shape=(
            jax.ShapeDtypeStruct((groups, PACKED, LANES), F32),
            jax.ShapeDtypeStruct((groups, STATIONS, FINE, LANES), F32),
        ),
        compiler_params=params,
        name="windows",
    )(data)
    sums = (total, FINE * LANES)
    high, low = pl.pallas_call(
        correlate_kernel,
        grid=(steps,),
        in_specs=[whole(*series.shape), whole(*win.shape), piece(height, DEPTH), whole(*scale.shape)],
        out_specs=(whole(*sums), whole(*sums)),
        out_shape=(jax.ShapeDtypeStruct(sums, BF16),) * 2,
        scratch_shapes=[pltpu.VMEM((MXU, DEPTH), BF16)] * 4,
        compiler_params=params,
        name="correlate",
    )(series, win, taps, scale)
    stack = pl.pallas_call(
        stack_kernel,
        out_shape=jax.ShapeDtypeStruct((tpl_dev, LAG_BLOCKS * LANES), F32),
        compiler_params=params,
        name="stack",
    )(owner, high, low)
    diff = pl.pallas_call(
        functools.partial(detect_kernel, ngx, ngy),
        out_shape=jax.ShapeDtypeStruct((4 * det_dev, DTLAG), F32),
        scratch_shapes=[
            pltpu.VMEM((4 * DET_COARSE * DET_ROWS, DET_DEPTH), BF16),
            pltpu.VMEM((DET_FINE * DET_ROWS, DET_DEPTH), BF16),
            pltpu.VMEM((4 * det_dev, DET_FINE * DET_ROWS), F32),
        ],
        compiler_params=params,
        name="detect",
    )(data, time_row, station_row, partner.T)
    return stack, diff.reshape(det_dev, 4, DTLAG)


def solution(mesh):
    return jax.shard_map(
        functools.partial(on_device, mesh.shape["gx"], mesh.shape["gy"]),
        mesh=mesh,
        in_specs=(
            P(("gx", "gy"), None, None),
            P(("gx", "gy"), None, None),
            P(("gx", "gy"), None),
            P(("gx", "gy")),
            P(("gx", "gy")),
            P(("gx", "gy"), None),
        ),
        out_specs=(P(("gx", "gy"), None), P(("gx", "gy"), None, None)),
        check_vma=False,
    )
```

time: 67.4 us -> 79.5 us (1.18)
  Pallas kernels: 39.9 us -> 65.7 us
  blocking collectives: 22.8 us -> 0 us
  waiting for transfers between devices: 0.01 us -> 5.83 us
  starting transfers between devices: 1.74 us -> 7.1 us
  local copies, waits for them, and re-layouts: 1.84 us -> 0.03 us
    pallas_call x7 -> x5, Pallas kernels: 29.1 us -> 55.1 us  [the longest x1 39 us: on_device(): pl.pallas_call(correlate_kernel, grid=(steps,), in_specs=[whole(*series.s...]
    all_to_all x1 -> x0, blocking collectives: 22.8 us -> none  [on_device(): lax.all_to_all(packed, ('gx', 'gy'), split_axis=0, concat_axis=0, axis_in...]
    all_to_all x0 -> x1, starting transfers between devices: none -> 7.1 us  [on_device(): lax.all_to_all(packed, ('gx', 'gy'), split_axis=0, concat_axis=0, tiled=T...]
    all_to_all x0 -> x1, waiting for transfers between devices: none -> 5.83 us  [on_device(): lax.all_to_all(packed, ('gx', 'gy'), split_axis=0, concat_axis=0, tiled=T...]
    unnamed x10, local copies, waits for them, and re-layouts: 1.84 us -> 0.03 us
    ppermute x1 -> x0, starting transfers between devices: 1.74 us -> none  [on_device(): far = lax.ppermute(near, 'gx', [(x, x ^ 1) for x in range(ngx)])]
  transfers between devices with their start and end apart: 1 -> 1, of which waited for: 0 -> 1; matrix products, arithmetic and copies ran while one was open for 0% -> 0% of each run, Pallas kernels for 28% -> 15%
where the time goes in v4:
time: 79.5 us; the launch traced here: 79.3 us
  Pallas kernels  65.7 us (83%)
  starting transfers between devices  7.1 us (9%)
  waiting for transfers between devices  5.83 us (7%)
    pallas_call x1, Pallas kernels, on_device(): pl.pallas_call(correlate_kernel, grid=(steps,), in_specs=[whole(*series.s...  39 us
    pallas_call x1, Pallas kernels, on_device(): pl.pallas_call(taps_kernel, grid=(steps,), in_specs=[whole(*tiles.shape)]...  11.2 us
    pallas_call x1, Pallas kernels, on_device(): pl.pallas_call(functools.partial(detect_kernel, ngx, ngy), out_shape=jax....  9.04 us
    all_to_all x1, starting transfers between devices, on_device(): lax.all_to_all(packed, ('gx', 'gy'), split_axis=0, concat_axis=0, tiled=T...  7.1 us
    all_to_all x1, waiting for transfers between devices, on_device(): lax.all_to_all(packed, ('gx', 'gy'), split_axis=0, concat_axis=0, tiled=T...  5.83 us
    pallas_call x1, Pallas kernels, on_device(): pl.pallas_call(windows_kernel, out_shape=(jax.ShapeDtypeStruct((groups, P...  2.2 us
    pallas_call x1, Pallas kernels, on_device(): pl.pallas_call(pack_kernel, out_shape=jax.ShapeDtypeStruct((groups, PACKE...  1.73 us
  transfers between devices with their start and end apart: 1, of which 1 were waited for; matrix products, arithmetic and copies ran while one was open for 0% of the time, Pallas kernels for 15%

profile of v4, /device:TPU:1, one launch (start us, length us, event | category | flops | bytes accessed | tf_op | source)
XLA Modules:
  0.0 79.3 jit_solution(17788881315436569884)
XLA Ops:
  0.6 0.0 copy-start.1
  0.6 0.0 copy-start
  0.6 1.7 %pack.1 = bf16[32,80,128]{2,1,0:T(8,128)(2,1)} custom-call(bf16[3,2,1536]{2,1,0:T(2,128)(2,1)} %bitcast.13, s32[1,64]{1,0:T(1,128)} %bitcast.8, s32[1,64]{1,0:T(1,128)} %bitcast.10), custom_call_target="tpu_custom_call" | custom-call | tf_op jit(solution)/shard_map/pack/pallas_call | solution.py:423
  2.4 7.1 %all-to-all-start = ((bf16[32,80,128]{2,1,0:T(8,128)(2,1)}), bf16[32,80,128]{2,1,0:T(8,128)(2,1)S(1)}, u32[]{:S(2)}, u32[]{:S(2)}) async-start(bf16[32,80,128]{2,1,0:T(8,128)(2,1)} %pack.1), calls=%async_computation | async-start | bytes 1310720 | tf_op jit(solution)/shard_map/all_to_all | solution.py:429
  9.5 0.0 copy-done.1
  9.5 0.0 copy-done
  9.5 1.0 %tiles.1 = (bf16[2048,384]{1,0:T(8,128)(2,1)S(1)}, f32[512,128]{1,0:T(8,128)S(1)}, bf16[32,512]{1,0:T(8,128)(2,1)S(1)}) custom-call(bf16[32,8,1536]{2,1,0:T(8,128)(2,1)S(1)} %copy-done, s32[8,32]{1,0:T(8,128)S(1)} %bitcast.6), custom_call_target="tpu_custom_call" | custom-call | tf_op jit(solution)/shard_map/tiles/pallas_call | solution.py:430
  10.5 11.2 %taps.1.taps_ref = bf16[16384,512]{1,0:T(8,128)(2,1)} custom-call(bf16[2048,384]{1,0:T(8,128)(2,1)S(1)} %get-tuple-element.12.sorted_ref), custom_call_target="tpu_custom_call" | custom-call | tf_op jit(solution)/shard_map/taps/pallas_call | solution.py:449
  21.7 5.8 %all-to-all-done.data_ref = bf16[32,80,128]{2,1,0:T(8,128)(2,1)S(1)} async-done(((bf16[32,80,128]{2,1,0:T(8,128)(2,1)}), bf16[32,80,128]{2,1,0:T(8,128)(2,1)S(1)}, u32[]{:S(2)}, u32[]{:S(2)}) %all-to-all-start) | async-done | bytes 655392 | tf_op jit(solution)/shard_map/all_to_all | solution.py:429
  27.5 2.2 %windows.1 = (f32[32,80,128]{2,1,0:T(8,128)S(1)}, f32[32,2,8,128]{3,2,1,0:T(8,128)S(1)}) custom-call(bf16[32,80,128]{2,1,0:T(8,128)(2,1)S(1)} %all-to-all-done.data_ref), custom_call_target="tpu_custom_call" | custom-call | tf_op jit(solution)/shard_map/windows/pallas_call | solution.py:459
  29.7 39.0 %correlate.1 = (bf16[512,1024]{1,0:T(8,128)(2,1)S(1)}, bf16[512,1024]{1,0:T(8,128)(2,1)S(1)}) custom-call(f32[32,80,128]{2,1,0:T(8,128)S(1)} %get-tuple-element.10.rows_ref, f32[32,2,8,128]{3,2,1,0:T(8,128)S(1)} %get-tuple-element.11.win_ref, bf16[16384,512]{1,0:T(8,128)(2,1)} %taps.1.taps_ref, f32[512,128]{1,0:T(8,128)S(1)} %get-tuple-element.13.scale_ref), custom_call_target="tpu_custom_call" | custom-call | tf_op jit(solution)/shard_map/correlate/pallas_call | solution.py:469
  68.7 0.0 copy-start.2
  68.8 0.0 copy-start.3
  68.8 0.0 copy-start.4
  68.8 1.5 %stack.1 = f32[32,1024]{1,0:T(8,128)} custom-call(bf16[32,512]{1,0:T(8,128)(2,1)S(1)} %get-tuple-element.9.owner_ref, bf16[512,1024]{1,0:T(8,128)(2,1)S(1)} %get-tuple-element.14.high_ref, bf16[512,1024]{1,0:T(8,128)(2,1)S(1)} %get-tuple-element.15.low_ref), custom_call_target="tpu_custom_call" | custom-call | tf_op jit(solution)/shard_map/stack/pallas_call | solution.py:479
  70.3 0.0 copy-done.2
  70.3 0.0 copy-done.3
  70.3 0.0 copy-done.4
  70.3 9.0 %detect.1 = f32[256,128]{1,0:T(8,128)} custom-call(bf16[32,80,128]{2,1,0:T(8,128)(2,1)S(1)} %all-to-all-done.data_ref, s32[1,64]{1,0:T(1,128)S(1)} %bitcast.9, s32[1,64]{1,0:T(1,128)S(1)} %bitcast.11, s32[4,64]{1,0:T(4,128)S(1)} %bitcast.7), custom_call_target="tpu_custom_call" | custom-call | tf_op jit(solution)/shard_map/detect/pallas_call | solution.py:485
Async XLA Ops:
  0.6 8.9 %copy-start.1 = (s32[32,8]{0,1:T(8,128)S(1)}, s32[32,8]{0,1:T(8,128)}, u32[]{:S(2)}) copy-start(s32[32,8]{0,1:T(8,128)} %param.8) | copy-start | bytes 3076
  0.6 8.9 %copy-start = (bf16[32,8,1536]{2,1,0:T(8,128)(2,1)S(1)}, bf16[32,8,1536]{2,1,0:T(8,128)(2,1)}, u32[]{:S(2)}) copy-start(bf16[32,8,1536]{2,1,0:T(8,128)(2,1)} %tiles_ref.1) | copy-start | bytes 2359300
  2.4 25.2 %all-to-all-start = ((bf16[32,80,128]{2,1,0:T(8,128)(2,1)}), bf16[32,80,128]{2,1,0:T(8,128)(2,1)S(1)}, u32[]{:S(2)}, u32[]{:S(2)}) async-start(bf16[32,80,128]{2,1,0:T(8,128)(2,1)} %pack.1), calls=%async_computation | async-start | bytes 1310720 | tf_op jit(solution)/shard_map/all_to_all | solution.py:429
  68.7 1.5 %copy-start.2 = (s32[64,4]{0,1:T(4,128)S(1)}, s32[64,4]{0,1:T(4,128)}, u32[]{:S(2)}) copy-start(s32[64,4]{0,1:T(4,128)} %param.11) | copy-start | bytes 3076
  68.8 1.5 %copy-start.3 = (s32[64]{0:T(128)S(1)}, s32[64]{0:T(128)}, u32[]{:S(2)}) copy-start(s32[64]{0:T(128)} %param.10) | copy-start | bytes 772
  68.8 1.5 %copy-start.4 = (s32[64]{0:T(128)S(1)}, s32[64]{0:T(128)}, u32[]{:S(2)}) copy-start(s32[64]{0:T(128)} %param.9) | copy-start | bytes 772

commit v5 on v3

--- a/solution.py
+++ b/solution.py
@@ -29,7 +29,6 @@
 PACKED = ROWS + 8
 MXU = 256
 PASSES = (CHANNELS * (TAPS + 1) + 1) // 2
-SENT = 128
 EPS = 1e-06
 F32 = jnp.float32
 BF16 = jnp.bfloat16
@@ -87,9 +86,27 @@
     rows_ref[ROWS : ROWS + 1, :] = jnp.concatenate([row.astype(F32), pad], axis=1)
     rows_ref[ROWS + 1 : ROWS + 2, :] = jnp.concatenate([shift.astype(F32), pad], axis=1)
     rows_ref[ROWS + 2 : PACKED, :] = jnp.zeros((PACKED - ROWS - 2, LANES), F32)
-    count = out_ref.shape[0]
-    out_ref[:, 0:PACKED] = jnp.broadcast_to(rows_ref[...].astype(BF16)[None], (count, PACKED, LANES))
-    out_ref[:, PACKED:] = jnp.zeros((count, SENT - PACKED, LANES), BF16)
+    out_ref[0] = rows_ref[...].astype(BF16)
+
+
+def join_kernel(near_ref, other_ref, after_ref, out_ref):
+    half = near_ref.shape[0]
+    out_ref[0:half] = near_ref[...]
+    out_ref[half:] = other_ref[...]
+
+
+def rounds(ngx, ngy):
+    masks = []
+    for axis, size in (("gy", ngy), ("gx", ngx)):
+        while size > 1:
+            size //= 2
+            masks.append((axis, size))
+    return masks
+
+
+def position(ngx, ngy, x, y):
+    away = {"gx": x ^ lax.axis_index("gx"), "gy": y ^ lax.axis_index("gy")}
+    return sum(((away[axis] // mask) & 1) << n for n, (axis, mask) in enumerate(rounds(ngx, ngy)))
 
 
 def tile_kernel(ngx, ngy, tiles_ref, station_ref, sorted_ref, scale_ref, owner_ref):
@@ -109,9 +126,7 @@
     rank = jnp.sum(jnp.where((st_col == st_row) & earlier, 1.0, 0.0), axis=0, keepdims=True)
     st = st_row.astype(jnp.int32)
     group = st // STATIONS
-    x, y = group // ngy, group % ngy
-    away = (x + lax.axis_index("gx")) % 2
-    place_of = away * (ngx * ngy // 2) + x // 2 * ngy + y
+    place_of = position(ngx, ngy, group // ngy, group % ngy)
     slot = (place_of * STATIONS + st % STATIONS) * SLOTS + rank.astype(jnp.int32)
     tiles = tiles_ref[...].reshape(count, row_len)
     step = 128
@@ -135,7 +150,7 @@
     major, chunk = iota((step, FINE, LANES), 1), iota((step, FINE, LANES), 2) // COARSE
 
     def body(q, carry):
-        x = data_ref[pl.ds(q * step, step), 0:PACKED].astype(F32)
+        x = data_ref[pl.ds(q * step, step)].astype(F32)
         rows_ref[pl.ds(q * step, step)] = x
         energy = sum(x[:, SPAN * c : SPAN * (c + 1)] * x[:, SPAN * c : SPAN * (c + 1)] for c in range(CHANNELS))
         sums = sum(dot(part, sums_of) for part in pieces(energy.reshape(step * SPAN, LANES), 3))
@@ -168,8 +183,11 @@
     now = None
     for block in range(BLOCKS):
         at = SPAN * c + BLOCKS * s + block
-        row = jnp.broadcast_to(rows_ref[g, at : at + 1, :], (COARSE, LANES))
-        later = pltpu.roll(row, FINE, 1, stride=FINE, stride_axis=0).astype(BF16)
+        row = rows_ref[g, pl.ds(at, FINE, stride=0), :]
+        turned = [
+            pltpu.roll(row, FINE * (1 + first), 1, stride=FINE, stride_axis=0) for first in range(0, COARSE, FINE)
+        ]
+        later = jnp.concatenate(turned, axis=0).astype(BF16)
         if block:
             out_ref[(block - 1) * COARSE : block * COARSE, c * LANES : (c + 1) * LANES] = jnp.where(
                 lane < bound, now, later
@@ -198,7 +216,7 @@
         out_ref[rows, at : at + LANES] = tail
 
 
-def taps_kernel(sorted_ref, out_ref):
+def taps_kernel(first, sorted_ref, after_ref, out_ref):
     height = FINE * STATIONS * SLOTS
     per_step = out_ref.shape[0] // height
     rows = STATIONS * SLOTS
@@ -206,7 +224,7 @@
     zero = jnp.zeros((rows, LANES), BF16)
 
     def body(i, carry):
-        at = (pl.program_id(0) * per_step + i) * rows
+        at = (first() * per_step + i) * rows
         tiles = sorted_ref[pl.ds(pl.multiple_of(at, rows), rows), :]
         out = out_ref.at[pl.ds(pl.multiple_of(i * height, height), height), :]
         for c in range(CHANNELS):
@@ -319,15 +337,10 @@
     shift = jnp.broadcast_to(shift, (det_dev, LANES))
     for bit in range(7):
         size = 1 << bit
-        moves = (shift // size) % 2 == 1
-        inner = lane < LANES - size
-        for c in range(CHANNELS):
-            turned = [rot(found[c][j], -size) for j in range(blocks)]
-            turned.append(turned[-1])
-            found[c] = [
-                jnp.where(moves, jnp.where(inner, turned[j], turned[j + 1]), found[c][j]) for j in range(blocks)
-            ]
-    return [found[c][: blocks - 1] for c in range(CHANNELS)]
+        moves = (shift & size) > 0
+        found = [[jnp.where(moves, rot(block, -size), block) for block in row] for row in found]
+    inside = lane < LANES - shift
+    return [[jnp.where(inside, row[j], row[j + 1]) for j in range(blocks - 1)] for row in found]
 
 
 def mean_square(blocks):
@@ -340,11 +353,14 @@
 
 
 def own_windows(data, time_ref, station_ref):
-    start = column(time_ref[...])
-    row = column(station_ref[...]) * BLOCKS + start // LANES
-    mine = cut(data, row, start % LANES, KEEP + 1)
+    n = time_ref.shape[1]
+    turned = iota((n, n), 0) ^ (DET_ROWS - 1) == iota((n, n), 1)
+    start = jnp.sum(jnp.where(turned, time_ref[...], 0), axis=1, keepdims=True)
+    station = jnp.sum(jnp.where(turned, station_ref[...], 0), axis=1, keepdims=True)
+    mine = cut(data, station * BLOCKS + start // LANES, start % LANES, KEEP + 1)
     scale = lax.rsqrt(CHANNELS * W * (mean_square([(block, None) for blocks in mine for block in blocks]) + EPS))
-    return mine, scale
+    scale = jnp.sum(jnp.where(turned, scale, 0.0), axis=0, keepdims=True)
+    return mine, column(scale)
 
 
 def partner_windows(data, chosen_row):
@@ -358,37 +374,32 @@
     return pieces_of, lax.rsqrt(mean_square(centre) + EPS)
 
 
-def turn_over(block):
-    n = block.shape[0]
-    return dot(ones_where(iota((n, n), 0) + iota((n, n), 1) == n - 1), block).astype(BF16)
-
-
-def differential(mine, windows, x_ref, w_ref, parts_ref):
+def differential(taps_ref, windows, x_ref, parts_ref):
     count = len(windows)
-    det_dev = mine[0][0].shape[0]
     height = count * DET_ROWS
     lane = iota((DET_ROWS, LANES), 1)
     wide = DET_FINE * DET_ROWS
     sub_lane = iota((8, LANES), 1) % DET_ROWS
-    for q in range(det_dev // DET_ROWS):
+    for q in range(taps_ref.shape[0]):
         rows = slice(q * DET_ROWS, (q + 1) * DET_ROWS)
-        build_taps([[turn_over(block[rows]) for block in blocks] for blocks in mine], DET_FINE, DET_ROWS, w_ref, 0, DET_ROWS)
         for d in range(count):
             source = [[block[rows] for block in blocks] for blocks in windows[d]]
+            ends = {}
             for a in range(DET_COARSE):
                 shift = DET_FINE * a
                 out = slice((a * count + d) * DET_ROWS, (a * count + d + 1) * DET_ROWS)
                 tail = None
                 for c in range(CHANNELS):
                     moved = [rot(block, -shift) for block in source[c]]
+                    ends[c, a] = moved[KEEP]
                     for j in range(KEEP):
                         block = jnp.where(lane < LANES - shift, moved[j], moved[j + 1]) if a else moved[j]
                         at = (c * KEEP + j) * LANES
                         x_ref[out, at : at + LANES] = block
-                    end = rot(source[c][KEEP], DET_FINE * c - shift)
+                    end = ends[c, a - c] if a >= c else rot(source[c][KEEP], DET_FINE * c - shift)
                     tail = end if tail is None else jnp.where(lane < DET_FINE * c, tail, end)
                 x_ref[out, DET_DEPTH - LANES : DET_DEPTH] = tail
-        raw = dot_nt(x_ref[0 : DET_COARSE * height, :], w_ref[...])
+        raw = dot_nt(x_ref[0 : DET_COARSE * height, :], taps_ref[q])
         for half in range(2):
             for row in range(0, height, 8):
                 upper = row % DET_ROWS // 8
@@ -404,27 +415,38 @@
     return sum(dot(part, order) for part in pieces(parts_ref[...], 2))
 
 
-def detect_kernel(
-    ngx, ngy, near_ref, far_ref, time_ref, station_ref, partner_ref, diff_ref, x_ref, w_ref, parts_ref
-):
+def own_kernel(data_ref, time_ref, station_ref, after_ref, taps_ref, scale_ref):
+    mine, scale = own_windows(data_ref[0], time_ref, station_ref)
+    scale_ref[...] = jnp.broadcast_to(scale, scale_ref.shape)
+    for q in range(taps_ref.shape[0]):
+        rows = slice(q * DET_ROWS, (q + 1) * DET_ROWS)
+        blocks = [[block[rows] for block in channel] for channel in mine]
+        build_taps(blocks, DET_FINE, DET_ROWS, taps_ref.at[q], 0, DET_ROWS)
+
+
+def cuts_kernel(ngx, ngy, near_ref, far_ref, scale_ref, partner_ref, windows_ref, scales_ref):
     gx, gy = lax.axis_index("gx"), lax.axis_index("gy")
-    mine, mine_scale = own_windows(near_ref[gx // 2 * ngy + gy, 0:PACKED], time_ref, station_ref)
-    windows, scales = [], []
     for d, (dx, dy) in enumerate(((1, 0), (-1, 0), (0, 1), (0, -1))):
         x, y = gx + dx, gy + dy
         valid = (x >= 0) & (x < ngx) & (y >= 0) & (y < ngy)
-        other = jnp.clip(x, 0, ngx - 1) // 2 * ngy + jnp.clip(y, 0, ngy - 1)
-        data = (far_ref if dx else near_ref)[other, 0:PACKED]
+        at = position(ngx, ngy, jnp.clip(x, 0, ngx - 1), jnp.clip(y, 0, ngy - 1)) % near_ref.shape[0]
+        data = (far_ref if dx else near_ref)[at]
         found, scale = partner_windows(data, partner_ref[d : d + 1, :])
-        windows.append(found)
-        scales.append(jnp.where(valid, mine_scale * scale, 0.0))
-    out = differential(mine, windows, x_ref, w_ref, parts_ref)
-    for q in range(time_ref.shape[1] // DET_ROWS):
+        for c in range(CHANNELS):
+            for j in range(KEEP + 1):
+                windows_ref[d, c, j] = found[c][j]
+        scales_ref[d] = jnp.where(valid, scale_ref[...] * scale, 0.0)
+
+
+def detect_kernel(taps_ref, windows_ref, scales_ref, diff_ref, x_ref, parts_ref):
+    windows = [[[windows_ref[d, c, j] for j in range(KEEP + 1)] for c in range(CHANNELS)] for d in range(4)]
+    out = differential(taps_ref, windows, x_ref, parts_ref)
+    for q in range(taps_ref.shape[0]):
         for d in range(4):
             at = (q * 4 + d) * DET_ROWS
             rows = slice(q * DET_ROWS, (q + 1) * DET_ROWS)
             diff_ref[pl.ds(q * DET_ROWS * 4 + d, DET_ROWS, stride=4), :] = (
-                out[at : at + DET_ROWS] * scales[d][rows]
+                out[at : at + DET_ROWS] * scales_ref[d, rows, :]
             )
 
 
@@ -438,14 +460,16 @@
     time_row, station_row = det_time.reshape(1, det_dev), det_station.reshape(1, det_dev)
     packed = pl.pallas_call(
         pack_kernel,
-        out_shape=jax.ShapeDtypeStruct((half, SENT, LANES), BF16),
+        out_shape=jax.ShapeDtypeStruct((1, PACKED, LANES), BF16),
         scratch_shapes=[pltpu.VMEM((PACKED, LANES), F32)],
         name="pack",
     )(waveforms.transpose(1, 0, 2), time_row, station_row)
-    members = [[x * ngy + y for x in range(parity, ngx, 2) for y in range(ngy)] for parity in range(2)]
-    near = lax.all_to_all(
-        packed, ("gx", "gy"), split_axis=0, concat_axis=0, axis_index_groups=members, tiled=True
-    )
+
+    def swap(value, axis, mask):
+        size = {"gx": ngx, "gy": ngy}[axis]
+        return lax.ppermute(value, axis, [(n, n ^ mask) for n in range(size)])
+
+    vmem, after = pl.BlockSpec(memory_space=pltpu.VMEM), pl.BlockSpec(memory_space=pl.ANY)
     tiles, scale, owner = pl.pallas_call(
         functools.partial(tile_kernel, ngx, ngy),
         out_shape=(
@@ -459,17 +483,65 @@
     steps = groups // 4
     height = 4 * FINE * rows
     depth = MXU * PASSES
-    taps = pl.pallas_call(
-        taps_kernel,
-        grid=(steps,),
-        in_specs=[pl.BlockSpec((total, row_len), lambda i: (0, 0))],
-        out_specs=pl.BlockSpec((height, depth), lambda i: (i, 0)),
-        out_shape=pltpu.HBM((steps * height, depth), BF16),
-        compiler_params=pltpu.CompilerParams(vmem_limit_bytes=(8 << 20) + total * row_len * 4),
-        name="taps",
-    )(tiles)
-    taps = pltpu.with_memory_space_constraint(taps, pltpu.HBM)
-    far = lax.ppermute(near, "gx", [(x, x ^ 1) for x in range(ngx)])
+    def shifted(call, near):
+        shape = (steps // 2 * height, depth)
+        limit = pltpu.CompilerParams(vmem_limit_bytes=(8 << 20) + total * row_len * 4)
+        if groups <= 32:
+            taps = pl.pallas_call(
+                functools.partial(taps_kernel, lambda: call),
+                in_specs=[vmem, after],
+                out_specs=vmem,
+                out_shape=pltpu.VMEM(shape, BF16),
+                compiler_params=limit,
+                name="taps",
+            )(tiles, near)
+            return pltpu.with_memory_space_constraint(taps, pltpu.VMEM)
+        taps = pl.pallas_call(
+            functools.partial(taps_kernel, lambda: pl.program_id(0)),
+            grid=(steps // 2,),
+            in_specs=[pl.BlockSpec((total // 2, row_len), lambda i: (call, 0)), after],
+            out_specs=pl.BlockSpec((height, depth), lambda i: (i, 0)),
+            out_shape=pltpu.HBM(shape, BF16),
+            compiler_params=limit,
+            name="taps",
+        )(tiles, near)
+        return pltpu.with_memory_space_constraint(taps, pltpu.HBM)
+
+    parts = det_dev // DET_ROWS
+
+    def own_detections(near):
+        return pl.pallas_call(
+            own_kernel,
+            out_shape=(
+                jax.ShapeDtypeStruct((parts, DET_FINE * DET_ROWS, DET_DEPTH), BF16),
+                jax.ShapeDtypeStruct((det_dev, LANES), F32),
+            ),
+            in_specs=[vmem, vmem, vmem, after],
+            compiler_params=pltpu.CompilerParams(vmem_limit_bytes=16 << 20),
+            name="own",
+        )(packed, time_row, station_row, near)
+
+    near, taps = packed, []
+    *first, last = rounds(ngx, ngy)
+    for n, (axis, mask) in enumerate(first):
+        other = swap(near, axis, mask)
+        beside = near
+        if n == 0:
+            beside = scale
+        elif n <= 2:
+            taps.append(shifted(n - 1, near))
+            beside = taps[-1]
+        elif n == len(first) - 1:
+            mine, mine_scale = own_detections(near)
+            beside = mine_scale
+        near = pl.pallas_call(
+            join_kernel,
+            out_shape=jax.ShapeDtypeStruct((2 * near.shape[0], PACKED, LANES), BF16),
+            in_specs=[vmem, vmem, after],
+            compiler_params=pltpu.CompilerParams(vmem_limit_bytes=16 << 20),
+            name="join",
+        )(near, other, beside)
+    far = swap(near, *last)
 
     def whole(*shape):
         return pl.BlockSpec(shape, lambda i: (0,) * len(shape))
@@ -493,7 +565,7 @@
             in_specs=[
                 whole(*series.shape),
                 whole(*win.shape),
-                pl.BlockSpec((height, depth), lambda i: (call * steps // 2 + i, 0)),
+                pl.BlockSpec((height, depth), lambda i: (i, 0)),
                 whole(*scale.shape),
             ],
             out_specs=(whole(*sums), whole(*sums)),
@@ -501,7 +573,7 @@
             scratch_shapes=[pltpu.VMEM((BLOCKS * COARSE, CHANNELS * LANES), BF16)] * 8,
             compiler_params=params,
             name="correlate",
-        )(series, win, taps, scale)
+        )(series, win, taps[call], scale)
 
     near_sums, far_sums = correlate(0, near), correlate(1, far)
     stack = pl.pallas_call(
@@ -510,17 +582,25 @@
         compiler_params=params,
         name="stack",
     )(owner, *near_sums, *far_sums)
+    cuts = pl.pallas_call(
+        functools.partial(cuts_kernel, ngx, ngy),
+        out_shape=(
+            jax.ShapeDtypeStruct((4, CHANNELS, KEEP + 1, det_dev, LANES), BF16),
+            jax.ShapeDtypeStruct((4, det_dev, LANES), F32),
+        ),
+        compiler_params=params,
+        name="cuts",
+    )(near, far, mine_scale, partner.T)
     diff = pl.pallas_call(
-        functools.partial(detect_kernel, ngx, ngy),
+        detect_kernel,
         out_shape=jax.ShapeDtypeStruct((4 * det_dev, DTLAG), F32),
         scratch_shapes=[
             pltpu.VMEM((4 * DET_COARSE * DET_ROWS, DET_DEPTH), BF16),
-            pltpu.VMEM((DET_FINE * DET_ROWS, DET_DEPTH), BF16),
             pltpu.VMEM((4 * det_dev, DET_FINE * DET_ROWS), F32),
         ],
-        compiler_params=pltpu.CompilerParams(vmem_limit_bytes=(16 << 20) + groups * (1 << 15)),
+        compiler_params=params,
         name="detect",
-    )(near, far, time_row, station_row, partner.T)
+    )(mine, *cuts)
     return stack, diff.reshape(det_dev, 4, DTLAG)
 
 

time: 67.4 us -> 46.5 us (0.69)
  blocking collectives: 22.8 us -> 0 us
  Pallas kernels: 39.9 us -> 31.2 us
  starting transfers between devices: 1.74 us -> 10 us
  waiting for transfers between devices: 0.01 us -> 1.57 us
  local copies, waits for them, and re-layouts: 1.84 us -> 2.56 us
    all_to_all x1 -> x0, blocking collectives: 22.8 us -> none  [on_device(): lax.all_to_all(packed, ('gx', 'gy'), split_axis=0, concat_axis=0, axis_in...]
    ppermute x1 -> x5, starting transfers between devices: 1.74 us -> 10 us  [swap(): return lax.ppermute(value, axis, [(n, n ^ mask) for n in range(size)])]
    pallas_call x3 -> x10, Pallas kernels: 19.5 us -> 14.7 us  [the longest x2 5.27 us: shifted(): pl.pallas_call(functools.partial(taps_kernel, lambda: call), in_specs=[vm...]
    pallas_call x2, Pallas kernels: 15.6 us -> 11.9 us  [correlate(): pl.pallas_call(functools.partial(correlate_kernel, call), grid=(steps //...]
    ppermute x1 -> x5, waiting for transfers between devices: 0.01 us -> 1.57 us  [swap(): return lax.ppermute(value, axis, [(n, n ^ mask) for n in range(size)])]
    unnamed x10 -> x12, local copies, waits for them, and re-layouts: 1.84 us -> 2.56 us
  transfers between devices with their start and end apart: 1 -> 5, of which waited for: 0 -> 1; matrix products, arithmetic and copies ran while one was open for 0% -> 0% of each run, Pallas kernels for 28% -> 32%
where the time goes in v5:
time: 46.5 us; the launch traced here: 46.2 us
  Pallas kernels  31.2 us (67%)
  starting transfers between devices  10 us (22%)
  local copies, waits for them, and re-layouts  2.56 us (6%)
  waiting for transfers between devices  1.57 us (3%)
  between operations  0.78 us (2%)
    pallas_call x2, Pallas kernels, correlate(): pl.pallas_call(functools.partial(correlate_kernel, call), grid=(steps //...  11.9 us
    ppermute x5, starting transfers between devices, swap(): return lax.ppermute(value, axis, [(n, n ^ mask) for n in range(size)])  10 us
    pallas_call x2, Pallas kernels, shifted(): pl.pallas_call(functools.partial(taps_kernel, lambda: call), in_specs=[vm...  5.27 us
    pallas_call x1, Pallas kernels, on_device(): pl.pallas_call(functools.partial(cuts_kernel, ngx, ngy), out_shape=(jax.S...  3.29 us
    pallas_call x1, Pallas kernels, on_device(): pl.pallas_call(detect_kernel, out_shape=jax.ShapeDtypeStruct((4 * det_dev...  3.29 us
    unnamed x12, local copies, waits for them, and re-layouts  2.56 us
    pallas_call x2, Pallas kernels, correlate(): pl.pallas_call(windows_kernel, out_shape=(jax.ShapeDtypeStruct((half, PAC...  2.22 us
    ppermute x5, waiting for transfers between devices, swap(): return lax.ppermute(value, axis, [(n, n ^ mask) for n in range(size)])  1.57 us
  transfers between devices with their start and end apart: 5, of which 1 were waited for; matrix products, arithmetic and copies ran while one was open for 0% of the time, Pallas kernels for 32%

profile of v5, /device:TPU:1, one launch (start us, length us, event | category | flops | bytes accessed | tf_op | source)
XLA Modules:
  0.0 46.2 jit_solution(8801893946872209247)
XLA Ops:
  0.6 1.4 %pack.1.near_ref.data_ref = bf16[1,80,128]{2,1,0:T(8,128)(2,1)} custom-call(bf16[3,2,1536]{2,1,0:T(2,128)(2,1)} %bitcast.13, s32[1,64]{1,0:T(1,128)} %bitcast.8, s32[1,64]{1,0:T(1,128)} %bitcast.10), custom_call_target="tpu_custom_call" | custom-call | tf_op jit(solution)/shard_map/pack/pallas_call | solution.py:461
  2.0 3.1 %collective-permute-start = (bf16[1,80,128]{2,1,0:T(8,128)(2,1)}, bf16[1,80,128]{2,1,0:T(8,128)(2,1)S(1)}, u32[]{:S(2)}, u32[]{:S(2)}) collective-permute-start(bf16[1,80,128]{2,1,0:T(8,128)(2,1)} %pack.1.near_ref.data_ref), channel_id=1, source_target_pairs={{0,2},{1,3},{2,0},{3,1},{4,6},{5,7},{6,4},{7,5},{8,10},{9,11},{10,... | collective-permute-start | bytes 61448 | tf_op jit(solution)/shard_map/ppermute | solution.py:470
  5.2 0.0 copy-start
  5.2 1.1 %copy-done = bf16[32,8,1536]{2,1,0:T(8,128)(2,1)S(1)} copy-done((bf16[32,8,1536]{2,1,0:T(8,128)(2,1)S(1)}, bf16[32,8,1536]{2,1,0:T(8,128)(2,1)}, u32[]{:S(2)}) %copy-start) | copy-done | bytes 786456
  6.3 0.0 copy-start.2
  6.3 0.7 %copy-done.2 = s32[32,8]{0,1:T(8,128)S(1)} copy-done((s32[32,8]{0,1:T(8,128)S(1)}, s32[32,8]{0,1:T(8,128)}, u32[]{:S(2)}) %copy-start.2) | copy-done | bytes 1048
  7.0 1.0 %tiles.1 = (bf16[512,1536]{1,0:T(8,128)(2,1)S(1)}, f32[512,128]{1,0:T(8,128)S(1)}, bf16[32,512]{1,0:T(8,128)(2,1)S(1)}) custom-call(bf16[32,8,1536]{2,1,0:T(8,128)(2,1)S(1)} %copy-done, s32[8,32]{1,0:T(8,128)S(1)} %bitcast.6), custom_call_target="tpu_custom_call" | custom-call | tf_op jit(solution)/shard_map/tiles/pallas_call | solution.py:473
  7.9 0.0 collective-permute-done.other_ref
  8.0 0.0 copy-start.1
  8.0 0.7 %copy-done.1 = bf16[1,80,128]{2,1,0:T(8,128)(2,1)S(1)} copy-done((bf16[1,80,128]{2,1,0:T(8,128)(2,1)S(1)}, bf16[1,80,128]{2,1,0:T(8,128)(2,1)}, u32[]{:S(2)}) %copy-start.1) | copy-done | bytes 20504
  8.7 1.3 %collective-permute-start.1 = (bf16[2,80,128]{2,1,0:T(8,128)(2,1)S(1)}, bf16[2,80,128]{2,1,0:T(8,128)(2,1)S(1)}, u32[]{:S(2)}, u32[]{:S(2)}) collective-permute-start(bf16[2,80,128]{2,1,0:T(8,128)(2,1)S(1)} %join.4.after_ref.near_ref), channel_id=1, source_target_pairs={{0,1},{1,0},{2,3},{3,2},{4,5},{5,4},{6,7},{7,6},{8,9},{9,8},{10,11... | collective-permute-start | bytes 122888 | tf_op jit(solution)/shard_map/ppermute | solution.py:470
  10.0 2.6 %taps.2.after_ref.taps_ref = bf16[2048,2048]{1,0:T(8,128)(2,1)S(1)} custom-call(bf16[512,1536]{1,0:T(8,128)(2,1)S(1)} %get-tuple-element.19.sorted_ref, bf16[2,80,128]{2,1,0:T(8,128)(2,1)S(1)} %join.4.after_ref.near_ref), custom_call_target="tpu_custom_call" | custom-call | tf_op jit(solution)/shard_map/taps/pallas_call | solution.py:490
  12.6 0.0 collective-permute-done.1.other_ref
  12.6 0.0 copy-start.4
  12.7 0.0 copy-start.5
  12.7 1.3 %collective-permute-start.2 = (bf16[4,80,128]{2,1,0:T(8,128)(2,1)S(1)}, bf16[4,80,128]{2,1,0:T(8,128)(2,1)S(1)}, u32[]{:S(2)}, u32[]{:S(2)}) collective-permute-start(bf16[4,80,128]{2,1,0:T(8,128)(2,1)S(1)} %join.5.after_ref.near_ref), channel_id=1, source_target_pairs={{0,16},{4,20},{8,24},{12,28},{16,0},{20,4},{24,8},{28,12},{1,17},{... | collective-permute-start | bytes 245768 | tf_op jit(solution)/shard_map/ppermute | solution.py:470
  14.0 2.6 %taps.3.after_ref.taps_ref = bf16[2048,2048]{1,0:T(8,128)(2,1)S(1)} custom-call(bf16[512,1536]{1,0:T(8,128)(2,1)S(1)} %get-tuple-element.19.sorted_ref, bf16[4,80,128]{2,1,0:T(8,128)(2,1)S(1)} %join.5.after_ref.near_ref), custom_call_target="tpu_custom_call" | custom-call | tf_op jit(solution)/shard_map/taps/pallas_call | solution.py:490
  16.6 0.0 collective-permute-done.2.other_ref
  16.7 1.3 %collective-permute-start.3 = (bf16[8,80,128]{2,1,0:T(8,128)(2,1)S(1)}, bf16[8,80,128]{2,1,0:T(8,128)(2,1)S(1)}, u32[]{:S(2)}, u32[]{:S(2)}) collective-permute-start(bf16[8,80,128]{2,1,0:T(8,128)(2,1)S(1)} %join.6.after_ref.near_ref), channel_id=1, source_target_pairs={{0,8},{4,12},{8,0},{12,4},{16,24},{20,28},{24,16},{28,20},{1,9},{5... | collective-permute-start | bytes 491528 | tf_op jit(solution)/shard_map/ppermute | solution.py:470
  17.9 0.0 copy-done.4
  17.9 0.0 copy-done.5
  17.9 1.4 %own.1 = (bf16[4,256,896]{2,1,0:T(8,128)(2,1)S(1)}, f32[64,128]{1,0:T(8,128)S(1)}) custom-call(bf16[1,80,128]{2,1,0:T(8,128)(2,1)S(1)} %copy-done.1, s32[1,64]{1,0:T(1,128)S(1)} %bitcast.9, s32[1,64]{1,0:T(1,128)S(1)} %bitcast.11, bf16[8,80,128]{2,1,0:T(8,128)(2,1)S(1)} %join.6.after_ref.near_ref), custom_call_target="tpu_custom_call" | custom-call | tf_op jit(solution)/shard_map/own/pallas_call | solution.py:513
  19.3 1.6 %collective-permute-done.3.other_ref = bf16[8,80,128]{2,1,0:T(8,128)(2,1)S(1)} collective-permute-done((bf16[8,80,128]{2,1,0:T(8,128)(2,1)S(1)}, bf16[8,80,128]{2,1,0:T(8,128)(2,1)S(1)}, u32[]{:S(2)}, u32[]{:S(2)}) %collective-permute-start.3) | collective-permute-done | bytes 163872 | tf_op jit(solution)/shard_map/ppermute | solution.py:470
  20.9 3.0 %collective-permute-start.4 = (bf16[16,80,128]{2,1,0:T(8,128)(2,1)S(1)}, bf16[16,80,128]{2,1,0:T(8,128)(2,1)S(1)}, u32[]{:S(2)}, u32[]{:S(2)}) collective-permute-start(bf16[16,80,128]{2,1,0:T(8,128)(2,1)S(1)} %join.7.data_ref.near_ref), channel_id=1, source_target_pairs={{0,4},{4,0},{8,12},{12,8},{16,20},{20,16},{24,28},{28,24},{1,5},{5... | collective-permute-start | bytes 983048 | tf_op jit(solution)/shard_map/ppermute | solution.py:470
  23.9 1.1 %windows.2 = (f32[16,80,128]{2,1,0:T(8,128)S(1)}, f32[16,2,8,128]{3,2,1,0:T(8,128)S(1)}) custom-call(bf16[16,80,128]{2,1,0:T(8,128)(2,1)S(1)} %join.7.data_ref.near_ref), custom_call_target="tpu_custom_call" | custom-call | tf_op jit(solution)/shard_map/windows/pallas_call | solution.py:553
  25.0 0.0 copy-start.3
  25.0 5.9 %correlate.2 = (bf16[256,1024]{1,0:T(8,128)(2,1)S(1)}, bf16[256,1024]{1,0:T(8,128)(2,1)S(1)}) custom-call(f32[16,80,128]{2,1,0:T(8,128)S(1)} %get-tuple-element.21.rows_ref, f32[16,2,8,128]{3,2,1,0:T(8,128)S(1)} %get-tuple-element.22.win_ref, bf16[2048,2048]{1,0:T(8,128)(2,1)S(1)} %taps.2.after_ref.taps_ref, f32[512,128]{1,0:T(8,128)S(1)} %get-tuple-element.18.after_ref.scale_ref), custom_call_target="tpu_custom_call" | custom-call | tf_op jit(solution)/shard_map/correlate/pallas_call | solution.py:562
  31.0 0.0 collective-permute-done.4.data_ref.far_ref
  31.0 1.1 %windows.3 = (f32[16,80,128]{2,1,0:T(8,128)S(1)}, f32[16,2,8,128]{3,2,1,0:T(8,128)S(1)}) custom-call(bf16[16,80,128]{2,1,0:T(8,128)(2,1)S(1)} %collective-permute-done.4.data_ref.far_ref), custom_call_target="tpu_custom_call" | custom-call | tf_op jit(solution)/shard_map/windows/pallas_call | solution.py:553
  32.1 5.9 %correlate.3 = (bf16[256,1024]{1,0:T(8,128)(2,1)S(1)}, bf16[256,1024]{1,0:T(8,128)(2,1)S(1)}) custom-call(f32[16,80,128]{2,1,0:T(8,128)S(1)} %get-tuple-element.25.rows_ref, f32[16,2,8,128]{3,2,1,0:T(8,128)S(1)} %get-tuple-element.26.win_ref, bf16[2048,2048]{1,0:T(8,128)(2,1)S(1)} %taps.3.after_ref.taps_ref, f32[512,128]{1,0:T(8,128)S(1)} %get-tuple-element.18.after_ref.scale_ref), custom_call_target="tpu_custom_call" | custom-call | tf_op jit(solution)/shard_map/correlate/pallas_call | solution.py:562
  38.0 0.0 copy-done.3
  38.1 3.3 %cuts.1 = (bf16[4,3,3,64,128]{4,3,2,1,0:T(8,128)(2,1)S(1)}, f32[4,64,128]{2,1,0:T(8,128)S(1)}) custom-call(bf16[16,80,128]{2,1,0:T(8,128)(2,1)S(1)} %join.7.data_ref.near_ref, bf16[16,80,128]{2,1,0:T(8,128)(2,1)S(1)} %collective-permute-done.4.data_ref.far_ref, f32[64,128]{1,0:T(8,128)S(1)} %get-tuple-element.20.after_ref.scale_ref, s32[4,64]{1,0:T(4,128)S(1)} %bitcast.7), custom_call_target="tpu_custom_call" | custom-call | tf_op jit(solution)/shard_map/cuts/pallas_call | solution.py:585
  41.3 3.3 %detect.1 = f32[256,128]{1,0:T(8,128)} custom-call(bf16[4,256,896]{2,1,0:T(8,128)(2,1)S(1)} %get-tuple-element.29.taps_ref, bf16[4,3,3,64,128]{4,3,2,1,0:T(8,128)(2,1)S(1)} %get-tuple-element.30.windows_ref, f32[4,64,128]{2,1,0:T(8,128)S(1)} %get-tuple-element.31.scales_ref), custom_call_target="tpu_custom_call" | custom-call | tf_op jit(solution)/shard_map/detect/pallas_call | solution.py:594
  44.6 1.5 %stack.1 = f32[32,1024]{1,0:T(8,128)} custom-call(bf16[32,512]{1,0:T(8,128)(2,1)S(1)} %get-tuple-element.17.owner_ref, bf16[256,1024]{1,0:T(8,128)(2,1)S(1)} %get-tuple-element.23.near_high_ref, bf16[256,1024]{1,0:T(8,128)(2,1)S(1)} %get-tuple-element.24.near_low_ref, bf16[256,1024]{1,0:T(8,128)(2,1)S(1)} %get-tuple-element.27.far_high_ref, ...), custom_call_target="tpu_custom_call" | custom-call | tf_op jit(solution)/shard_map/stack/pallas_call | solution.py:579
  (4 shorter events, 0.0 us)
Async XLA Ops:
  2.0 5.9 %collective-permute-start = (bf16[1,80,128]{2,1,0:T(8,128)(2,1)}, bf16[1,80,128]{2,1,0:T(8,128)(2,1)S(1)}, u32[]{:S(2)}, u32[]{:S(2)}) collective-permute-start(bf16[1,80,128]{2,1,0:T(8,128)(2,1)} %pack.1.near_ref.data_ref), channel_id=1, source_target_pairs={{0,2},{1,3},{2,0},{3,1},{4,6},{5,7},{6,4},{7,5},{8,10},{9,11},{10,... | collective-permute-start | bytes 61448 | tf_op jit(solution)/shard_map/ppermute | solution.py:470
  5.2 1.1 %copy-start = (bf16[32,8,1536]{2,1,0:T(8,128)(2,1)S(1)}, bf16[32,8,1536]{2,1,0:T(8,128)(2,1)}, u32[]{:S(2)}) copy-start(bf16[32,8,1536]{2,1,0:T(8,128)(2,1)} %tiles_ref.1) | copy-start | bytes 2359300
  6.3 0.7 %copy-start.2 = (s32[32,8]{0,1:T(8,128)S(1)}, s32[32,8]{0,1:T(8,128)}, u32[]{:S(2)}) copy-start(s32[32,8]{0,1:T(8,128)} %param.8) | copy-start | bytes 3076
  8.0 0.7 %copy-start.1 = (bf16[1,80,128]{2,1,0:T(8,128)(2,1)S(1)}, bf16[1,80,128]{2,1,0:T(8,128)(2,1)}, u32[]{:S(2)}) copy-start(bf16[1,80,128]{2,1,0:T(8,128)(2,1)} %pack.1.near_ref.data_ref) | copy-start | bytes 61444
  8.7 3.9 %collective-permute-start.1 = (bf16[2,80,128]{2,1,0:T(8,128)(2,1)S(1)}, bf16[2,80,128]{2,1,0:T(8,128)(2,1)S(1)}, u32[]{:S(2)}, u32[]{:S(2)}) collective-permute-start(bf16[2,80,128]{2,1,0:T(8,128)(2,1)S(1)} %join.4.after_ref.near_ref), channel_id=1, source_target_pairs={{0,1},{1,0},{2,3},{3,2},{4,5},{5,4},{6,7},{7,6},{8,9},{9,8},{10,11... | collective-permute-start | bytes 122888 | tf_op jit(solution)/shard_map/ppermute | solution.py:470
  12.6 5.3 %copy-start.4 = (s32[64]{0:T(128)S(1)}, s32[64]{0:T(128)}, u32[]{:S(2)}) copy-start(s32[64]{0:T(128)} %param.10) | copy-start | bytes 772
  12.7 5.3 %copy-start.5 = (s32[64]{0:T(128)S(1)}, s32[64]{0:T(128)}, u32[]{:S(2)}) copy-start(s32[64]{0:T(128)} %param.9) | copy-start | bytes 772
  12.7 4.0 %collective-permute-start.2 = (bf16[4,80,128]{2,1,0:T(8,128)(2,1)S(1)}, bf16[4,80,128]{2,1,0:T(8,128)(2,1)S(1)}, u32[]{:S(2)}, u32[]{:S(2)}) collective-permute-start(bf16[4,80,128]{2,1,0:T(8,128)(2,1)S(1)} %join.5.after_ref.near_ref), channel_id=1, source_target_pairs={{0,16},{4,20},{8,24},{12,28},{16,0},{20,4},{24,8},{28,12},{1,17},{... | collective-permute-start | bytes 245768 | tf_op jit(solution)/shard_map/ppermute | solution.py:470
  16.7 4.2 %collective-permute-start.3 = (bf16[8,80,128]{2,1,0:T(8,128)(2,1)S(1)}, bf16[8,80,128]{2,1,0:T(8,128)(2,1)S(1)}, u32[]{:S(2)}, u32[]{:S(2)}) collective-permute-start(bf16[8,80,128]{2,1,0:T(8,128)(2,1)S(1)} %join.6.after_ref.near_ref), channel_id=1, source_target_pairs={{0,8},{4,12},{8,0},{12,4},{16,24},{20,28},{24,16},{28,20},{1,9},{5... | collective-permute-start | bytes 491528 | tf_op jit(solution)/shard_map/ppermute | solution.py:470
  20.9 10.1 %collective-permute-start.4 = (bf16[16,80,128]{2,1,0:T(8,128)(2,1)S(1)}, bf16[16,80,128]{2,1,0:T(8,128)(2,1)S(1)}, u32[]{:S(2)}, u32[]{:S(2)}) collective-permute-start(bf16[16,80,128]{2,1,0:T(8,128)(2,1)S(1)} %join.7.data_ref.near_ref), channel_id=1, source_target_pairs={{0,4},{4,0},{8,12},{12,8},{16,20},{20,16},{24,28},{28,24},{1,5},{5... | collective-permute-start | bytes 983048 | tf_op jit(solution)/shard_map/ppermute | solution.py:470
  25.0 13.0 %copy-start.3 = (s32[64,4]{0,1:T(4,128)S(1)}, s32[64,4]{0,1:T(4,128)}, u32[]{:S(2)}) copy-start(s32[64,4]{0,1:T(4,128)} %param.11) | copy-start | bytes 3076

commit v6 on v5

--- a/solution.py
+++ b/solution.py
@@ -72,7 +72,11 @@
     return jnp.sum(jnp.where(diagonal, row, 0), axis=1, keepdims=True)
 
 
-def pack_kernel(wave_ref, time_ref, station_ref, out_ref, rows_ref):
+def pack_kernel(wave_ref, *refs):
+    small_refs, out_ref, copy_refs, rows_ref = refs[:4], refs[4], refs[5:9], refs[9]
+    for source_ref, copy_ref in zip(small_refs, copy_refs):
+        copy_ref[...] = source_ref[...]
+    time_ref, station_ref = small_refs[:2]
     start = time_ref[...] - HALF
     row = BLOCKS * station_ref[...] + start // LANES
     shift = start % LANES
@@ -89,7 +93,8 @@
     out_ref[0] = rows_ref[...].astype(BF16)
 
 
-def join_kernel(near_ref, other_ref, after_ref, out_ref):
+def join_kernel(near_ref, other_ref, *refs):
+    out_ref = refs[-1]
     half = near_ref.shape[0]
     out_ref[0:half] = near_ref[...]
     out_ref[half:] = other_ref[...]
@@ -109,7 +114,9 @@
     return sum(((away[axis] // mask) & 1) << n for n, (axis, mask) in enumerate(rounds(ngx, ngy)))
 
 
-def tile_kernel(ngx, ngy, tiles_ref, station_ref, sorted_ref, scale_ref, owner_ref):
+def tile_kernel(ngx, ngy, templates_ref, station_ref, sorted_ref, scale_ref, owner_ref, tiles_ref, semaphore):
+    copy = pltpu.make_async_copy(templates_ref, tiles_ref, semaphore)
+    copy.start()
     tpl_dev, k_slots, row_len = tiles_ref.shape
     count = tpl_dev * k_slots
     total = sorted_ref.shape[0]
@@ -128,6 +135,7 @@
     group = st // STATIONS
     place_of = position(ngx, ngy, group // ngy, group % ngy)
     slot = (place_of * STATIONS + st % STATIONS) * SLOTS + rank.astype(jnp.int32)
+    copy.wait()
     tiles = tiles_ref[...].reshape(count, row_len)
     step = 128
     for first in range(0, total, step):
@@ -242,7 +250,7 @@
     lax.fori_loop(0, per_step, body, 0)
 
 
-def correlate_kernel(call, rows_ref, win_ref, taps_ref, scale_ref, high_ref, low_ref, *refs):
+def correlate_kernel(start, rows_ref, win_ref, taps_ref, scale_ref, high_ref, low_ref, *refs):
     x_refs = [[refs[4 * bank + 2 * n : 4 * bank + 2 * n + 2] for n in range(2)] for bank in range(2)]
     groups = rows_ref.shape[0]
     rows = STATIONS * SLOTS
@@ -264,14 +272,14 @@
 
     def store_lags(i, raw):
         g = step * 4 + i
-        scale = scale_ref[pl.ds(pl.multiple_of((call * groups + g) * rows, rows), rows), :]
+        scale = scale_ref[pl.ds(pl.multiple_of((start + g) * rows, rows), rows), :]
         at = pl.ds(pl.multiple_of(g * rows, rows), rows)
         for b in range(FINE):
             value, window = [], []
             for s in range(STATIONS):
                 first = b * rows + s * SLOTS
                 value.append(raw[first : first + SLOTS, s * LANES : (s + 1) * LANES])
-                window.append(jnp.broadcast_to(win_ref[g, s, b : b + 1, :], (SLOTS, LANES)))
+                window.append(win_ref[g, s, pl.ds(b, SLOTS, stride=0), :])
             value = jnp.concatenate(value, axis=0) * scale * jnp.concatenate(window, axis=0)
             high, low = pieces(value, 2)
             high_ref[at, b * LANES : (b + 1) * LANES] = high
@@ -304,11 +312,13 @@
     pl.run_scoped(four_groups, *[pltpu.ACC(n % 2)((height, MXU), F32) for n in range(4)])
 
 
-def stack_kernel(owner_ref, near_high_ref, near_low_ref, far_high_ref, far_low_ref, stack_ref):
-    half = near_high_ref.shape[0]
-    total = 0.0
-    for near, far in ((near_high_ref, far_high_ref), (near_low_ref, far_low_ref)):
-        total = total + dot(owner_ref[:, 0:half], near[...]) + dot(owner_ref[:, half:], far[...])
+def stack_kernel(owner_ref, *refs):
+    stack_ref = refs[-1]
+    total, first = 0.0, 0
+    for high_ref, low_ref in zip(refs[0:-1:2], refs[1:-1:2]):
+        owner = owner_ref[:, first : first + high_ref.shape[0]]
+        total = total + dot(owner, high_ref[...]) + dot(owner, low_ref[...])
+        first += high_ref.shape[0]
     tpl_dev = stack_ref.shape[0]
     block_of = iota((tpl_dev, FINE * LANES), 1) % LANES // COARSE
     place = iota((FINE * LANES, LANES), 0)
@@ -458,12 +468,14 @@
     rows = STATIONS * SLOTS
     total = groups * rows
     time_row, station_row = det_time.reshape(1, det_dev), det_station.reshape(1, det_dev)
-    packed = pl.pallas_call(
+    small = (time_row, station_row, partner.T, tpl_stations.T)
+    packed, time_row, station_row, partners, tile_stations = pl.pallas_call(
         pack_kernel,
-        out_shape=jax.ShapeDtypeStruct((1, PACKED, LANES), BF16),
+        out_shape=(jax.ShapeDtypeStruct((1, PACKED, LANES), BF16),)
+        + tuple(pltpu.VMEM(value.shape, value.dtype) for value in small),
         scratch_shapes=[pltpu.VMEM((PACKED, LANES), F32)],
         name="pack",
-    )(waveforms.transpose(1, 0, 2), time_row, station_row)
+    )(waveforms.transpose(1, 0, 2), *small)
 
     def swap(value, axis, mask):
         size = {"gx": ngx, "gy": ngy}[axis]
@@ -477,9 +489,11 @@
             jax.ShapeDtypeStruct((total, LANES), F32),
             jax.ShapeDtypeStruct((tpl_dev, total), BF16),
         ),
+        in_specs=[after, vmem],
+        scratch_shapes=[pltpu.VMEM(templates.shape, BF16), pltpu.SemaphoreType.DMA],
         compiler_params=pltpu.CompilerParams(vmem_limit_bytes=24 << 20),
         name="tiles",
-    )(templates, tpl_stations.T)
+    )(pltpu.with_memory_space_constraint(templates, pltpu.HBM), tile_stations)
     steps = groups // 4
     height = 4 * FINE * rows
     depth = MXU * PASSES
@@ -521,6 +535,40 @@
             name="own",
         )(packed, time_row, station_row, near)
 
+    def whole(*shape):
+        return pl.BlockSpec(shape, lambda i: (0,) * len(shape))
+
+    params = pltpu.CompilerParams(vmem_limit_bytes=(16 << 20) + groups * (1 << 17))
+
+    def correlate(data, taps, start):
+        count = data.shape[0]
+        sums = (count * rows, FINE * LANES)
+        first = start % half // 4
+        series, win = pl.pallas_call(
+            windows_kernel,
+            out_shape=(
+                jax.ShapeDtypeStruct((count, PACKED, LANES), F32),
+                jax.ShapeDtypeStruct((count, STATIONS, FINE, LANES), F32),
+            ),
+            compiler_params=params,
+            name="windows",
+        )(data)
+        return pl.pallas_call(
+            functools.partial(correlate_kernel, start),
+            grid=(count // 4,),
+            in_specs=[
+                whole(*series.shape),
+                whole(*win.shape),
+                pl.BlockSpec((height, depth), lambda i: (first + i, 0)),
+                whole(*scale.shape),
+            ],
+            out_specs=(whole(*sums), whole(*sums)),
+            out_shape=(jax.ShapeDtypeStruct(sums, BF16),) * 2,
+            scratch_shapes=[pltpu.VMEM((BLOCKS * COARSE, CHANNELS * LANES), BF16)] * 8,
+            compiler_params=params,
+            name="correlate",
+        )(series, win, taps, scale)
+
     near, taps = packed, []
     *first, last = rounds(ngx, ngy)
     for n, (axis, mask) in enumerate(first):
@@ -533,55 +581,24 @@
             beside = taps[-1]
         elif n == len(first) - 1:
             mine, mine_scale = own_detections(near)
-            beside = mine_scale
+            sums = [*correlate(near, taps[0], 0)]
+            beside = sums[0]
         near = pl.pallas_call(
             join_kernel,
             out_shape=jax.ShapeDtypeStruct((2 * near.shape[0], PACKED, LANES), BF16),
-            in_specs=[vmem, vmem, after],
+            in_specs=[vmem, vmem, after, after],
             compiler_params=pltpu.CompilerParams(vmem_limit_bytes=16 << 20),
             name="join",
-        )(near, other, beside)
+        )(near, other, beside, mine_scale if n == len(first) - 1 else beside)
     far = swap(near, *last)
 
-    def whole(*shape):
-        return pl.BlockSpec(shape, lambda i: (0,) * len(shape))
-
-    sums = (half * rows, FINE * LANES)
-    params = pltpu.CompilerParams(vmem_limit_bytes=(16 << 20) + groups * (1 << 17))
-
-    def correlate(call, data):
-        series, win = pl.pallas_call(
-            windows_kernel,
-            out_shape=(
-                jax.ShapeDtypeStruct((half, PACKED, LANES), F32),
-                jax.ShapeDtypeStruct((half, STATIONS, FINE, LANES), F32),
-            ),
-            compiler_params=params,
-            name="windows",
-        )(data)
-        return pl.pallas_call(
-            functools.partial(correlate_kernel, call),
-            grid=(steps // 2,),
-            in_specs=[
-                whole(*series.shape),
-                whole(*win.shape),
-                pl.BlockSpec((height, depth), lambda i: (i, 0)),
-                whole(*scale.shape),
-            ],
-            out_specs=(whole(*sums), whole(*sums)),
-            out_shape=(jax.ShapeDtypeStruct(sums, BF16),) * 2,
-            scratch_shapes=[pltpu.VMEM((BLOCKS * COARSE, CHANNELS * LANES), BF16)] * 8,
-            compiler_params=params,
-            name="correlate",
-        )(series, win, taps[call], scale)
-
-    near_sums, far_sums = correlate(0, near), correlate(1, far)
+    sums += [*correlate(other, taps[0], half // 2), *correlate(far, taps[1], half)]
     stack = pl.pallas_call(
         stack_kernel,
         out_shape=jax.ShapeDtypeStruct((tpl_dev, LAG_BLOCKS * LANES), F32),
         compiler_params=params,
         name="stack",
-    )(owner, *near_sums, *far_sums)
+    )(owner, *sums)
     cuts = pl.pallas_call(
         functools.partial(cuts_kernel, ngx, ngy),
         out_shape=(
@@ -590,7 +607,7 @@
         ),
         compiler_params=params,
         name="cuts",
-    )(near, far, mine_scale, partner.T)
+    )(near, far, mine_scale, partners)
     diff = pl.pallas_call(
         detect_kernel,
         out_shape=jax.ShapeDtypeStruct((4 * det_dev, DTLAG), F32),

time: 46.5 us -> 43.8 us (0.942)
  local copies, waits for them, and re-layouts: 2.56 us -> 0.73 us
  waiting for transfers between devices: 1.57 us -> 0.01 us
  Pallas kernels: 31.2 us -> 32.5 us
  starting transfers between devices: 10 us -> 9.53 us
    unnamed x12 -> x4, local copies, waits for them, and re-layouts: 2.56 us -> 0.73 us
    ppermute x5, waiting for transfers between devices: 1.57 us -> 0.01 us  [swap(): return lax.ppermute(value, axis, [(n, n ^ mask) for n in range(size)])]
    pallas_call x1, Pallas kernels: 0.96 us -> 1.9 us  [on_device(): pl.pallas_call(functools.partial(tile_kernel, ngx, ngy), out_shape=(jax.S...]
    ppermute x5, starting transfers between devices: 10 us -> 9.53 us  [swap(): return lax.ppermute(value, axis, [(n, n ^ mask) for n in range(size)])]
    pallas_call x5 -> x7, Pallas kernels: 15.5 us -> 15.8 us  [the longest x3 12.2 us: correlate(): pl.pallas_call(functools.partial(correlate_kernel, start), grid=(count //...]
  transfers between devices with their start and end apart: 5 -> 5, of which waited for: 1 -> 0; matrix products, arithmetic and copies ran while one was open for 0% -> 0% of each run, Pallas kernels for 32% -> 36%
where the time goes in v6:
time: 43.8 us; the launch traced here: 43.5 us
  Pallas kernels  32.5 us (74%)
  starting transfers between devices  9.53 us (22%)
  between operations  0.79 us (2%)
  local copies, waits for them, and re-layouts  0.73 us (2%)
    pallas_call x3, Pallas kernels, correlate(): pl.pallas_call(functools.partial(correlate_kernel, start), grid=(count //...  12.2 us
    ppermute x5, starting transfers between devices, swap(): return lax.ppermute(value, axis, [(n, n ^ mask) for n in range(size)])  9.53 us
    pallas_call x2, Pallas kernels, shifted(): pl.pallas_call(functools.partial(taps_kernel, lambda: call), in_specs=[vm...  5.27 us
    pallas_call x1, Pallas kernels, on_device(): pl.pallas_call(detect_kernel, out_shape=jax.ShapeDtypeStruct((4 * det_dev...  3.3 us
    pallas_call x1, Pallas kernels, on_device(): pl.pallas_call(functools.partial(cuts_kernel, ngx, ngy), out_shape=(jax.S...  3.29 us
    pallas_call x3, Pallas kernels, correlate(): pl.pallas_call(windows_kernel, out_shape=(jax.ShapeDtypeStruct((count, PA...  2.18 us
    pallas_call x1, Pallas kernels, on_device(): pl.pallas_call(functools.partial(tile_kernel, ngx, ngy), out_shape=(jax.S...  1.9 us
    pallas_call x1, Pallas kernels, on_device(): pl.pallas_call(stack_kernel, out_shape=jax.ShapeDtypeStruct((tpl_dev, LAG...  1.49 us
  transfers between devices with their start and end apart: 5, of which 0 were waited for; matrix products, arithmetic and copies ran while one was open for 0% of the time, Pallas kernels for 36%

profile of v6, /device:TPU:1, one launch (start us, length us, event | category | flops | bytes accessed | tf_op | source)
XLA Modules:
  0.0 43.5 jit_solution(5973947918435646681)
XLA Ops:
  0.6 1.4 %pack.1 = (bf16[1,80,128]{2,1,0:T(8,128)(2,1)}, s32[1,64]{1,0:T(1,128)S(1)}, s32[1,64]{1,0:T(1,128)S(1)}, s32[4,64]{1,0:T(4,128)S(1)}, s32[8,32]{1,0:T(8,128)S(1)}) custom-call(bf16[3,2,1536]{2,1,0:T(2,128)(2,1)} %bitcast.7, s32[1,64]{1,0:T(1,128)} %bitcast.10, s32[1,64]{1,0:T(1,128)} %bitcast.11, s32[4,64]{1,0:T(4,128)} %bitcast.9, s32[8,32]{1,0:T(8,128)} %bitcast.8), custom_call_target="tpu_custom_call" | custom-call | tf_op jit(solution)/shard_map/pack/pallas_call | solution.py:472
  2.0 3.1 %collective-permute-start = (bf16[1,80,128]{2,1,0:T(8,128)(2,1)}, bf16[1,80,128]{2,1,0:T(8,128)(2,1)S(1)}, u32[]{:S(2)}, u32[]{:S(2)}) collective-permute-start(bf16[1,80,128]{2,1,0:T(8,128)(2,1)} %get-tuple-element.28.near_ref.data_ref), channel_id=1, source_target_pairs={{0,2},{1,3},{2,0},{3,1},{4,6},{5,7},{6,4},{7,5},{8,10},{9,11},{10,... | collective-permute-start | bytes 61448 | tf_op jit(solution)/shard_map/ppermute | solution.py:482
  5.2 1.9 %tiles.1 = (bf16[512,1536]{1,0:T(8,128)(2,1)S(1)}, f32[512,128]{1,0:T(8,128)S(1)}, bf16[32,512]{1,0:T(8,128)(2,1)S(1)}) custom-call(bf16[32,8,1536]{2,1,0:T(8,128)(2,1)} %templates_ref.1, s32[8,32]{1,0:T(8,128)S(1)} %get-tuple-element.26.station_ref), custom_call_target="tpu_custom_call" | custom-call | tf_op jit(solution)/shard_map/tiles/pallas_call | solution.py:485
  7.1 0.0 collective-permute-done.other_ref
  7.1 0.0 copy-start
  7.1 0.7 %copy-done = bf16[1,80,128]{2,1,0:T(8,128)(2,1)S(1)} copy-done((bf16[1,80,128]{2,1,0:T(8,128)(2,1)S(1)}, bf16[1,80,128]{2,1,0:T(8,128)(2,1)}, u32[]{:S(2)}) %copy-start) | copy-done | bytes 20504
  7.8 1.3 %collective-permute-start.1 = (bf16[2,80,128]{2,1,0:T(8,128)(2,1)S(1)}, bf16[2,80,128]{2,1,0:T(8,128)(2,1)S(1)}, u32[]{:S(2)}, u32[]{:S(2)}) collective-permute-start(bf16[2,80,128]{2,1,0:T(8,128)(2,1)S(1)} %join.4.after_ref.near_ref), channel_id=1, source_target_pairs={{0,1},{1,0},{2,3},{3,2},{4,5},{5,4},{6,7},{7,6},{8,9},{9,8},{10,11... | collective-permute-start | bytes 122888 | tf_op jit(solution)/shard_map/ppermute | solution.py:482
  9.1 2.6 %taps.2.refs_0_.refs_1_.taps_ref = bf16[2048,2048]{1,0:T(8,128)(2,1)S(1)} custom-call(bf16[512,1536]{1,0:T(8,128)(2,1)S(1)} %get-tuple-element.30.sorted_ref, bf16[2,80,128]{2,1,0:T(8,128)(2,1)S(1)} %join.4.after_ref.near_ref), custom_call_target="tpu_custom_call" | custom-call | tf_op jit(solution)/shard_map/taps/pallas_call | solution.py:504
  11.8 0.0 collective-permute-done.1.other_ref
  11.8 1.3 %collective-permute-start.2 = (bf16[4,80,128]{2,1,0:T(8,128)(2,1)S(1)}, bf16[4,80,128]{2,1,0:T(8,128)(2,1)S(1)}, u32[]{:S(2)}, u32[]{:S(2)}) collective-permute-start(bf16[4,80,128]{2,1,0:T(8,128)(2,1)S(1)} %join.5.after_ref.near_ref), channel_id=1, source_target_pairs={{0,16},{4,20},{8,24},{12,28},{16,0},{20,4},{24,8},{28,12},{1,17},{... | collective-permute-start | bytes 245768 | tf_op jit(solution)/shard_map/ppermute | solution.py:482
  13.1 2.6 %taps.3.refs_0_.refs_1_.taps_ref = bf16[2048,2048]{1,0:T(8,128)(2,1)S(1)} custom-call(bf16[512,1536]{1,0:T(8,128)(2,1)S(1)} %get-tuple-element.30.sorted_ref, bf16[4,80,128]{2,1,0:T(8,128)(2,1)S(1)} %join.5.after_ref.near_ref), custom_call_target="tpu_custom_call" | custom-call | tf_op jit(solution)/shard_map/taps/pallas_call | solution.py:504
  15.7 0.0 collective-permute-done.2.other_ref
  15.8 0.0 copy-start.1
  15.8 1.3 %collective-permute-start.3 = (bf16[8,80,128]{2,1,0:T(8,128)(2,1)S(1)}, bf16[8,80,128]{2,1,0:T(8,128)(2,1)S(1)}, u32[]{:S(2)}, u32[]{:S(2)}) collective-permute-start(bf16[8,80,128]{2,1,0:T(8,128)(2,1)S(1)} %join.6.data_ref.after_ref.near_ref), channel_id=1, source_target_pairs={{0,8},{4,12},{8,0},{12,4},{16,24},{20,28},{24,16},{28,20},{1,9},{5... | collective-permute-start | bytes 491528 | tf_op jit(solution)/shard_map/ppermute | solution.py:482
  17.1 0.5 %windows.3 = (f32[8,80,128]{2,1,0:T(8,128)S(1)}, f32[8,2,8,128]{3,2,1,0:T(8,128)S(1)}) custom-call(bf16[8,80,128]{2,1,0:T(8,128)(2,1)S(1)} %join.6.data_ref.after_ref.near_ref), custom_call_target="tpu_custom_call" | custom-call | tf_op jit(solution)/shard_map/windows/pallas_call | solution.py:547
  17.6 3.1 %correlate.3 = (bf16[128,1024]{1,0:T(8,128)(2,1)S(1)}, bf16[128,1024]{1,0:T(8,128)(2,1)S(1)}) custom-call(f32[8,80,128]{2,1,0:T(8,128)S(1)} %get-tuple-element.31.rows_ref, f32[8,2,8,128]{3,2,1,0:T(8,128)S(1)} %get-tuple-element.32.win_ref, bf16[2048,2048]{1,0:T(8,128)(2,1)S(1)} %taps.2.refs_0_.refs_1_.taps_ref, ...), custom_call_target="tpu_custom_call" | custom-call | tf_op jit(solution)/shard_map/correlate/pallas_call | solution.py:556
  20.7 0.0 copy-done.1
  20.7 1.4 %own.1 = (bf16[4,256,896]{2,1,0:T(8,128)(2,1)S(1)}, f32[64,128]{1,0:T(8,128)S(1)}) custom-call(bf16[1,80,128]{2,1,0:T(8,128)(2,1)S(1)} %copy-done.1, s32[1,64]{1,0:T(1,128)S(1)} %get-tuple-element.39.time_ref, s32[1,64]{1,0:T(1,128)S(1)} %get-tuple-element.40.station_ref, bf16[8,80,128]{2,1,0:T(8,128)(2,1)S(1)} %join.6.data_ref.after_ref.near_ref), custom_call_target="tpu_custom_call" | custom-call | tf_op jit(solution)/shard_map/own/pallas_call | solution.py:527
  22.1 0.0 collective-permute-done.3.data_ref.other_ref
  22.2 2.5 %collective-permute-start.4 = (bf16[16,80,128]{2,1,0:T(8,128)(2,1)S(1)}, bf16[16,80,128]{2,1,0:T(8,128)(2,1)S(1)}, u32[]{:S(2)}, u32[]{:S(2)}) collective-permute-start(bf16[16,80,128]{2,1,0:T(8,128)(2,1)S(1)} %join.7.near_ref), channel_id=1, source_target_pairs={{0,4},{4,0},{8,12},{12,8},{16,20},{20,16},{24,28},{28,24},{1,5},{5... | collective-permute-start | bytes 983048 | tf_op jit(solution)/shard_map/ppermute | solution.py:482
  24.7 0.5 %windows.4 = (f32[8,80,128]{2,1,0:T(8,128)S(1)}, f32[8,2,8,128]{3,2,1,0:T(8,128)S(1)}) custom-call(bf16[8,80,128]{2,1,0:T(8,128)(2,1)S(1)} %collective-permute-done.3.data_ref.other_ref), custom_call_target="tpu_custom_call" | custom-call | tf_op jit(solution)/shard_map/windows/pallas_call | solution.py:547
  25.2 3.1 %correlate.4 = (bf16[128,1024]{1,0:T(8,128)(2,1)S(1)}, bf16[128,1024]{1,0:T(8,128)(2,1)S(1)}) custom-call(f32[8,80,128]{2,1,0:T(8,128)S(1)} %get-tuple-element.35.rows_ref, f32[8,2,8,128]{3,2,1,0:T(8,128)S(1)} %get-tuple-element.36.win_ref, bf16[2048,2048]{1,0:T(8,128)(2,1)S(1)} %taps.2.refs_0_.refs_1_.taps_ref, ...), custom_call_target="tpu_custom_call" | custom-call | tf_op jit(solution)/shard_map/correlate/pallas_call | solution.py:556
  28.3 0.0 collective-permute-done.4.data_ref.far_ref
  28.3 1.1 %windows.5 = (f32[16,80,128]{2,1,0:T(8,128)S(1)}, f32[16,2,8,128]{3,2,1,0:T(8,128)S(1)}) custom-call(bf16[16,80,128]{2,1,0:T(8,128)(2,1)S(1)} %collective-permute-done.4.data_ref.far_ref), custom_call_target="tpu_custom_call" | custom-call | tf_op jit(solution)/shard_map/windows/pallas_call | solution.py:547
  29.4 6.0 %correlate.5 = (bf16[256,1024]{1,0:T(8,128)(2,1)S(1)}, bf16[256,1024]{1,0:T(8,128)(2,1)S(1)}) custom-call(f32[16,80,128]{2,1,0:T(8,128)S(1)} %get-tuple-element.42.rows_ref, f32[16,2,8,128]{3,2,1,0:T(8,128)S(1)} %get-tuple-element.43.win_ref, bf16[2048,2048]{1,0:T(8,128)(2,1)S(1)} %taps.3.refs_0_.refs_1_.taps_ref, ...), custom_call_target="tpu_custom_call" | custom-call | tf_op jit(solution)/shard_map/correlate/pallas_call | solution.py:556
  35.5 3.3 %cuts.1 = (bf16[4,3,3,64,128]{4,3,2,1,0:T(8,128)(2,1)S(1)}, f32[4,64,128]{2,1,0:T(8,128)S(1)}) custom-call(bf16[16,80,128]{2,1,0:T(8,128)(2,1)S(1)} %join.7.near_ref, bf16[16,80,128]{2,1,0:T(8,128)(2,1)S(1)} %collective-permute-done.4.data_ref.far_ref, f32[64,128]{1,0:T(8,128)S(1)} %get-tuple-element.41.refs_1_.scale_ref, ...), custom_call_target="tpu_custom_call" | custom-call | tf_op jit(solution)/shard_map/cuts/pallas_call | solution.py:602
  38.8 3.3 %detect.1 = f32[256,128]{1,0:T(8,128)} custom-call(bf16[4,256,896]{2,1,0:T(8,128)(2,1)S(1)} %get-tuple-element.46.taps_ref, bf16[4,3,3,64,128]{4,3,2,1,0:T(8,128)(2,1)S(1)} %get-tuple-element.48.windows_ref, f32[4,64,128]{2,1,0:T(8,128)S(1)} %get-tuple-element.49.scales_ref), custom_call_target="tpu_custom_call" | custom-call | tf_op jit(solution)/shard_map/detect/pallas_call | solution.py:611
  42.1 1.5 %stack.1 = f32[32,1024]{1,0:T(8,128)} custom-call(bf16[32,512]{1,0:T(8,128)(2,1)S(1)} %get-tuple-element.27.owner_ref, bf16[128,1024]{1,0:T(8,128)(2,1)S(1)} %get-tuple-element.33.refs_0_, bf16[128,1024]{1,0:T(8,128)(2,1)S(1)} %get-tuple-element.34.refs_1_, bf16[128,1024]{1,0:T(8,128)(2,1)S(1)} %get-tuple-element.37.refs_2_, ...), custom_call_target="tpu_custom_call" | custom-call | tf_op jit(solution)/shard_map/stack/pallas_call | solution.py:596
  (4 shorter events, 0.1 us)
Async XLA Ops:
  2.0 5.0 %collective-permute-start = (bf16[1,80,128]{2,1,0:T(8,128)(2,1)}, bf16[1,80,128]{2,1,0:T(8,128)(2,1)S(1)}, u32[]{:S(2)}, u32[]{:S(2)}) collective-permute-start(bf16[1,80,128]{2,1,0:T(8,128)(2,1)} %get-tuple-element.28.near_ref.data_ref), channel_id=1, source_target_pairs={{0,2},{1,3},{2,0},{3,1},{4,6},{5,7},{6,4},{7,5},{8,10},{9,11},{10,... | collective-permute-start | bytes 61448 | tf_op jit(solution)/shard_map/ppermute | solution.py:482
  7.1 0.7 %copy-start = (bf16[1,80,128]{2,1,0:T(8,128)(2,1)S(1)}, bf16[1,80,128]{2,1,0:T(8,128)(2,1)}, u32[]{:S(2)}) copy-start(bf16[1,80,128]{2,1,0:T(8,128)(2,1)} %get-tuple-element.28.near_ref.data_ref) | copy-start | bytes 61444
  7.8 3.9 %collective-permute-start.1 = (bf16[2,80,128]{2,1,0:T(8,128)(2,1)S(1)}, bf16[2,80,128]{2,1,0:T(8,128)(2,1)S(1)}, u32[]{:S(2)}, u32[]{:S(2)}) collective-permute-start(bf16[2,80,128]{2,1,0:T(8,128)(2,1)S(1)} %join.4.after_ref.near_ref), channel_id=1, source_target_pairs={{0,1},{1,0},{2,3},{3,2},{4,5},{5,4},{6,7},{7,6},{8,9},{9,8},{10,11... | collective-permute-start | bytes 122888 | tf_op jit(solution)/shard_map/ppermute | solution.py:482
  11.8 4.0 %collective-permute-start.2 = (bf16[4,80,128]{2,1,0:T(8,128)(2,1)S(1)}, bf16[4,80,128]{2,1,0:T(8,128)(2,1)S(1)}, u32[]{:S(2)}, u32[]{:S(2)}) collective-permute-start(bf16[4,80,128]{2,1,0:T(8,128)(2,1)S(1)} %join.5.after_ref.near_ref), channel_id=1, source_target_pairs={{0,16},{4,20},{8,24},{12,28},{16,0},{20,4},{24,8},{28,12},{1,17},{... | collective-permute-start | bytes 245768 | tf_op jit(solution)/shard_map/ppermute | solution.py:482
  15.8 4.9 %copy-start.1 = (bf16[1,80,128]{2,1,0:T(8,128)(2,1)S(1)}, bf16[1,80,128]{2,1,0:T(8,128)(2,1)}, u32[]{:S(2)}) copy-start(bf16[1,80,128]{2,1,0:T(8,128)(2,1)} %get-tuple-element.28.near_ref.data_ref) | copy-start | bytes 61444
  15.8 6.3 %collective-permute-start.3 = (bf16[8,80,128]{2,1,0:T(8,128)(2,1)S(1)}, bf16[8,80,128]{2,1,0:T(8,128)(2,1)S(1)}, u32[]{:S(2)}, u32[]{:S(2)}) collective-permute-start(bf16[8,80,128]{2,1,0:T(8,128)(2,1)S(1)} %join.6.data_ref.after_ref.near_ref), channel_id=1, source_target_pairs={{0,8},{4,12},{8,0},{12,4},{16,24},{20,28},{24,16},{28,20},{1,9},{5... | collective-permute-start | bytes 491528 | tf_op jit(solution)/shard_map/ppermute | solution.py:482
  22.2 6.2 %collective-permute-start.4 = (bf16[16,80,128]{2,1,0:T(8,128)(2,1)S(1)}, bf16[16,80,128]{2,1,0:T(8,128)(2,1)S(1)}, u32[]{:S(2)}, u32[]{:S(2)}) collective-permute-start(bf16[16,80,128]{2,1,0:T(8,128)(2,1)S(1)} %join.7.near_ref), channel_id=1, source_target_pairs={{0,4},{4,0},{8,12},{12,8},{16,20},{20,16},{24,28},{28,24},{1,5},{5... | collective-permute-start | bytes 983048 | tf_op jit(solution)/shard_map/ppermute | solution.py:482

commit v7 on v6

--- a/solution.py
+++ b/solution.py
@@ -28,7 +28,8 @@
 ROWS = CHANNELS * SPAN
 PACKED = ROWS + 8
 MXU = 256
-PASSES = (CHANNELS * (TAPS + 1) + 1) // 2
+PARTS = [(0, j) for j in range(TAPS + 1)] + [(c, j) for c in (1, 2) for j in range(TAPS)] + [(CHANNELS, 0)]
+PASSES = len(PARTS) // 2
 EPS = 1e-06
 F32 = jnp.float32
 BF16 = jnp.bfloat16
@@ -201,6 +202,13 @@
                 lane < bound, now, later
             )
         now = later
+        rows = slice((block - TAPS) * COARSE, (block - TAPS + 1) * COARSE)
+        if c == 1 and block >= TAPS:
+            out_ref[rows, CHANNELS * LANES :] = later
+        if c == 2 and block >= TAPS:
+            end = [pltpu.roll(row, FINE * first, 1, stride=FINE, stride_axis=0) for first in range(0, COARSE, FINE)]
+            end = jnp.concatenate(end, axis=0).astype(BF16)
+            out_ref[rows, CHANNELS * LANES :] = jnp.where(lane < LANES // 2, out_ref[rows, CHANNELS * LANES :], end)
     out_ref[(BLOCKS - 1) * COARSE : BLOCKS * COARSE, c * LANES : (c + 1) * LANES] = now
 
 
@@ -235,16 +243,27 @@
         at = (first() * per_step + i) * rows
         tiles = sorted_ref[pl.ds(pl.multiple_of(at, rows), rows), :]
         out = out_ref.at[pl.ds(pl.multiple_of(i * height, height), height), :]
-        for c in range(CHANNELS):
-            blocks = [tiles[:, (TAPS * c + j) * LANES : (TAPS * c + j + 1) * LANES] for j in range(TAPS)]
-            for b in range(FINE):
+        for b in range(FINE):
+            place = slice(b * rows, (b + 1) * rows)
+            past = []
+            block = 0
+            for c in range(CHANNELS):
                 before = zero
-                for j in range(TAPS + 1):
-                    moved = rot(blocks[j], b) if j < TAPS else zero
-                    lanes = slice((c * (TAPS + 1) + j) * LANES, (c * (TAPS + 1) + j + 1) * LANES)
-                    out[b * rows : (b + 1) * rows, lanes] = jnp.where(lane < b, before, moved) if b else moved
+                for j in range(TAPS):
+                    tile = tiles[:, (TAPS * c + j) * LANES : (TAPS * c + j + 1) * LANES]
+                    moved = rot(tile, b)
+                    lanes = slice(block * LANES, (block + 1) * LANES)
+                    out[place, lanes] = jnp.where(lane < b, before, moved) if b else moved
                     before = moved
-        out[:, CHANNELS * (TAPS + 1) * LANES :] = jnp.zeros((height, LANES), BF16)
+                    block += 1
+                past.append(jnp.where(lane < b, before, zero) if b else zero)
+                if c == 0:
+                    out[place, block * LANES : (block + 1) * LANES] = past[0]
+                    block += 1
+            if b:
+                end = rot(tile, b - FINE)
+                past[1] = jnp.where((lane >= LANES - FINE) & (lane < LANES - FINE + b), end, past[1])
+            out[place, block * LANES : (block + 1) * LANES] = past[1]
         return carry
 
     lax.fori_loop(0, per_step, body, 0)
@@ -256,8 +275,6 @@
     rows = STATIONS * SLOTS
     height = FINE * rows
     step = pl.program_id(0)
-    parts = [(c, j) for c in range(CHANNELS) for j in range(TAPS + 1)]
-    parts = parts + parts[:1]
 
     def builds(first, bank):
         for n in range(2):
@@ -290,7 +307,7 @@
             for n in range(2):
                 data = [
                     jnp.concatenate(
-                        [ref[j * COARSE : j * COARSE + LANES, c * LANES : (c + 1) * LANES] for c, j in parts[2 * t : 2 * t + 2]],
+                        [ref[j * COARSE : j * COARSE + LANES, c * LANES : (c + 1) * LANES] for c, j in PARTS[2 * t : 2 * t + 2]],
                         axis=1,
                     )
                     for ref in x_refs[bank][n]
@@ -337,7 +354,8 @@
 def cut(data, row, shift, blocks):
     det_dev = row.shape[0]
     row_iota, lane = iota((det_dev, PACKED), 1), iota((det_dev, LANES), 1)
-    picks = [row_iota == row + (SPAN * c + j) for c in range(CHANNELS) for j in range(blocks)]
+    away = row_iota - row
+    picks = [away == SPAN * c + j for c in range(CHANNELS) for j in range(blocks)]
     picks = jnp.concatenate([jnp.where(pick, 1.0, 0.0) for pick in picks], axis=0).astype(BF16)
     found = dot(picks, data).astype(BF16)
     found = [
@@ -384,7 +402,7 @@
     return pieces_of, lax.rsqrt(mean_square(centre) + EPS)
 
 
-def differential(taps_ref, windows, x_ref, parts_ref):
+def differential(taps_ref, windows, x_ref, raw_ref, parts_ref):
     count = len(windows)
     height = count * DET_ROWS
     lane = iota((DET_ROWS, LANES), 1)
@@ -405,17 +423,18 @@
                     for j in range(KEEP):
                         block = jnp.where(lane < LANES - shift, moved[j], moved[j + 1]) if a else moved[j]
                         at = (c * KEEP + j) * LANES
-                        x_ref[out, at : at + LANES] = block
+                        x_ref[q % 2, out, at : at + LANES] = block
                     end = ends[c, a - c] if a >= c else rot(source[c][KEEP], DET_FINE * c - shift)
                     tail = end if tail is None else jnp.where(lane < DET_FINE * c, tail, end)
-                x_ref[out, DET_DEPTH - LANES : DET_DEPTH] = tail
-        raw = dot_nt(x_ref[0 : DET_COARSE * height, :], taps_ref[q])
+                x_ref[q % 2, out, DET_DEPTH - LANES : DET_DEPTH] = tail
+        raw_ref[q] = dot_nt(x_ref[q % 2], taps_ref[q])
+    for q in range(taps_ref.shape[0]):
         for half in range(2):
             for row in range(0, height, 8):
                 upper = row % DET_ROWS // 8
                 total = jnp.zeros((8, LANES), F32)
                 for a in range(DET_COARSE):
-                    part = raw[a * height + row : a * height + row + 8, half * LANES : (half + 1) * LANES]
+                    part = raw_ref[q, a * height + row : a * height + row + 8, half * LANES : (half + 1) * LANES]
                     base = a + 1 if upper else a + LANES - DET_ROWS + 1
                     part = pltpu.roll(part, base, 1, stride=1, stride_axis=0)
                     total = jnp.where(sub_lane == 8 * upper + a, part, total)
@@ -448,9 +467,9 @@
         scales_ref[d] = jnp.where(valid, scale_ref[...] * scale, 0.0)
 
 
-def detect_kernel(taps_ref, windows_ref, scales_ref, diff_ref, x_ref, parts_ref):
+def detect_kernel(taps_ref, windows_ref, scales_ref, diff_ref, x_ref, raw_ref, parts_ref):
     windows = [[[windows_ref[d, c, j] for j in range(KEEP + 1)] for c in range(CHANNELS)] for d in range(4)]
-    out = differential(taps_ref, windows, x_ref, parts_ref)
+    out = differential(taps_ref, windows, x_ref, raw_ref, parts_ref)
     for q in range(taps_ref.shape[0]):
         for d in range(4):
             at = (q * 4 + d) * DET_ROWS
@@ -471,7 +490,7 @@
     small = (time_row, station_row, partner.T, tpl_stations.T)
     packed, time_row, station_row, partners, tile_stations = pl.pallas_call(
         pack_kernel,
-        out_shape=(jax.ShapeDtypeStruct((1, PACKED, LANES), BF16),)
+        out_shape=(pltpu.VMEM((1, PACKED, LANES), BF16),)
         + tuple(pltpu.VMEM(value.shape, value.dtype) for value in small),
         scratch_shapes=[pltpu.VMEM((PACKED, LANES), F32)],
         name="pack",
@@ -564,7 +583,7 @@
             ],
             out_specs=(whole(*sums), whole(*sums)),
             out_shape=(jax.ShapeDtypeStruct(sums, BF16),) * 2,
-            scratch_shapes=[pltpu.VMEM((BLOCKS * COARSE, CHANNELS * LANES), BF16)] * 8,
+            scratch_shapes=[pltpu.VMEM((BLOCKS * COARSE, CHANNELS * LANES + LANES), BF16)] * 8,
             compiler_params=params,
             name="correlate",
         )(series, win, taps, scale)
@@ -573,23 +592,23 @@
     *first, last = rounds(ngx, ngy)
     for n, (axis, mask) in enumerate(first):
         other = swap(near, axis, mask)
-        beside = near
+        beside = (near,)
         if n == 0:
-            beside = scale
+            mine, mine_scale = own_detections(near)
+            beside = (scale, mine_scale)
         elif n <= 2:
             taps.append(shifted(n - 1, near))
-            beside = taps[-1]
+            beside = (taps[-1],)
         elif n == len(first) - 1:
-            mine, mine_scale = own_detections(near)
             sums = [*correlate(near, taps[0], 0)]
-            beside = sums[0]
+            beside = (sums[0],)
         near = pl.pallas_call(
             join_kernel,
             out_shape=jax.ShapeDtypeStruct((2 * near.shape[0], PACKED, LANES), BF16),
-            in_specs=[vmem, vmem, after, after],
+            in_specs=[vmem, vmem] + [after] * len(beside),
             compiler_params=pltpu.CompilerParams(vmem_limit_bytes=16 << 20),
             name="join",
-        )(near, other, beside, mine_scale if n == len(first) - 1 else beside)
+        )(near, other, *beside)
     far = swap(near, *last)
 
     sums += [*correlate(other, taps[0], half // 2), *correlate(far, taps[1], half)]
@@ -612,7 +631,8 @@
         detect_kernel,
         out_shape=jax.ShapeDtypeStruct((4 * det_dev, DTLAG), F32),
         scratch_shapes=[
-            pltpu.VMEM((4 * DET_COARSE * DET_ROWS, DET_DEPTH), BF16),
+            pltpu.VMEM((2, 4 * DET_COARSE * DET_ROWS, DET_DEPTH), BF16),
+            pltpu.VMEM((parts, 4 * DET_COARSE * DET_ROWS, DET_FINE * DET_ROWS), F32),
             pltpu.VMEM((4 * det_dev, DET_FINE * DET_ROWS), F32),
         ],
         compiler_params=params,

time: 43.8 us -> 40.3 us (0.920)
  Pallas kernels: 32.5 us -> 29.7 us
  local copies, waits for them, and re-layouts: 0.73 us -> 0 us
    pallas_call x3, Pallas kernels: 12.2 us -> 11.2 us  [correlate(): pl.pallas_call(functools.partial(correlate_kernel, start), grid=(count //...]
    pallas_call x1, Pallas kernels: 3.29 us -> 2.54 us  [on_device(): pl.pallas_call(functools.partial(cuts_kernel, ngx, ngy), out_shape=(jax.S...]
    unnamed x4 -> x0, local copies, waits for them, and re-layouts: 0.73 us -> none
    pallas_call x1, Pallas kernels: 1.4 us -> 0.8 us  [on_device(): pl.pallas_call(pack_kernel, out_shape=(pltpu.VMEM((1, PACKED, LANES), BF1...]
    pallas_call x1, Pallas kernels: 3.3 us -> 2.75 us  [on_device(): pl.pallas_call(detect_kernel, out_shape=jax.ShapeDtypeStruct((4 * det_dev...]
  transfers between devices with their start and end apart: 5 -> 5, of which waited for: 0 -> 0; matrix products, arithmetic and copies ran while one was open for 0% -> 0% of each run, Pallas kernels for 36% -> 39%
where the time goes in v7:
time: 40.3 us; the launch traced here: 40.1 us
  Pallas kernels  29.7 us (74%)
  starting transfers between devices  9.57 us (24%)
  between operations  0.77 us (2%)
    pallas_call x3, Pallas kernels, correlate(): pl.pallas_call(functools.partial(correlate_kernel, start), grid=(count //...  11.2 us
    ppermute x5, starting transfers between devices, swap(): return lax.ppermute(value, axis, [(n, n ^ mask) for n in range(size)])  9.57 us
    pallas_call x2, Pallas kernels, shifted(): pl.pallas_call(functools.partial(taps_kernel, lambda: call), in_specs=[vm...  5.45 us
    pallas_call x1, Pallas kernels, on_device(): pl.pallas_call(detect_kernel, out_shape=jax.ShapeDtypeStruct((4 * det_dev...  2.75 us
    pallas_call x1, Pallas kernels, on_device(): pl.pallas_call(functools.partial(cuts_kernel, ngx, ngy), out_shape=(jax.S...  2.54 us
    pallas_call x3, Pallas kernels, correlate(): pl.pallas_call(windows_kernel, out_shape=(jax.ShapeDtypeStruct((count, PA...  2.19 us
    pallas_call x1, Pallas kernels, on_device(): pl.pallas_call(functools.partial(tile_kernel, ngx, ngy), out_shape=(jax.S...  1.9 us
    pallas_call x1, Pallas kernels, on_device(): pl.pallas_call(stack_kernel, out_shape=jax.ShapeDtypeStruct((tpl_dev, LAG...  1.5 us
  transfers between devices with their start and end apart: 5, of which 0 were waited for; matrix products, arithmetic and copies ran while one was open for 0% of the time, Pallas kernels for 39%

profile of v7, /device:TPU:1, one launch (start us, length us, event | category | flops | bytes accessed | tf_op | source)
XLA Modules:
  0.0 40.1 jit_solution(9592290158704908023)
XLA Ops:
  0.6 0.8 %pack.1 = (bf16[1,80,128]{2,1,0:T(8,128)(2,1)S(1)}, s32[1,64]{1,0:T(1,128)S(1)}, s32[1,64]{1,0:T(1,128)S(1)}, s32[4,64]{1,0:T(4,128)S(1)}, s32[8,32]{1,0:T(8,128)S(1)}) custom-call(bf16[3,2,1536]{2,1,0:T(2,128)(2,1)} %bitcast.7, s32[1,64]{1,0:T(1,128)} %bitcast.10, s32[1,64]{1,0:T(1,128)} %bitcast.11, s32[4,64]{1,0:T(4,128)} %bitcast.9, s32[8,32]{1,0:T(8,128)} %bitcast.8), custom_call_target="tpu_custom_call" | custom-call | tf_op jit(solution)/shard_map/pack/pallas_call | solution.py:491
  1.4 3.2 %collective-permute-start = (bf16[1,80,128]{2,1,0:T(8,128)(2,1)S(1)}, bf16[1,80,128]{2,1,0:T(8,128)(2,1)S(1)}, u32[]{:S(2)}, u32[]{:S(2)}) collective-permute-start(bf16[1,80,128]{2,1,0:T(8,128)(2,1)S(1)} %get-tuple-element.28.data_ref.after_ref.near_ref), channel_id=1, source_target_pairs={{0,2},{1,3},{2,0},{3,1},{4,6},{5,7},{6,4},{7,5},{8,10},{9,11},{10,... | collective-permute-start | bytes 61448 | tf_op jit(solution)/shard_map/ppermute | solution.py:501
  4.6 1.9 %tiles.1 = (bf16[512,1536]{1,0:T(8,128)(2,1)S(1)}, f32[512,128]{1,0:T(8,128)S(1)}, bf16[32,512]{1,0:T(8,128)(2,1)S(1)}) custom-call(bf16[32,8,1536]{2,1,0:T(8,128)(2,1)} %templates_ref.1, s32[8,32]{1,0:T(8,128)S(1)} %get-tuple-element.26.station_ref), custom_call_target="tpu_custom_call" | custom-call | tf_op jit(solution)/shard_map/tiles/pallas_call | solution.py:504
  6.5 1.4 %own.1 = (bf16[4,256,896]{2,1,0:T(8,128)(2,1)S(1)}, f32[64,128]{1,0:T(8,128)S(1)}) custom-call(bf16[1,80,128]{2,1,0:T(8,128)(2,1)S(1)} %get-tuple-element.28.data_ref.after_ref.near_ref, s32[1,64]{1,0:T(1,128)S(1)} %get-tuple-element.30.time_ref, s32[1,64]{1,0:T(1,128)S(1)} %get-tuple-element.31.station_ref, ...), custom_call_target="tpu_custom_call" | custom-call | tf_op jit(solution)/shard_map/own/pallas_call | solution.py:546
  7.9 0.0 collective-permute-done.other_ref
  8.0 1.4 %collective-permute-start.1 = (bf16[2,80,128]{2,1,0:T(8,128)(2,1)S(1)}, bf16[2,80,128]{2,1,0:T(8,128)(2,1)S(1)}, u32[]{:S(2)}, u32[]{:S(2)}) collective-permute-start(bf16[2,80,128]{2,1,0:T(8,128)(2,1)S(1)} %join.4.after_ref.near_ref), channel_id=1, source_target_pairs={{0,1},{1,0},{2,3},{3,2},{4,5},{5,4},{6,7},{7,6},{8,9},{9,8},{10,11... | collective-permute-start | bytes 122888 | tf_op jit(solution)/shard_map/ppermute | solution.py:501
  9.3 2.7 %taps.2.refs_0_.taps_ref = bf16[2048,1792]{1,0:T(8,128)(2,1)S(1)} custom-call(bf16[512,1536]{1,0:T(8,128)(2,1)S(1)} %get-tuple-element.33.sorted_ref, bf16[2,80,128]{2,1,0:T(8,128)(2,1)S(1)} %join.4.after_ref.near_ref), custom_call_target="tpu_custom_call" | custom-call | tf_op jit(solution)/shard_map/taps/pallas_call | solution.py:523
  12.0 0.0 collective-permute-done.1.other_ref
  12.1 1.3 %collective-permute-start.2 = (bf16[4,80,128]{2,1,0:T(8,128)(2,1)S(1)}, bf16[4,80,128]{2,1,0:T(8,128)(2,1)S(1)}, u32[]{:S(2)}, u32[]{:S(2)}) collective-permute-start(bf16[4,80,128]{2,1,0:T(8,128)(2,1)S(1)} %join.5.after_ref.near_ref), channel_id=1, source_target_pairs={{0,16},{4,20},{8,24},{12,28},{16,0},{20,4},{24,8},{28,12},{1,17},{... | collective-permute-start | bytes 245768 | tf_op jit(solution)/shard_map/ppermute | solution.py:501
  13.4 2.7 %taps.3.refs_0_.taps_ref = bf16[2048,1792]{1,0:T(8,128)(2,1)S(1)} custom-call(bf16[512,1536]{1,0:T(8,128)(2,1)S(1)} %get-tuple-element.33.sorted_ref, bf16[4,80,128]{2,1,0:T(8,128)(2,1)S(1)} %join.5.after_ref.near_ref), custom_call_target="tpu_custom_call" | custom-call | tf_op jit(solution)/shard_map/taps/pallas_call | solution.py:523
  16.1 0.0 collective-permute-done.2.other_ref
  16.1 1.3 %collective-permute-start.3 = (bf16[8,80,128]{2,1,0:T(8,128)(2,1)S(1)}, bf16[8,80,128]{2,1,0:T(8,128)(2,1)S(1)}, u32[]{:S(2)}, u32[]{:S(2)}) collective-permute-start(bf16[8,80,128]{2,1,0:T(8,128)(2,1)S(1)} %join.6.data_ref.near_ref), channel_id=1, source_target_pairs={{0,8},{4,12},{8,0},{12,4},{16,24},{20,28},{24,16},{28,20},{1,9},{5... | collective-permute-start | bytes 491528 | tf_op jit(solution)/shard_map/ppermute | solution.py:501
  17.4 0.5 %windows.3 = (f32[8,80,128]{2,1,0:T(8,128)S(1)}, f32[8,2,8,128]{3,2,1,0:T(8,128)S(1)}) custom-call(bf16[8,80,128]{2,1,0:T(8,128)(2,1)S(1)} %join.6.data_ref.near_ref), custom_call_target="tpu_custom_call" | custom-call | tf_op jit(solution)/shard_map/windows/pallas_call | solution.py:566
  18.0 2.9 %correlate.3 = (bf16[128,1024]{1,0:T(8,128)(2,1)S(1)}, bf16[128,1024]{1,0:T(8,128)(2,1)S(1)}) custom-call(f32[8,80,128]{2,1,0:T(8,128)S(1)} %get-tuple-element.34.rows_ref, f32[8,2,8,128]{3,2,1,0:T(8,128)S(1)} %get-tuple-element.35.win_ref, bf16[2048,1792]{1,0:T(8,128)(2,1)S(1)} %taps.2.refs_0_.taps_ref, f32[512,128]{1,0:T(8,128)S(1)} %get-tuple-element.29.refs_0_.scale_ref), custom_call_target="tpu_custom_call" | custom-call | tf_op jit(solution)/shard_map/correlate/pallas_call | solution.py:575
  20.8 0.0 collective-permute-done.3.data_ref.other_ref
  20.9 2.4 %collective-permute-start.4 = (bf16[16,80,128]{2,1,0:T(8,128)(2,1)S(1)}, bf16[16,80,128]{2,1,0:T(8,128)(2,1)S(1)}, u32[]{:S(2)}, u32[]{:S(2)}) collective-permute-start(bf16[16,80,128]{2,1,0:T(8,128)(2,1)S(1)} %join.7.near_ref), channel_id=1, source_target_pairs={{0,4},{4,0},{8,12},{12,8},{16,20},{20,16},{24,28},{28,24},{1,5},{5... | collective-permute-start | bytes 983048 | tf_op jit(solution)/shard_map/ppermute | solution.py:501
  23.3 0.5 %windows.4 = (f32[8,80,128]{2,1,0:T(8,128)S(1)}, f32[8,2,8,128]{3,2,1,0:T(8,128)S(1)}) custom-call(bf16[8,80,128]{2,1,0:T(8,128)(2,1)S(1)} %collective-permute-done.3.data_ref.other_ref), custom_call_target="tpu_custom_call" | custom-call | tf_op jit(solution)/shard_map/windows/pallas_call | solution.py:566
  23.8 2.9 %correlate.4 = (bf16[128,1024]{1,0:T(8,128)(2,1)S(1)}, bf16[128,1024]{1,0:T(8,128)(2,1)S(1)}) custom-call(f32[8,80,128]{2,1,0:T(8,128)S(1)} %get-tuple-element.38.rows_ref, f32[8,2,8,128]{3,2,1,0:T(8,128)S(1)} %get-tuple-element.39.win_ref, bf16[2048,1792]{1,0:T(8,128)(2,1)S(1)} %taps.2.refs_0_.taps_ref, f32[512,128]{1,0:T(8,128)S(1)} %get-tuple-element.29.refs_0_.scale_ref), custom_call_target="tpu_custom_call" | custom-call | tf_op jit(solution)/shard_map/correlate/pallas_call | solution.py:575
  26.7 0.0 collective-permute-done.4.data_ref.far_ref
  26.7 1.1 %windows.5 = (f32[16,80,128]{2,1,0:T(8,128)S(1)}, f32[16,2,8,128]{3,2,1,0:T(8,128)S(1)}) custom-call(bf16[16,80,128]{2,1,0:T(8,128)(2,1)S(1)} %collective-permute-done.4.data_ref.far_ref), custom_call_target="tpu_custom_call" | custom-call | tf_op jit(solution)/shard_map/windows/pallas_call | solution.py:566
  27.8 5.4 %correlate.5 = (bf16[256,1024]{1,0:T(8,128)(2,1)S(1)}, bf16[256,1024]{1,0:T(8,128)(2,1)S(1)}) custom-call(f32[16,80,128]{2,1,0:T(8,128)S(1)} %get-tuple-element.42.rows_ref, f32[16,2,8,128]{3,2,1,0:T(8,128)S(1)} %get-tuple-element.43.win_ref, bf16[2048,1792]{1,0:T(8,128)(2,1)S(1)} %taps.3.refs_0_.taps_ref, f32[512,128]{1,0:T(8,128)S(1)} %get-tuple-element.29.refs_0_.scale_ref), custom_call_target="tpu_custom_call" | custom-call | tf_op jit(solution)/shard_map/correlate/pallas_call | solution.py:575
  33.3 2.5 %cuts.1 = (bf16[4,3,3,64,128]{4,3,2,1,0:T(8,128)(2,1)S(1)}, f32[4,64,128]{2,1,0:T(8,128)S(1)}) custom-call(bf16[16,80,128]{2,1,0:T(8,128)(2,1)S(1)} %join.7.near_ref, bf16[16,80,128]{2,1,0:T(8,128)(2,1)S(1)} %collective-permute-done.4.data_ref.far_ref, f32[64,128]{1,0:T(8,128)S(1)} %get-tuple-element.32.refs_1_.scale_ref, ...), custom_call_target="tpu_custom_call" | custom-call | tf_op jit(solution)/shard_map/cuts/pallas_call | solution.py:621
  35.8 2.7 %detect.1 = f32[256,128]{1,0:T(8,128)} custom-call(bf16[4,256,896]{2,1,0:T(8,128)(2,1)S(1)} %get-tuple-element.46.taps_ref, bf16[4,3,3,64,128]{4,3,2,1,0:T(8,128)(2,1)S(1)} %get-tuple-element.48.windows_ref, f32[4,64,128]{2,1,0:T(8,128)S(1)} %get-tuple-element.49.scales_ref), custom_call_target="tpu_custom_call" | custom-call | tf_op jit(solution)/shard_map/detect/pallas_call | solution.py:630
  38.6 1.5 %stack.1 = f32[32,1024]{1,0:T(8,128)} custom-call(bf16[32,512]{1,0:T(8,128)(2,1)S(1)} %get-tuple-element.27.owner_ref, bf16[128,1024]{1,0:T(8,128)(2,1)S(1)} %get-tuple-element.36.refs_0_, bf16[128,1024]{1,0:T(8,128)(2,1)S(1)} %get-tuple-element.37.refs_1_, bf16[128,1024]{1,0:T(8,128)(2,1)S(1)} %get-tuple-element.40.refs_2_, ...), custom_call_target="tpu_custom_call" | custom-call | tf_op jit(solution)/shard_map/stack/pallas_call | solution.py:615
  (4 shorter events, 0.1 us)
Async XLA Ops:
  1.4 6.5 %collective-permute-start = (bf16[1,80,128]{2,1,0:T(8,128)(2,1)S(1)}, bf16[1,80,128]{2,1,0:T(8,128)(2,1)S(1)}, u32[]{:S(2)}, u32[]{:S(2)}) collective-permute-start(bf16[1,80,128]{2,1,0:T(8,128)(2,1)S(1)} %get-tuple-element.28.data_ref.after_ref.near_ref), channel_id=1, source_target_pairs={{0,2},{1,3},{2,0},{3,1},{4,6},{5,7},{6,4},{7,5},{8,10},{9,11},{10,... | collective-permute-start | bytes 61448 | tf_op jit(solution)/shard_map/ppermute | solution.py:501
  8.0 4.1 %collective-permute-start.1 = (bf16[2,80,128]{2,1,0:T(8,128)(2,1)S(1)}, bf16[2,80,128]{2,1,0:T(8,128)(2,1)S(1)}, u32[]{:S(2)}, u32[]{:S(2)}) collective-permute-start(bf16[2,80,128]{2,1,0:T(8,128)(2,1)S(1)} %join.4.after_ref.near_ref), channel_id=1, source_target_pairs={{0,1},{1,0},{2,3},{3,2},{4,5},{5,4},{6,7},{7,6},{8,9},{9,8},{10,11... | collective-permute-start | bytes 122888 | tf_op jit(solution)/shard_map/ppermute | solution.py:501
  12.1 4.0 %collective-permute-start.2 = (bf16[4,80,128]{2,1,0:T(8,128)(2,1)S(1)}, bf16[4,80,128]{2,1,0:T(8,128)(2,1)S(1)}, u32[]{:S(2)}, u32[]{:S(2)}) collective-permute-start(bf16[4,80,128]{2,1,0:T(8,128)(2,1)S(1)} %join.5.after_ref.near_ref), channel_id=1, source_target_pairs={{0,16},{4,20},{8,24},{12,28},{16,0},{20,4},{24,8},{28,12},{1,17},{... | collective-permute-start | bytes 245768 | tf_op jit(solution)/shard_map/ppermute | solution.py:501
  16.1 4.7 %collective-permute-start.3 = (bf16[8,80,128]{2,1,0:T(8,128)(2,1)S(1)}, bf16[8,80,128]{2,1,0:T(8,128)(2,1)S(1)}, u32[]{:S(2)}, u32[]{:S(2)}) collective-permute-start(bf16[8,80,128]{2,1,0:T(8,128)(2,1)S(1)} %join.6.data_ref.near_ref), channel_id=1, source_target_pairs={{0,8},{4,12},{8,0},{12,4},{16,24},{20,28},{24,16},{28,20},{1,9},{5... | collective-permute-start | bytes 491528 | tf_op jit(solution)/shard_map/ppermute | solution.py:501
  20.9 5.8 %collective-permute-start.4 = (bf16[16,80,128]{2,1,0:T(8,128)(2,1)S(1)}, bf16[16,80,128]{2,1,0:T(8,128)(2,1)S(1)}, u32[]{:S(2)}, u32[]{:S(2)}) collective-permute-start(bf16[16,80,128]{2,1,0:T(8,128)(2,1)S(1)} %join.7.near_ref), channel_id=1, source_target_pairs={{0,4},{4,0},{8,12},{12,8},{16,20},{20,16},{24,28},{28,24},{1,5},{5... | collective-permute-start | bytes 983048 | tf_op jit(solution)/shard_map/ppermute | solution.py:501

commit v8 on v7

--- a/solution.py
+++ b/solution.py
@@ -151,7 +151,7 @@
 
 def windows_kernel(data_ref, rows_ref, win_ref):
     groups = data_ref.shape[0]
-    step = min(8, groups)
+    step = min(16, groups)
     column_of = iota((LANES, LANES), 1)
     sample = FINE * (COARSE - 1 - column_of % COARSE) + column_of // COARSE
     row = iota((LANES, LANES), 0)
@@ -162,7 +162,9 @@
         x = data_ref[pl.ds(q * step, step)].astype(F32)
         rows_ref[pl.ds(q * step, step)] = x
         energy = sum(x[:, SPAN * c : SPAN * (c + 1)] * x[:, SPAN * c : SPAN * (c + 1)] for c in range(CHANNELS))
-        sums = sum(dot(part, sums_of) for part in pieces(energy.reshape(step * SPAN, LANES), 3))
+        count = step * SPAN
+        sums = dot(jnp.concatenate(pieces(energy.reshape(count, LANES), 3), axis=0), sums_of)
+        sums = sums[0:count] + sums[count : 2 * count] + sums[2 * count :]
         sums = sums.reshape(step, SPAN, 3 * LANES)
         for s in range(STATIONS):
             at = BLOCKS * s
@@ -453,29 +455,37 @@
         build_taps(blocks, DET_FINE, DET_ROWS, taps_ref.at[q], 0, DET_ROWS)
 
 
-def cuts_kernel(ngx, ngy, near_ref, far_ref, scale_ref, partner_ref, windows_ref, scales_ref):
+MOVES = ((1, 0), (-1, 0), (0, 1), (0, -1))
+
+
+def cuts_kernel(ngx, ngy, directions, data_ref, scale_ref, partner_ref, *refs):
+    windows_ref, scales_ref = refs[-2:]
     gx, gy = lax.axis_index("gx"), lax.axis_index("gy")
-    for d, (dx, dy) in enumerate(((1, 0), (-1, 0), (0, 1), (0, -1))):
-        x, y = gx + dx, gy + dy
+    for n, d in enumerate(directions):
+        x, y = gx + MOVES[d][0], gy + MOVES[d][1]
         valid = (x >= 0) & (x < ngx) & (y >= 0) & (y < ngy)
-        at = position(ngx, ngy, jnp.clip(x, 0, ngx - 1), jnp.clip(y, 0, ngy - 1)) % near_ref.shape[0]
-        data = (far_ref if dx else near_ref)[at]
-        found, scale = partner_windows(data, partner_ref[d : d + 1, :])
+        at = position(ngx, ngy, jnp.clip(x, 0, ngx - 1), jnp.clip(y, 0, ngy - 1)) % data_ref.shape[0]
+        found, scale = partner_windows(data_ref[at], partner_ref[d : d + 1, :])
         for c in range(CHANNELS):
             for j in range(KEEP + 1):
-                windows_ref[d, c, j] = found[c][j]
-        scales_ref[d] = jnp.where(valid, scale_ref[...] * scale, 0.0)
-
-
-def detect_kernel(taps_ref, windows_ref, scales_ref, diff_ref, x_ref, raw_ref, parts_ref):
-    windows = [[[windows_ref[d, c, j] for j in range(KEEP + 1)] for c in range(CHANNELS)] for d in range(4)]
+                windows_ref[n, c, j] = found[c][j]
+        scales_ref[n] = jnp.where(valid, scale_ref[...] * scale, 0.0)
+
+
+def detect_kernel(taps_ref, *refs):
+    cuts, (diff_ref, x_ref, raw_ref, parts_ref) = refs[:4], refs[4:]
+    windows, scales = [], []
+    for windows_ref, scales_ref in (cuts[0:2], cuts[2:4]):
+        for n in range(2):
+            windows.append([[windows_ref[n, c, j] for j in range(KEEP + 1)] for c in range(CHANNELS)])
+            scales.append(scales_ref.at[n])
     out = differential(taps_ref, windows, x_ref, raw_ref, parts_ref)
     for q in range(taps_ref.shape[0]):
         for d in range(4):
             at = (q * 4 + d) * DET_ROWS
             rows = slice(q * DET_ROWS, (q + 1) * DET_ROWS)
             diff_ref[pl.ds(q * DET_ROWS * 4 + d, DET_ROWS, stride=4), :] = (
-                out[at : at + DET_ROWS] * scales_ref[d, rows, :]
+                out[at : at + DET_ROWS] * scales[d][rows, :]
             )
 
 
@@ -588,6 +598,18 @@
             name="correlate",
         )(series, win, taps, scale)
 
+    def cut_windows(directions, data):
+        count = len(directions)
+        return pl.pallas_call(
+            functools.partial(cuts_kernel, ngx, ngy, directions),
+            out_shape=(
+                jax.ShapeDtypeStruct((count, CHANNELS, KEEP + 1, det_dev, LANES), BF16),
+                jax.ShapeDtypeStruct((count, det_dev, LANES), F32),
+            ),
+            compiler_params=params,
+            name="cuts",
+        )(data, mine_scale, partners)
+
     near, taps = packed, []
     *first, last = rounds(ngx, ngy)
     for n, (axis, mask) in enumerate(first):
@@ -601,7 +623,8 @@
             beside = (taps[-1],)
         elif n == len(first) - 1:
             sums = [*correlate(near, taps[0], 0)]
-            beside = (sums[0],)
+            near_cuts = cut_windows((2, 3), near)
+            beside = (sums[0], near_cuts[0])
         near = pl.pallas_call(
             join_kernel,
             out_shape=jax.ShapeDtypeStruct((2 * near.shape[0], PACKED, LANES), BF16),
@@ -618,15 +641,7 @@
         compiler_params=params,
         name="stack",
     )(owner, *sums)
-    cuts = pl.pallas_call(
-        functools.partial(cuts_kernel, ngx, ngy),
-        out_shape=(
-            jax.ShapeDtypeStruct((4, CHANNELS, KEEP + 1, det_dev, LANES), BF16),
-            jax.ShapeDtypeStruct((4, det_dev, LANES), F32),
-        ),
-        compiler_params=params,
-        name="cuts",
-    )(near, far, mine_scale, partners)
+    far_cuts = cut_windows((0, 1), far)
     diff = pl.pallas_call(
         detect_kernel,
         out_shape=jax.ShapeDtypeStruct((4 * det_dev, DTLAG), F32),
@@ -637,7 +652,7 @@
         ],
         compiler_params=params,
         name="detect",
-    )(mine, *cuts)
+    )(mine, *far_cuts, *near_cuts)
     return stack, diff.reshape(det_dev, 4, DTLAG)
 
 

time: 40.3 us -> 39.7 us (0.985)
    pallas_call x1 -> x2, Pallas kernels: 2.54 us -> 2.73 us  [cut_windows(): pl.pallas_call(functools.partial(cuts_kernel, ngx, ngy, directions), out_...]
  transfers between devices with their start and end apart: 5 -> 5, of which waited for: 0 -> 0; matrix products, arithmetic and copies ran while one was open for 0% -> 0% of each run, Pallas kernels for 39% -> 43%
where the time goes in v8:
time: 39.7 us; the launch traced here: 39.5 us
  Pallas kernels  29.5 us (74%)
  starting transfers between devices  9.17 us (23%)
  between operations  0.78 us (2%)
    pallas_call x3, Pallas kernels, correlate(): pl.pallas_call(functools.partial(correlate_kernel, start), grid=(count //...  11.2 us
    ppermute x5, starting transfers between devices, swap(): return lax.ppermute(value, axis, [(n, n ^ mask) for n in range(size)])  9.17 us
    pallas_call x2, Pallas kernels, shifted(): pl.pallas_call(functools.partial(taps_kernel, lambda: call), in_specs=[vm...  5.45 us
    pallas_call x1, Pallas kernels, on_device(): pl.pallas_call(detect_kernel, out_shape=jax.ShapeDtypeStruct((4 * det_dev...  2.74 us
    pallas_call x2, Pallas kernels, cut_windows(): pl.pallas_call(functools.partial(cuts_kernel, ngx, ngy, directions), out_...  2.73 us
    pallas_call x1, Pallas kernels, on_device(): pl.pallas_call(functools.partial(tile_kernel, ngx, ngy), out_shape=(jax.S...  1.9 us
    pallas_call x3, Pallas kernels, correlate(): pl.pallas_call(windows_kernel, out_shape=(jax.ShapeDtypeStruct((count, PA...  1.79 us
    pallas_call x1, Pallas kernels, on_device(): pl.pallas_call(stack_kernel, out_shape=jax.ShapeDtypeStruct((tpl_dev, LAG...  1.5 us
  transfers between devices with their start and end apart: 5, of which 0 were waited for; matrix products, arithmetic and copies ran while one was open for 0% of the time, Pallas kernels for 43%

profile of v8, /device:TPU:1, one launch (start us, length us, event | category | flops | bytes accessed | tf_op | source)
XLA Modules:
  0.0 39.5 jit_solution(18399964411440330281)
XLA Ops:
  0.6 0.8 %pack.1 = (bf16[1,80,128]{2,1,0:T(8,128)(2,1)S(1)}, s32[1,64]{1,0:T(1,128)S(1)}, s32[1,64]{1,0:T(1,128)S(1)}, s32[4,64]{1,0:T(4,128)S(1)}, s32[8,32]{1,0:T(8,128)S(1)}) custom-call(bf16[3,2,1536]{2,1,0:T(2,128)(2,1)} %bitcast.7, s32[1,64]{1,0:T(1,128)} %bitcast.10, s32[1,64]{1,0:T(1,128)} %bitcast.11, s32[4,64]{1,0:T(4,128)} %bitcast.9, s32[8,32]{1,0:T(8,128)} %bitcast.8), custom_call_target="tpu_custom_call" | custom-call | tf_op jit(solution)/shard_map/pack/pallas_call | solution.py:501
  1.4 3.2 %collective-permute-start = (bf16[1,80,128]{2,1,0:T(8,128)(2,1)S(1)}, bf16[1,80,128]{2,1,0:T(8,128)(2,1)S(1)}, u32[]{:S(2)}, u32[]{:S(2)}) collective-permute-start(bf16[1,80,128]{2,1,0:T(8,128)(2,1)S(1)} %get-tuple-element.30.data_ref.after_ref.near_ref), channel_id=1, source_target_pairs={{0,2},{1,3},{2,0},{3,1},{4,6},{5,7},{6,4},{7,5},{8,10},{9,11},{10,... | collective-permute-start | bytes 61448 | tf_op jit(solution)/shard_map/ppermute | solution.py:511
  4.6 1.9 %tiles.1 = (bf16[512,1536]{1,0:T(8,128)(2,1)S(1)}, f32[512,128]{1,0:T(8,128)S(1)}, bf16[32,512]{1,0:T(8,128)(2,1)S(1)}) custom-call(bf16[32,8,1536]{2,1,0:T(8,128)(2,1)} %templates_ref.1, s32[8,32]{1,0:T(8,128)S(1)} %get-tuple-element.28.station_ref), custom_call_target="tpu_custom_call" | custom-call | tf_op jit(solution)/shard_map/tiles/pallas_call | solution.py:514
  6.5 1.4 %own.1 = (bf16[4,256,896]{2,1,0:T(8,128)(2,1)S(1)}, f32[64,128]{1,0:T(8,128)S(1)}) custom-call(bf16[1,80,128]{2,1,0:T(8,128)(2,1)S(1)} %get-tuple-element.30.data_ref.after_ref.near_ref, s32[1,64]{1,0:T(1,128)S(1)} %get-tuple-element.32.time_ref, s32[1,64]{1,0:T(1,128)S(1)} %get-tuple-element.33.station_ref, ...), custom_call_target="tpu_custom_call" | custom-call | tf_op jit(solution)/shard_map/own/pallas_call | solution.py:556
  7.9 0.0 collective-permute-done.other_ref
  8.0 1.4 %collective-permute-start.1 = (bf16[2,80,128]{2,1,0:T(8,128)(2,1)S(1)}, bf16[2,80,128]{2,1,0:T(8,128)(2,1)S(1)}, u32[]{:S(2)}, u32[]{:S(2)}) collective-permute-start(bf16[2,80,128]{2,1,0:T(8,128)(2,1)S(1)} %join.4.after_ref.near_ref), channel_id=1, source_target_pairs={{0,1},{1,0},{2,3},{3,2},{4,5},{5,4},{6,7},{7,6},{8,9},{9,8},{10,11... | collective-permute-start | bytes 122888 | tf_op jit(solution)/shard_map/ppermute | solution.py:511
  9.3 2.7 %taps.2.refs_0_.taps_ref = bf16[2048,1792]{1,0:T(8,128)(2,1)S(1)} custom-call(bf16[512,1536]{1,0:T(8,128)(2,1)S(1)} %get-tuple-element.35.sorted_ref, bf16[2,80,128]{2,1,0:T(8,128)(2,1)S(1)} %join.4.after_ref.near_ref), custom_call_target="tpu_custom_call" | custom-call | tf_op jit(solution)/shard_map/taps/pallas_call | solution.py:533
  12.0 0.0 collective-permute-done.1.other_ref
  12.1 1.3 %collective-permute-start.2 = (bf16[4,80,128]{2,1,0:T(8,128)(2,1)S(1)}, bf16[4,80,128]{2,1,0:T(8,128)(2,1)S(1)}, u32[]{:S(2)}, u32[]{:S(2)}) collective-permute-start(bf16[4,80,128]{2,1,0:T(8,128)(2,1)S(1)} %join.5.after_ref.near_ref), channel_id=1, source_target_pairs={{0,16},{4,20},{8,24},{12,28},{16,0},{20,4},{24,8},{28,12},{1,17},{... | collective-permute-start | bytes 245768 | tf_op jit(solution)/shard_map/ppermute | solution.py:511
  13.4 2.7 %taps.3.refs_0_.taps_ref = bf16[2048,1792]{1,0:T(8,128)(2,1)S(1)} custom-call(bf16[512,1536]{1,0:T(8,128)(2,1)S(1)} %get-tuple-element.35.sorted_ref, bf16[4,80,128]{2,1,0:T(8,128)(2,1)S(1)} %join.5.after_ref.near_ref), custom_call_target="tpu_custom_call" | custom-call | tf_op jit(solution)/shard_map/taps/pallas_call | solution.py:533
  16.1 0.0 collective-permute-done.2.other_ref
  16.1 1.3 %collective-permute-start.3 = (bf16[8,80,128]{2,1,0:T(8,128)(2,1)S(1)}, bf16[8,80,128]{2,1,0:T(8,128)(2,1)S(1)}, u32[]{:S(2)}, u32[]{:S(2)}) collective-permute-start(bf16[8,80,128]{2,1,0:T(8,128)(2,1)S(1)} %join.6.data_ref.near_ref), channel_id=1, source_target_pairs={{0,8},{4,12},{8,0},{12,4},{16,24},{20,28},{24,16},{28,20},{1,9},{5... | collective-permute-start | bytes 491528 | tf_op jit(solution)/shard_map/ppermute | solution.py:511
  17.4 0.5 %windows.3 = (f32[8,80,128]{2,1,0:T(8,128)S(1)}, f32[8,2,8,128]{3,2,1,0:T(8,128)S(1)}) custom-call(bf16[8,80,128]{2,1,0:T(8,128)(2,1)S(1)} %join.6.data_ref.near_ref), custom_call_target="tpu_custom_call" | custom-call | tf_op jit(solution)/shard_map/windows/pallas_call | solution.py:576
  18.0 1.4 %cuts.2 = (bf16[2,3,3,64,128]{4,3,2,1,0:T(8,128)(2,1)S(1)}, f32[2,64,128]{2,1,0:T(8,128)S(1)}) custom-call(bf16[8,80,128]{2,1,0:T(8,128)(2,1)S(1)} %join.6.data_ref.near_ref, f32[64,128]{1,0:T(8,128)S(1)} %get-tuple-element.34.refs_1_.scale_ref, s32[4,64]{1,0:T(4,128)S(1)} %get-tuple-element.44.partner_ref), custom_call_target="tpu_custom_call" | custom-call | tf_op jit(solution)/shard_map/cuts/pallas_call | solution.py:603
  19.3 2.9 %correlate.3 = (bf16[128,1024]{1,0:T(8,128)(2,1)S(1)}, bf16[128,1024]{1,0:T(8,128)(2,1)S(1)}) custom-call(f32[8,80,128]{2,1,0:T(8,128)S(1)} %get-tuple-element.36.rows_ref, f32[8,2,8,128]{3,2,1,0:T(8,128)S(1)} %get-tuple-element.37.win_ref, bf16[2048,1792]{1,0:T(8,128)(2,1)S(1)} %taps.2.refs_0_.taps_ref, f32[512,128]{1,0:T(8,128)S(1)} %get-tuple-element.31.refs_0_.scale_ref), custom_call_target="tpu_custom_call" | custom-call | tf_op jit(solution)/shard_map/correlate/pallas_call | solution.py:585
  22.2 0.0 collective-permute-done.3.data_ref.other_ref
  22.3 2.0 %collective-permute-start.4 = (bf16[16,80,128]{2,1,0:T(8,128)(2,1)S(1)}, bf16[16,80,128]{2,1,0:T(8,128)(2,1)S(1)}, u32[]{:S(2)}, u32[]{:S(2)}) collective-permute-start(bf16[16,80,128]{2,1,0:T(8,128)(2,1)S(1)} %join.7), channel_id=1, source_target_pairs={{0,4},{4,0},{8,12},{12,8},{16,20},{20,16},{24,28},{28,24},{1,5},{5... | collective-permute-start | bytes 983048 | tf_op jit(solution)/shard_map/ppermute | solution.py:511
  24.3 0.5 %windows.4 = (f32[8,80,128]{2,1,0:T(8,128)S(1)}, f32[8,2,8,128]{3,2,1,0:T(8,128)S(1)}) custom-call(bf16[8,80,128]{2,1,0:T(8,128)(2,1)S(1)} %collective-permute-done.3.data_ref.other_ref), custom_call_target="tpu_custom_call" | custom-call | tf_op jit(solution)/shard_map/windows/pallas_call | solution.py:576
  24.8 2.9 %correlate.4 = (bf16[128,1024]{1,0:T(8,128)(2,1)S(1)}, bf16[128,1024]{1,0:T(8,128)(2,1)S(1)}) custom-call(f32[8,80,128]{2,1,0:T(8,128)S(1)} %get-tuple-element.40.rows_ref, f32[8,2,8,128]{3,2,1,0:T(8,128)S(1)} %get-tuple-element.41.win_ref, bf16[2048,1792]{1,0:T(8,128)(2,1)S(1)} %taps.2.refs_0_.taps_ref, f32[512,128]{1,0:T(8,128)S(1)} %get-tuple-element.31.refs_0_.scale_ref), custom_call_target="tpu_custom_call" | custom-call | tf_op jit(solution)/shard_map/correlate/pallas_call | solution.py:585
  27.7 0.0 collective-permute-done.4.data_ref
  27.7 0.7 %windows.5 = (f32[16,80,128]{2,1,0:T(8,128)S(1)}, f32[16,2,8,128]{3,2,1,0:T(8,128)S(1)}) custom-call(bf16[16,80,128]{2,1,0:T(8,128)(2,1)S(1)} %collective-permute-done.4.data_ref), custom_call_target="tpu_custom_call" | custom-call | tf_op jit(solution)/shard_map/windows/pallas_call | solution.py:576
  28.4 5.4 %correlate.5 = (bf16[256,1024]{1,0:T(8,128)(2,1)S(1)}, bf16[256,1024]{1,0:T(8,128)(2,1)S(1)}) custom-call(f32[16,80,128]{2,1,0:T(8,128)S(1)} %get-tuple-element.46.rows_ref, f32[16,2,8,128]{3,2,1,0:T(8,128)S(1)} %get-tuple-element.47.win_ref, bf16[2048,1792]{1,0:T(8,128)(2,1)S(1)} %taps.3.refs_0_.taps_ref, f32[512,128]{1,0:T(8,128)S(1)} %get-tuple-element.31.refs_0_.scale_ref), custom_call_target="tpu_custom_call" | custom-call | tf_op jit(solution)/shard_map/correlate/pallas_call | solution.py:585
  33.9 1.4 %cuts.3 = (bf16[2,3,3,64,128]{4,3,2,1,0:T(8,128)(2,1)S(1)}, f32[2,64,128]{2,1,0:T(8,128)S(1)}) custom-call(bf16[16,80,128]{2,1,0:T(8,128)(2,1)S(1)} %collective-permute-done.4.data_ref, f32[64,128]{1,0:T(8,128)S(1)} %get-tuple-element.34.refs_1_.scale_ref, s32[4,64]{1,0:T(4,128)S(1)} %get-tuple-element.44.partner_ref), custom_call_target="tpu_custom_call" | custom-call | tf_op jit(solution)/shard_map/cuts/pallas_call | solution.py:603
  35.2 2.7 %detect.1 = f32[256,128]{1,0:T(8,128)} custom-call(bf16[4,256,896]{2,1,0:T(8,128)(2,1)S(1)} %get-tuple-element.50.taps_ref, bf16[2,3,3,64,128]{4,3,2,1,0:T(8,128)(2,1)S(1)} %get-tuple-element.51.refs_0_, f32[2,64,128]{2,1,0:T(8,128)S(1)} %get-tuple-element.52.refs_1_, bf16[2,3,3,64,128]{4,3,2,1,0:T(8,128)(2,1)S(1)} %get-tuple-element.45.refs_1_.refs_2_, ...), custom_call_target="tpu_custom_call" | custom-call | tf_op jit(solution)/shard_map/detect/pallas_call | solution.py:645
  38.0 1.5 %stack.1 = f32[32,1024]{1,0:T(8,128)} custom-call(bf16[32,512]{1,0:T(8,128)(2,1)S(1)} %get-tuple-element.29.owner_ref, bf16[128,1024]{1,0:T(8,128)(2,1)S(1)} %get-tuple-element.38.refs_0_, bf16[128,1024]{1,0:T(8,128)(2,1)S(1)} %get-tuple-element.39.refs_1_, bf16[128,1024]{1,0:T(8,128)(2,1)S(1)} %get-tuple-element.42.refs_2_, ...), custom_call_target="tpu_custom_call" | custom-call | tf_op jit(solution)/shard_map/stack/pallas_call | solution.py:638
  (4 shorter events, 0.1 us)
Async XLA Ops:
  1.4 6.5 %collective-permute-start = (bf16[1,80,128]{2,1,0:T(8,128)(2,1)S(1)}, bf16[1,80,128]{2,1,0:T(8,128)(2,1)S(1)}, u32[]{:S(2)}, u32[]{:S(2)}) collective-permute-start(bf16[1,80,128]{2,1,0:T(8,128)(2,1)S(1)} %get-tuple-element.30.data_ref.after_ref.near_ref), channel_id=1, source_target_pairs={{0,2},{1,3},{2,0},{3,1},{4,6},{5,7},{6,4},{7,5},{8,10},{9,11},{10,... | collective-permute-start | bytes 61448 | tf_op jit(solution)/shard_map/ppermute | solution.py:511
  8.0 4.1 %collective-permute-start.1 = (bf16[2,80,128]{2,1,0:T(8,128)(2,1)S(1)}, bf16[2,80,128]{2,1,0:T(8,128)(2,1)S(1)}, u32[]{:S(2)}, u32[]{:S(2)}) collective-permute-start(bf16[2,80,128]{2,1,0:T(8,128)(2,1)S(1)} %join.4.after_ref.near_ref), channel_id=1, source_target_pairs={{0,1},{1,0},{2,3},{3,2},{4,5},{5,4},{6,7},{7,6},{8,9},{9,8},{10,11... | collective-permute-start | bytes 122888 | tf_op jit(solution)/shard_map/ppermute | solution.py:511
  12.1 4.0 %collective-permute-start.2 = (bf16[4,80,128]{2,1,0:T(8,128)(2,1)S(1)}, bf16[4,80,128]{2,1,0:T(8,128)(2,1)S(1)}, u32[]{:S(2)}, u32[]{:S(2)}) collective-permute-start(bf16[4,80,128]{2,1,0:T(8,128)(2,1)S(1)} %join.5.after_ref.near_ref), channel_id=1, source_target_pairs={{0,16},{4,20},{8,24},{12,28},{16,0},{20,4},{24,8},{28,12},{1,17},{... | collective-permute-start | bytes 245768 | tf_op jit(solution)/shard_map/ppermute | solution.py:511
  16.1 6.1 %collective-permute-start.3 = (bf16[8,80,128]{2,1,0:T(8,128)(2,1)S(1)}, bf16[8,80,128]{2,1,0:T(8,128)(2,1)S(1)}, u32[]{:S(2)}, u32[]{:S(2)}) collective-permute-start(bf16[8,80,128]{2,1,0:T(8,128)(2,1)S(1)} %join.6.data_ref.near_ref), channel_id=1, source_target_pairs={{0,8},{4,12},{8,0},{12,4},{16,24},{20,28},{24,16},{28,20},{1,9},{5... | collective-permute-start | bytes 491528 | tf_op jit(solution)/shard_map/ppermute | solution.py:511
  22.3 5.4 %collective-permute-start.4 = (bf16[16,80,128]{2,1,0:T(8,128)(2,1)S(1)}, bf16[16,80,128]{2,1,0:T(8,128)(2,1)S(1)}, u32[]{:S(2)}, u32[]{:S(2)}) collective-permute-start(bf16[16,80,128]{2,1,0:T(8,128)(2,1)S(1)} %join.7), channel_id=1, source_target_pairs={{0,4},{4,0},{8,12},{12,8},{16,20},{20,16},{24,28},{28,24},{1,5},{5... | collective-permute-start | bytes 983048 | tf_op jit(solution)/shard_map/ppermute | solution.py:511

commit v9 on v8

--- a/solution.py
+++ b/solution.py
@@ -472,21 +472,20 @@
         scales_ref[n] = jnp.where(valid, scale_ref[...] * scale, 0.0)
 
 
-def detect_kernel(taps_ref, *refs):
-    cuts, (diff_ref, x_ref, raw_ref, parts_ref) = refs[:4], refs[4:]
-    windows, scales = [], []
-    for windows_ref, scales_ref in (cuts[0:2], cuts[2:4]):
-        for n in range(2):
-            windows.append([[windows_ref[n, c, j] for j in range(KEEP + 1)] for c in range(CHANNELS)])
-            scales.append(scales_ref.at[n])
+def detect_kernel(last, taps_ref, windows_ref, scales_ref, *refs):
+    out_ref, x_ref, raw_ref, parts_ref = refs[-4:]
+    windows = [[[windows_ref[n, c, j] for j in range(KEEP + 1)] for c in range(CHANNELS)] for n in range(2)]
     out = differential(taps_ref, windows, x_ref, raw_ref, parts_ref)
     for q in range(taps_ref.shape[0]):
-        for d in range(4):
-            at = (q * 4 + d) * DET_ROWS
-            rows = slice(q * DET_ROWS, (q + 1) * DET_ROWS)
-            diff_ref[pl.ds(q * DET_ROWS * 4 + d, DET_ROWS, stride=4), :] = (
-                out[at : at + DET_ROWS] * scales[d][rows, :]
-            )
+        for n in range(2):
+            at = (q * 2 + n) * DET_ROWS
+            value = out[at : at + DET_ROWS] * scales_ref[n, q * DET_ROWS : (q + 1) * DET_ROWS, :]
+            if last:
+                first = q * DET_ROWS * 4 + n
+                out_ref[pl.ds(first, DET_ROWS, stride=4), :] = value
+                out_ref[pl.ds(first + 2, DET_ROWS, stride=4), :] = refs[0][at : at + DET_ROWS, :]
+            else:
+                out_ref[at : at + DET_ROWS, :] = value
 
 
 def on_device(ngx, ngy, waveforms, templates, tpl_stations, det_station, det_time, partner):
@@ -610,6 +609,20 @@
             name="cuts",
         )(data, mine_scale, partners)
 
+    def detect(cuts, *done):
+        high = 2 * DET_COARSE * DET_ROWS
+        return pl.pallas_call(
+            functools.partial(detect_kernel, len(done)),
+            out_shape=jax.ShapeDtypeStruct(((4 if done else 2) * det_dev, DTLAG), F32),
+            scratch_shapes=[
+                pltpu.VMEM((2, high, DET_DEPTH), BF16),
+                pltpu.VMEM((parts, high, DET_FINE * DET_ROWS), F32),
+                pltpu.VMEM((2 * det_dev, DET_FINE * DET_ROWS), F32),
+            ],
+            compiler_params=params,
+            name="detect",
+        )(mine, *cuts, *done)
+
     near, taps = packed, []
     *first, last = rounds(ngx, ngy)
     for n, (axis, mask) in enumerate(first):
@@ -623,8 +636,11 @@
             beside = (taps[-1],)
         elif n == len(first) - 1:
             sums = [*correlate(near, taps[0], 0)]
+            near_lags = detect(near_cuts)
+            beside = (sums[0], near_lags)
+        if near.shape[0] == ngy:
             near_cuts = cut_windows((2, 3), near)
-            beside = (sums[0], near_cuts[0])
+            beside += (near_cuts[0],)
         near = pl.pallas_call(
             join_kernel,
             out_shape=jax.ShapeDtypeStruct((2 * near.shape[0], PACKED, LANES), BF16),
@@ -642,17 +658,7 @@
         name="stack",
     )(owner, *sums)
     far_cuts = cut_windows((0, 1), far)
-    diff = pl.pallas_call(
-        detect_kernel,
-        out_shape=jax.ShapeDtypeStruct((4 * det_dev, DTLAG), F32),
-        scratch_shapes=[
-            pltpu.VMEM((2, 4 * DET_COARSE * DET_ROWS, DET_DEPTH), BF16),
-            pltpu.VMEM((parts, 4 * DET_COARSE * DET_ROWS, DET_FINE * DET_ROWS), F32),
-            pltpu.VMEM((4 * det_dev, DET_FINE * DET_ROWS), F32),
-        ],
-        compiler_params=params,
-        name="detect",
-    )(mine, *far_cuts, *near_cuts)
+    diff = detect(far_cuts, near_lags)
     return stack, diff.reshape(det_dev, 4, DTLAG)
 
 

time: 39.7 us -> 39.7 us (level)
    pallas_call x1 -> x2, Pallas kernels: 2.74 us -> 3 us  [detect(): pl.pallas_call(functools.partial(detect_kernel, len(done)), out_shape=jax...]
  transfers between devices with their start and end apart: 5 -> 5, of which waited for: 0 -> 0; matrix products, arithmetic and copies ran while one was open for 0% -> 0% of each run, Pallas kernels for 43% -> 46%
where the time goes in v9:
time: 39.7 us; the launch traced here: 39.5 us
  Pallas kernels  29.7 us (75%)
  starting transfers between devices  9 us (23%)
  between operations  0.78 us (2%)
    pallas_call x3, Pallas kernels, correlate(): pl.pallas_call(functools.partial(correlate_kernel, start), grid=(count //...  11.1 us
    ppermute x5, starting transfers between devices, swap(): return lax.ppermute(value, axis, [(n, n ^ mask) for n in range(size)])  9 us
    pallas_call x2, Pallas kernels, shifted(): pl.pallas_call(functools.partial(taps_kernel, lambda: call), in_specs=[vm...  5.45 us
    pallas_call x2, Pallas kernels, detect(): pl.pallas_call(functools.partial(detect_kernel, len(done)), out_shape=jax...  3 us
    pallas_call x2, Pallas kernels, cut_windows(): pl.pallas_call(functools.partial(cuts_kernel, ngx, ngy, directions), out_...  2.73 us
    pallas_call x1, Pallas kernels, on_device(): pl.pallas_call(functools.partial(tile_kernel, ngx, ngy), out_shape=(jax.S...  1.9 us
    pallas_call x3, Pallas kernels, correlate(): pl.pallas_call(windows_kernel, out_shape=(jax.ShapeDtypeStruct((count, PA...  1.8 us
    pallas_call x1, Pallas kernels, on_device(): pl.pallas_call(stack_kernel, out_shape=jax.ShapeDtypeStruct((tpl_dev, LAG...  1.5 us
  transfers between devices with their start and end apart: 5, of which 0 were waited for; matrix products, arithmetic and copies ran while one was open for 0% of the time, Pallas kernels for 46%

profile of v9, /device:TPU:1, one launch (start us, length us, event | category | flops | bytes accessed | tf_op | source)
XLA Modules:
  0.0 39.5 jit_solution(5570836209358374785)
XLA Ops:
  0.6 0.8 %pack.1 = (bf16[1,80,128]{2,1,0:T(8,128)(2,1)S(1)}, s32[1,64]{1,0:T(1,128)S(1)}, s32[1,64]{1,0:T(1,128)S(1)}, s32[4,64]{1,0:T(4,128)S(1)}, s32[8,32]{1,0:T(8,128)S(1)}) custom-call(bf16[3,2,1536]{2,1,0:T(2,128)(2,1)} %bitcast.7, s32[1,64]{1,0:T(1,128)} %bitcast.10, s32[1,64]{1,0:T(1,128)} %bitcast.11, s32[4,64]{1,0:T(4,128)} %bitcast.9, s32[8,32]{1,0:T(8,128)} %bitcast.8), custom_call_target="tpu_custom_call" | custom-call | tf_op jit(solution)/shard_map/pack/pallas_call | solution.py:500
  1.4 3.2 %collective-permute-start = (bf16[1,80,128]{2,1,0:T(8,128)(2,1)S(1)}, bf16[1,80,128]{2,1,0:T(8,128)(2,1)S(1)}, u32[]{:S(2)}, u32[]{:S(2)}) collective-permute-start(bf16[1,80,128]{2,1,0:T(8,128)(2,1)S(1)} %get-tuple-element.30.data_ref.after_ref.near_ref), channel_id=1, source_target_pairs={{0,2},{1,3},{2,0},{3,1},{4,6},{5,7},{6,4},{7,5},{8,10},{9,11},{10,... | collective-permute-start | bytes 61448 | tf_op jit(solution)/shard_map/ppermute | solution.py:510
  4.6 1.4 %own.1 = (bf16[4,256,896]{2,1,0:T(8,128)(2,1)S(1)}, f32[64,128]{1,0:T(8,128)S(1)}) custom-call(bf16[1,80,128]{2,1,0:T(8,128)(2,1)S(1)} %get-tuple-element.30.data_ref.after_ref.near_ref, s32[1,64]{1,0:T(1,128)S(1)} %get-tuple-element.32.time_ref, s32[1,64]{1,0:T(1,128)S(1)} %get-tuple-element.33.station_ref, ...), custom_call_target="tpu_custom_call" | custom-call | tf_op jit(solution)/shard_map/own/pallas_call | solution.py:555
  6.0 1.9 %tiles.1 = (bf16[512,1536]{1,0:T(8,128)(2,1)S(1)}, f32[512,128]{1,0:T(8,128)S(1)}, bf16[32,512]{1,0:T(8,128)(2,1)S(1)}) custom-call(bf16[32,8,1536]{2,1,0:T(8,128)(2,1)} %templates_ref.1, s32[8,32]{1,0:T(8,128)S(1)} %get-tuple-element.28.station_ref), custom_call_target="tpu_custom_call" | custom-call | tf_op jit(solution)/shard_map/tiles/pallas_call | solution.py:513
  7.9 0.0 collective-permute-done.other_ref
  8.0 1.4 %collective-permute-start.1 = (bf16[2,80,128]{2,1,0:T(8,128)(2,1)S(1)}, bf16[2,80,128]{2,1,0:T(8,128)(2,1)S(1)}, u32[]{:S(2)}, u32[]{:S(2)}) collective-permute-start(bf16[2,80,128]{2,1,0:T(8,128)(2,1)S(1)} %join.4.after_ref.near_ref), channel_id=1, source_target_pairs={{0,1},{1,0},{2,3},{3,2},{4,5},{5,4},{6,7},{7,6},{8,9},{9,8},{10,11... | collective-permute-start | bytes 122888 | tf_op jit(solution)/shard_map/ppermute | solution.py:510
  9.3 2.7 %taps.2.refs_0_.taps_ref = bf16[2048,1792]{1,0:T(8,128)(2,1)S(1)} custom-call(bf16[512,1536]{1,0:T(8,128)(2,1)S(1)} %get-tuple-element.35.sorted_ref, bf16[2,80,128]{2,1,0:T(8,128)(2,1)S(1)} %join.4.after_ref.near_ref), custom_call_target="tpu_custom_call" | custom-call | tf_op jit(solution)/shard_map/taps/pallas_call | solution.py:532
  12.0 0.0 collective-permute-done.1.other_ref
  12.1 1.3 %collective-permute-start.2 = (bf16[4,80,128]{2,1,0:T(8,128)(2,1)S(1)}, bf16[4,80,128]{2,1,0:T(8,128)(2,1)S(1)}, u32[]{:S(2)}, u32[]{:S(2)}) collective-permute-start(bf16[4,80,128]{2,1,0:T(8,128)(2,1)S(1)} %join.5.after_ref.data_ref.near_ref), channel_id=1, source_target_pairs={{0,16},{4,20},{8,24},{12,28},{16,0},{20,4},{24,8},{28,12},{1,17},{... | collective-permute-start | bytes 245768 | tf_op jit(solution)/shard_map/ppermute | solution.py:510
  13.4 2.7 %taps.3.refs_0_.taps_ref = bf16[2048,1792]{1,0:T(8,128)(2,1)S(1)} custom-call(bf16[512,1536]{1,0:T(8,128)(2,1)S(1)} %get-tuple-element.35.sorted_ref, bf16[4,80,128]{2,1,0:T(8,128)(2,1)S(1)} %join.5.after_ref.data_ref.near_ref), custom_call_target="tpu_custom_call" | custom-call | tf_op jit(solution)/shard_map/taps/pallas_call | solution.py:532
  16.1 1.4 %cuts.2 = (bf16[2,3,3,64,128]{4,3,2,1,0:T(8,128)(2,1)S(1)}, f32[2,64,128]{2,1,0:T(8,128)S(1)}) custom-call(bf16[4,80,128]{2,1,0:T(8,128)(2,1)S(1)} %join.5.after_ref.data_ref.near_ref, f32[64,128]{1,0:T(8,128)S(1)} %get-tuple-element.34.refs_1_.scale_ref, s32[4,64]{1,0:T(4,128)S(1)} %get-tuple-element.36.partner_ref), custom_call_target="tpu_custom_call" | custom-call | tf_op jit(solution)/shard_map/cuts/pallas_call | solution.py:602
  17.5 0.0 collective-permute-done.2.other_ref
  17.5 1.3 %collective-permute-start.3 = (bf16[8,80,128]{2,1,0:T(8,128)(2,1)S(1)}, bf16[8,80,128]{2,1,0:T(8,128)(2,1)S(1)}, u32[]{:S(2)}, u32[]{:S(2)}) collective-permute-start(bf16[8,80,128]{2,1,0:T(8,128)(2,1)S(1)} %join.6.data_ref.near_ref), channel_id=1, source_target_pairs={{0,8},{4,12},{8,0},{12,4},{16,24},{20,28},{24,16},{28,20},{1,9},{5... | collective-permute-start | bytes 491528 | tf_op jit(solution)/shard_map/ppermute | solution.py:510
  18.8 1.2 %detect.2.refs_1_.refs_0_ = f32[128,128]{1,0:T(8,128)S(1)} custom-call(bf16[4,256,896]{2,1,0:T(8,128)(2,1)S(1)} %get-tuple-element.46.taps_ref, bf16[2,3,3,64,128]{4,3,2,1,0:T(8,128)(2,1)S(1)} %get-tuple-element.37.refs_1_.windows_ref, f32[2,64,128]{2,1,0:T(8,128)S(1)} %get-tuple-element.47.scales_ref), custom_call_target="tpu_custom_call" | custom-call | tf_op jit(solution)/shard_map/detect/pallas_call | solution.py:614
  20.0 0.6 %windows.3 = (f32[8,80,128]{2,1,0:T(8,128)S(1)}, f32[8,2,8,128]{3,2,1,0:T(8,128)S(1)}) custom-call(bf16[8,80,128]{2,1,0:T(8,128)(2,1)S(1)} %join.6.data_ref.near_ref), custom_call_target="tpu_custom_call" | custom-call | tf_op jit(solution)/shard_map/windows/pallas_call | solution.py:575
  20.5 2.8 %correlate.3 = (bf16[128,1024]{1,0:T(8,128)(2,1)S(1)}, bf16[128,1024]{1,0:T(8,128)(2,1)S(1)}) custom-call(f32[8,80,128]{2,1,0:T(8,128)S(1)} %get-tuple-element.38.rows_ref, f32[8,2,8,128]{3,2,1,0:T(8,128)S(1)} %get-tuple-element.39.win_ref, bf16[2048,1792]{1,0:T(8,128)(2,1)S(1)} %taps.2.refs_0_.taps_ref, f32[512,128]{1,0:T(8,128)S(1)} %get-tuple-element.31.refs_0_.scale_ref), custom_call_target="tpu_custom_call" | custom-call | tf_op jit(solution)/shard_map/correlate/pallas_call | solution.py:584
  23.4 0.0 collective-permute-done.3.data_ref.other_ref
  23.4 1.9 %collective-permute-start.4 = (bf16[16,80,128]{2,1,0:T(8,128)(2,1)S(1)}, bf16[16,80,128]{2,1,0:T(8,128)(2,1)S(1)}, u32[]{:S(2)}, u32[]{:S(2)}) collective-permute-start(bf16[16,80,128]{2,1,0:T(8,128)(2,1)S(1)} %join.7), channel_id=1, source_target_pairs={{0,4},{4,0},{8,12},{12,8},{16,20},{20,16},{24,28},{28,24},{1,5},{5... | collective-permute-start | bytes 983048 | tf_op jit(solution)/shard_map/ppermute | solution.py:510
  25.3 0.5 %windows.4 = (f32[8,80,128]{2,1,0:T(8,128)S(1)}, f32[8,2,8,128]{3,2,1,0:T(8,128)S(1)}) custom-call(bf16[8,80,128]{2,1,0:T(8,128)(2,1)S(1)} %collective-permute-done.3.data_ref.other_ref), custom_call_target="tpu_custom_call" | custom-call | tf_op jit(solution)/shard_map/windows/pallas_call | solution.py:575
  25.8 2.8 %correlate.4 = (bf16[128,1024]{1,0:T(8,128)(2,1)S(1)}, bf16[128,1024]{1,0:T(8,128)(2,1)S(1)}) custom-call(f32[8,80,128]{2,1,0:T(8,128)S(1)} %get-tuple-element.42.rows_ref, f32[8,2,8,128]{3,2,1,0:T(8,128)S(1)} %get-tuple-element.43.win_ref, bf16[2048,1792]{1,0:T(8,128)(2,1)S(1)} %taps.2.refs_0_.taps_ref, f32[512,128]{1,0:T(8,128)S(1)} %get-tuple-element.31.refs_0_.scale_ref), custom_call_target="tpu_custom_call" | custom-call | tf_op jit(solution)/shard_map/correlate/pallas_call | solution.py:584
  28.7 0.0 collective-permute-done.4.data_ref
  28.7 1.4 %cuts.3 = (bf16[2,3,3,64,128]{4,3,2,1,0:T(8,128)(2,1)S(1)}, f32[2,64,128]{2,1,0:T(8,128)S(1)}) custom-call(bf16[16,80,128]{2,1,0:T(8,128)(2,1)S(1)} %collective-permute-done.4.data_ref, f32[64,128]{1,0:T(8,128)S(1)} %get-tuple-element.34.refs_1_.scale_ref, s32[4,64]{1,0:T(4,128)S(1)} %get-tuple-element.36.partner_ref), custom_call_target="tpu_custom_call" | custom-call | tf_op jit(solution)/shard_map/cuts/pallas_call | solution.py:602
  30.0 1.8 %detect.3 = f32[256,128]{1,0:T(8,128)} custom-call(bf16[4,256,896]{2,1,0:T(8,128)(2,1)S(1)} %get-tuple-element.46.taps_ref, bf16[2,3,3,64,128]{4,3,2,1,0:T(8,128)(2,1)S(1)} %get-tuple-element.52.windows_ref, f32[2,64,128]{2,1,0:T(8,128)S(1)} %get-tuple-element.53.scales_ref, f32[128,128]{1,0:T(8,128)S(1)} %detect.2.refs_1_.refs_0_), custom_call_target="tpu_custom_call" | custom-call | tf_op jit(solution)/shard_map/detect/pallas_call | solution.py:614
  31.9 0.7 %windows.5 = (f32[16,80,128]{2,1,0:T(8,128)S(1)}, f32[16,2,8,128]{3,2,1,0:T(8,128)S(1)}) custom-call(bf16[16,80,128]{2,1,0:T(8,128)(2,1)S(1)} %collective-permute-done.4.data_ref), custom_call_target="tpu_custom_call" | custom-call | tf_op jit(solution)/shard_map/windows/pallas_call | solution.py:575
  32.6 5.4 %correlate.5 = (bf16[256,1024]{1,0:T(8,128)(2,1)S(1)}, bf16[256,1024]{1,0:T(8,128)(2,1)S(1)}) custom-call(f32[16,80,128]{2,1,0:T(8,128)S(1)} %get-tuple-element.48.rows_ref, f32[16,2,8,128]{3,2,1,0:T(8,128)S(1)} %get-tuple-element.49.win_ref, bf16[2048,1792]{1,0:T(8,128)(2,1)S(1)} %taps.3.refs_0_.taps_ref, f32[512,128]{1,0:T(8,128)S(1)} %get-tuple-element.31.refs_0_.scale_ref), custom_call_target="tpu_custom_call" | custom-call | tf_op jit(solution)/shard_map/correlate/pallas_call | solution.py:584
  38.0 1.5 %stack.1 = f32[32,1024]{1,0:T(8,128)} custom-call(bf16[32,512]{1,0:T(8,128)(2,1)S(1)} %get-tuple-element.29.owner_ref, bf16[128,1024]{1,0:T(8,128)(2,1)S(1)} %get-tuple-element.40.refs_0_, bf16[128,1024]{1,0:T(8,128)(2,1)S(1)} %get-tuple-element.41.refs_1_, bf16[128,1024]{1,0:T(8,128)(2,1)S(1)} %get-tuple-element.44.refs_2_, ...), custom_call_target="tpu_custom_call" | custom-call | tf_op jit(solution)/shard_map/stack/pallas_call | solution.py:654
  (4 shorter events, 0.1 us)
Async XLA Ops:
  1.4 6.5 %collective-permute-start = (bf16[1,80,128]{2,1,0:T(8,128)(2,1)S(1)}, bf16[1,80,128]{2,1,0:T(8,128)(2,1)S(1)}, u32[]{:S(2)}, u32[]{:S(2)}) collective-permute-start(bf16[1,80,128]{2,1,0:T(8,128)(2,1)S(1)} %get-tuple-element.30.data_ref.after_ref.near_ref), channel_id=1, source_target_pairs={{0,2},{1,3},{2,0},{3,1},{4,6},{5,7},{6,4},{7,5},{8,10},{9,11},{10,... | collective-permute-start | bytes 61448 | tf_op jit(solution)/shard_map/ppermute | solution.py:510
  8.0 4.1 %collective-permute-start.1 = (bf16[2,80,128]{2,1,0:T(8,128)(2,1)S(1)}, bf16[2,80,128]{2,1,0:T(8,128)(2,1)S(1)}, u32[]{:S(2)}, u32[]{:S(2)}) collective-permute-start(bf16[2,80,128]{2,1,0:T(8,128)(2,1)S(1)} %join.4.after_ref.near_ref), channel_id=1, source_target_pairs={{0,1},{1,0},{2,3},{3,2},{4,5},{5,4},{6,7},{7,6},{8,9},{9,8},{10,11... | collective-permute-start | bytes 122888 | tf_op jit(solution)/shard_map/ppermute | solution.py:510
  12.1 5.4 %collective-permute-start.2 = (bf16[4,80,128]{2,1,0:T(8,128)(2,1)S(1)}, bf16[4,80,128]{2,1,0:T(8,128)(2,1)S(1)}, u32[]{:S(2)}, u32[]{:S(2)}) collective-permute-start(bf16[4,80,128]{2,1,0:T(8,128)(2,1)S(1)} %join.5.after_ref.data_ref.near_ref), channel_id=1, source_target_pairs={{0,16},{4,20},{8,24},{12,28},{16,0},{20,4},{24,8},{28,12},{1,17},{... | collective-permute-start | bytes 245768 | tf_op jit(solution)/shard_map/ppermute | solution.py:510
  17.5 5.9 %collective-permute-start.3 = (bf16[8,80,128]{2,1,0:T(8,128)(2,1)S(1)}, bf16[8,80,128]{2,1,0:T(8,128)(2,1)S(1)}, u32[]{:S(2)}, u32[]{:S(2)}) collective-permute-start(bf16[8,80,128]{2,1,0:T(8,128)(2,1)S(1)} %join.6.data_ref.near_ref), channel_id=1, source_target_pairs={{0,8},{4,12},{8,0},{12,4},{16,24},{20,28},{24,16},{28,20},{1,9},{5... | collective-permute-start | bytes 491528 | tf_op jit(solution)/shard_map/ppermute | solution.py:510
  23.4 5.3 %collective-permute-start.4 = (bf16[16,80,128]{2,1,0:T(8,128)(2,1)S(1)}, bf16[16,80,128]{2,1,0:T(8,128)(2,1)S(1)}, u32[]{:S(2)}, u32[]{:S(2)}) collective-permute-start(bf16[16,80,128]{2,1,0:T(8,128)(2,1)S(1)} %join.7), channel_id=1, source_target_pairs={{0,4},{4,0},{8,12},{12,8},{16,20},{20,16},{24,28},{28,24},{1,5},{5... | collective-permute-start | bytes 983048 | tf_op jit(solution)/shard_map/ppermute | solution.py:510
